TPU v7x, 32 devices: a whole 2x2x4 slice. The times are simulated.
32 devices in a mesh: section: 2 (over x), dp: 16 (over z, y, core).
Axes of the slice: x: 2, y: 2, z: 4, core: 2. Of those that a mesh axis runs over, the one named last changes fastest.
Arguments:
- sources: bfloat16 [13824, 1024], P('dp'), may hold values from -6 to 6
- targets: bfloat16 [8192, 1024], P('dp'), may hold values from -6 to 6
- cotangent: bfloat16 [8192, 1024], P('dp'), may hold values from -6 to 6
- source_lengths: int32 [16, 2], P('dp'), may hold values from 48 to 768, as said below
- target_lengths: int32 [16, 2], P('dp'), may hold values from 128 to 256, as said below
- attn_qkv: bfloat16 [2, 1024, 3072], P('section'), may hold values from -0.1875 to 0.1875
- attn_out: bfloat16 [2, 1024, 1024], P('section'), may hold values from -0.75 to 0.75
- ffn_in: bfloat16 [2, 1024, 4096], P('section'), may hold values from -0.1875 to 0.1875
- ffn_out: bfloat16 [2, 4096, 1024], P('section'), may hold values from -0.09375 to 0.09375
- norm_gains: float32 [2, 2, 1024], P('section'), may hold values from 0.5 to 1.5
- prefix_pairs: bfloat16 [2, 2, 30, 1024], P('section'), may hold values from -6 to 6
- adapt_down: bfloat16 [2, 1024, 512], P('section'), may hold values from -0.1875 to 0.1875
- adapt_down_bias: float32 [2, 512], P('section'), may hold values from -3 to 3
- adapt_up: bfloat16 [2, 512, 1024], P('section'), may hold values from -0.0625 to 0.0625
- adapt_up_bias: float32 [2, 1024], P('section'), may hold values from -0.6 to 0.6
- cross_query: bfloat16 [1024, 1024], replicated, may hold values from -0.1875 to 0.1875
- cross_pairs: bfloat16 [1024, 2048], replicated, may hold values from -0.1875 to 0.1875
- cross_out: bfloat16 [1024, 1024], replicated, may hold values from -0.75 to 0.75
- cross_gain: float32 [1024], replicated, may hold values from 0.5 to 1.5
Outputs:
- decoder_output: bfloat16 [8192, 1024], P('dp', 'section')
- source_grad: bfloat16 [13824, 1024], P('dp', 'section')
- target_grad: bfloat16 [8192, 1024], P('dp', 'section')
- prefix_grad: float32 [2, 2, 30, 1024], P('section')
- down_grad: float32 [2, 1024, 512], P('section')
- down_bias_grad: float32 [2, 512], P('section')
- up_grad: float32 [2, 512, 1024], P('section')
- up_bias_grad: float32 [2, 1024], P('section')
Inputs may be any that keep to these rules, and one draw needn't show every extreme that they name: `source_lengths`: row i holds data index i's lengths: the first column (long bucket) lies from 97 to 768 and equals 768 for some i; the second (short bucket) lies from 48 to 96 and equals 96 for some i. `target_lengths`: each column equals 256 for some row.
All inputs are finite; a program needn't handle non-finite values.
Results may differ from a plain program's by a relative error of at most 0.023.
Values may be sent and summed in bfloat16 or wider, within the bound.
A program may use at most 448 MiB of HBM per device.

v0:
```python
import jax
import jax.numpy as jnp
from jax import lax
from jax.sharding import PartitionSpec as P

HD = 64
PRE = 30
SRC_LONG = 768
SRC_SHORT = 96
TGT = 256


norm_eps = 1e-05
big_negative = -1e30
adapter_scale = 4.0
block_limit = 512


def for_sending(value):
    return jax.tree.map(lambda a: a.astype(jnp.bfloat16) if a.dtype == jnp.float32 else a, value)


def from_behind(block, axis, distance):
    devices = range(lax.axis_size(axis))
    route = [(i - distance, i) for i in devices if i - distance in devices]
    return lax.ppermute(block, axis, route)


def to_low(values):
    return values.astype(jnp.bfloat16)


def matmul(left_side, right_side):
    return jnp.dot(left_side, right_side, preferred_element_type=jnp.float32)


def matmul_tn(left_side, right_side):
    return lax.dot_general(
        left_side, right_side, (((0,), (0,)), ((), ())), preferred_element_type=jnp.float32
    )


def matmul_nt(left_side, right_side):
    return lax.dot_general(
        left_side, right_side, (((1,), (1,)), ((), ())), preferred_element_type=jnp.float32
    )


def layer_norm(values, weight):
    centered = values - jnp.mean(values, axis=-1, keepdims=True)
    return (
        centered
        * lax.rsqrt(jnp.mean(centered * centered, axis=-1, keepdims=True) + norm_eps)
        * weight
    )


def norm_back(values, weight, grad_in):
    return jax.vjp(lambda inner_value: layer_norm(inner_value, weight), values)[1](grad_in)[0]


def exact_gelu(values):
    return jax.nn.gelu(values, approximate=False)


def gelu_back(values, grad_in):
    return jax.vjp(exact_gelu, values)[1](grad_in)[0]


def key_allowed(row_start, row_count, prefix_len, key_rows, length, causal):
    grid_shape = (row_count, prefix_len + key_rows)
    query_pos = row_start + lax.broadcasted_iota(jnp.int32, grid_shape, 0)
    key_pos = lax.broadcasted_iota(jnp.int32, grid_shape, 1) - prefix_len
    allowed = key_pos < length
    if causal:
        allowed = jnp.logical_and(allowed, key_pos <= query_pos)
    return allowed


def split_heads(values):
    return values.reshape(values.shape[0], values.shape[1] // HD, HD)


def block_scores(query_block, key_heads, block_start, prefix_len, length, causal):
    scores = jnp.einsum(
        "qhd,khd->hqk", query_block, key_heads, preferred_element_type=jnp.float32
    ) * HD ** (-0.5)
    allowed = key_allowed(
        block_start,
        query_block.shape[0],
        prefix_len,
        key_heads.shape[0] - prefix_len,
        length,
        causal,
    )
    return jnp.where(allowed[None], scores, big_negative)


def attend_forward(queries, keys_all, values_all, prefix_len, length, causal):
    query_heads = split_heads(queries)
    key_heads = split_heads(keys_all)
    value_heads = split_heads(values_all)
    attended, log_totals = ([], [])
    for block_start in range(0, queries.shape[0], block_limit):
        query_block = query_heads[block_start : block_start + block_limit]
        scores = block_scores(query_block, key_heads, block_start, prefix_len, length, causal)
        row_peak = jnp.max(scores, axis=-1, keepdims=True)
        exp_scores = jnp.exp(scores - row_peak)
        row_totals = jnp.sum(exp_scores, axis=-1, keepdims=True)
        soft_weights = to_low(exp_scores / row_totals)
        mixed_heads = jnp.einsum(
            "hqk,khd->qhd", soft_weights, value_heads, preferred_element_type=jnp.float32
        )
        attended.append(to_low(mixed_heads.reshape(mixed_heads.shape[0], -1)))
        log_totals.append((row_peak + jnp.log(row_totals))[:, :, 0])
    return (jnp.concatenate(attended, 0), jnp.concatenate(log_totals, 1))


def attend_backward(
    queries, keys_all, values_all, log_totals, out_grad, prefix_len, length, causal
):
    query_heads = split_heads(queries)
    key_heads = split_heads(keys_all)
    value_heads = split_heads(values_all)
    grad_heads = split_heads(out_grad)
    query_grads = []
    key_grad = jnp.zeros(key_heads.shape, jnp.float32)
    value_grad = jnp.zeros(value_heads.shape, jnp.float32)
    for block_start in range(0, queries.shape[0], block_limit):
        query_block = query_heads[block_start : block_start + block_limit]
        grad_block = grad_heads[block_start : block_start + block_limit]
        scores = block_scores(query_block, key_heads, block_start, prefix_len, length, causal)
        soft_exact = jnp.exp(scores - log_totals[:, block_start : block_start + block_limit, None])
        weight_grad = jnp.einsum(
            "qhd,khd->hqk", grad_block, value_heads, preferred_element_type=jnp.float32
        )
        row_dot = jnp.sum(soft_exact * weight_grad, axis=-1, keepdims=True)
        score_grad = to_low(soft_exact * (weight_grad - row_dot) * HD ** (-0.5))
        block_grad = jnp.einsum(
            "hqk,khd->qhd", score_grad, key_heads, preferred_element_type=jnp.float32
        )
        query_grads.append(block_grad.reshape(block_grad.shape[0], -1))
        key_grad = key_grad + jnp.einsum(
            "hqk,qhd->khd", score_grad, query_block, preferred_element_type=jnp.float32
        )
        value_grad = value_grad + jnp.einsum(
            "hqk,qhd->khd", to_low(soft_exact), grad_block, preferred_element_type=jnp.float32
        )
    key_count = keys_all.shape[0]
    return (
        jnp.concatenate(query_grads, 0),
        key_grad.reshape(key_count, -1),
        value_grad.reshape(key_count, -1),
    )


def self_forward(tokens, length, causal, weights):
    model_width = tokens.shape[1]
    qkv_rows = to_low(matmul(tokens, weights["qkv"]))
    keys_all = jnp.concatenate(
        [weights["prefix"][0], qkv_rows[:, model_width : 2 * model_width]], 0
    )
    values_all = jnp.concatenate([weights["prefix"][1], qkv_rows[:, 2 * model_width :]], 0)
    attended, log_totals = attend_forward(
        qkv_rows[:, :model_width], keys_all, values_all, PRE, length, causal
    )
    return (tokens.astype(jnp.float32) + matmul(attended, weights["out"]), (qkv_rows, log_totals))


def self_backward(sum_grad, tokens, saved, length, causal, weights):
    qkv_rows, log_totals = saved
    model_width = tokens.shape[1]
    keys_all = jnp.concatenate(
        [weights["prefix"][0], qkv_rows[:, model_width : 2 * model_width]], 0
    )
    values_all = jnp.concatenate([weights["prefix"][1], qkv_rows[:, 2 * model_width :]], 0)
    out_grad = to_low(matmul_nt(to_low(sum_grad), weights["out"]))
    query_grad, key_grad, value_grad = attend_backward(
        qkv_rows[:, :model_width], keys_all, values_all, log_totals, out_grad, PRE, length, causal
    )
    qkv_grad = to_low(jnp.concatenate([query_grad, key_grad[PRE:], value_grad[PRE:]], 1))
    tokens_grad = sum_grad + matmul_nt(qkv_grad, weights["qkv"])
    return (tokens_grad, jnp.stack([key_grad[:PRE], value_grad[:PRE]]))


def ffn_forward(normed, weights):
    normed_low = to_low(normed)
    hidden = matmul(normed_low, weights["ffn_in"])
    active = to_low(exact_gelu(hidden))
    adapter_pre = matmul(normed_low, weights["down"]) + weights["down_bias"]
    adapter_act = to_low(exact_gelu(adapter_pre))
    adapter_out = matmul(adapter_act, weights["up"]) + weights["up_bias"]
    summed = normed + matmul(active, weights["ffn_out"]) + adapter_scale * adapter_out
    return (summed, (normed_low, hidden, adapter_pre, adapter_act))


def ffn_backward(sum_grad, saved, weights):
    normed_low, hidden, adapter_pre, adapter_act = saved
    branch_grad = to_low(sum_grad)
    adapter_grad = to_low(adapter_scale * sum_grad)
    up_grad = matmul_tn(adapter_act, adapter_grad)
    up_bias_grad = jnp.sum(adapter_grad.astype(jnp.float32), axis=0)
    pre_grad = to_low(gelu_back(adapter_pre, matmul_nt(adapter_grad, weights["up"])))
    down_grad = matmul_tn(normed_low, pre_grad)
    down_bias_grad = jnp.sum(pre_grad.astype(jnp.float32), axis=0)
    hidden_grad = to_low(gelu_back(hidden, matmul_nt(branch_grad, weights["ffn_out"])))
    normed_grad = (
        sum_grad + matmul_nt(pre_grad, weights["down"]) + matmul_nt(hidden_grad, weights["ffn_in"])
    )
    return (normed_grad, (down_grad, down_bias_grad, up_grad, up_bias_grad))


def encoder_forward(tokens, length, weights):
    first_sum, attn_saved = self_forward(tokens, length, False, weights)
    normed = layer_norm(first_sum, weights["gains"][0])
    second_sum, ffn_saved = ffn_forward(normed, weights)
    memory = to_low(layer_norm(second_sum, weights["gains"][1]))
    return (memory, (first_sum, second_sum, attn_saved, ffn_saved))


def encoder_blank(row_count, model_width, hidden_width, adapter_width):
    float_rows = jnp.zeros((row_count, model_width), jnp.float32)
    attn_blank = (
        jnp.zeros((row_count, 3 * model_width), jnp.bfloat16),
        jnp.zeros((model_width // HD, row_count), jnp.float32),
    )
    ffn_blank = (
        jnp.zeros((row_count, model_width), jnp.bfloat16),
        jnp.zeros((row_count, hidden_width), jnp.float32),
        jnp.zeros((row_count, adapter_width), jnp.float32),
        jnp.zeros((row_count, adapter_width), jnp.bfloat16),
    )
    return (float_rows, float_rows, attn_blank, ffn_blank)


def encoder_backward(tokens, length, saved, memory_grad, weights):
    first_sum, second_sum, attn_saved, ffn_saved = saved
    second_grad = norm_back(second_sum, weights["gains"][1], memory_grad.astype(jnp.float32))
    normed_grad, adapter_grads = ffn_backward(second_grad, ffn_saved, weights)
    first_grad = norm_back(first_sum, weights["gains"][0], normed_grad)
    tokens_grad, prefix_grad = self_backward(first_grad, tokens, attn_saved, length, False, weights)
    return (to_low(tokens_grad), (prefix_grad,) + adapter_grads)


def decoder_pass(targets, cotangent, target_len, source_len, pair_rows, weights, cross_params):
    model_width = targets.shape[1]
    first_sum, attn_saved = self_forward(targets, target_len, True, weights)
    normed = layer_norm(first_sum, weights["gains"][0])
    cross_queries = to_low(matmul(to_low(normed), cross_params["query"]))
    cross_keys = pair_rows[:, :model_width]
    cross_values = pair_rows[:, model_width:]
    cross_att, cross_totals = attend_forward(
        cross_queries, cross_keys, cross_values, 0, source_len, False
    )
    second_sum = normed + matmul(cross_att, cross_params["out"])
    middle = layer_norm(second_sum, cross_params["gain"])
    third_sum, ffn_saved = ffn_forward(middle, weights)
    final_norm = layer_norm(third_sum, weights["gains"][1])
    valid_rows = lax.broadcasted_iota(jnp.int32, (targets.shape[0], 1), 0) < target_len
    output = to_low(jnp.where(valid_rows, final_norm, 0.0))
    third_grad = norm_back(
        third_sum, weights["gains"][1], jnp.where(valid_rows, cotangent.astype(jnp.float32), 0.0)
    )
    middle_grad, adapter_grads = ffn_backward(third_grad, ffn_saved, weights)
    second_grad = norm_back(second_sum, cross_params["gain"], middle_grad)
    att_grad = to_low(matmul_nt(to_low(second_grad), cross_params["out"]))
    query_grad, key_grad, value_grad = attend_backward(
        cross_queries, cross_keys, cross_values, cross_totals, att_grad, 0, source_len, False
    )
    pairs_grad = to_low(jnp.concatenate([key_grad, value_grad], 1))
    normed_grad = second_grad + matmul_nt(to_low(query_grad), cross_params["query"])
    first_grad = norm_back(first_sum, weights["gains"][0], normed_grad)
    tokens_grad, prefix_grad = self_backward(
        first_grad, targets, attn_saved, target_len, True, weights
    )
    return (output, to_low(tokens_grad), pairs_grad, (prefix_grad,) + adapter_grads)


def unchanged(pipe_state):
    return pipe_state


def chained(first_work, second_work):
    return lambda pipe_state: second_work(first_work(pipe_state))


def forward_transfer(pipe_state, bucket):
    new_state = dict(pipe_state)
    new_state["recv" + str(bucket)] = from_behind(
        for_sending(pipe_state["send" + str(bucket)]), "section", 1
    )
    return new_state


def backward_transfer(pipe_state, bucket):
    new_state = dict(pipe_state)
    new_state["grad_in" + str(bucket)] = from_behind(
        for_sending(pipe_state["back" + str(bucket)]), "section", -1
    )
    return new_state


def per_device(
    sources,
    targets,
    cotangent,
    source_lengths,
    target_lengths,
    attn_qkv,
    attn_out,
    ffn_in,
    ffn_out,
    norm_gains,
    prefix_pairs,
    adapt_down,
    adapt_down_bias,
    adapt_up,
    adapt_up_bias,
    cross_query,
    cross_pairs,
    cross_out,
    cross_gain,
):
    is_encoder = lax.axis_index("section") == 0
    weights = dict(
        qkv=attn_qkv[0],
        out=attn_out[0],
        ffn_in=ffn_in[0],
        ffn_out=ffn_out[0],
        gains=norm_gains[0],
        prefix=prefix_pairs[0],
        down=adapt_down[0],
        down_bias=adapt_down_bias[0],
        up=adapt_up[0],
        up_bias=adapt_up_bias[0],
    )
    cross_params = dict(query=cross_query, pairs=cross_pairs, out=cross_out, gain=cross_gain)
    bucket_rows = (SRC_LONG, SRC_SHORT)
    offsets = (0, SRC_LONG)
    model_width = sources.shape[1]
    hidden_width = ffn_in.shape[2]
    adapter_width = adapt_down.shape[2]

    def source_part(bucket):
        return sources[offsets[bucket] : offsets[bucket] + bucket_rows[bucket]]

    def target_part(block_array, bucket):
        return block_array[bucket * TGT : (bucket + 1) * TGT]

    pipe_state = {}
    for bucket in range(2):
        blank_payload = jnp.zeros((bucket_rows[bucket], model_width), jnp.bfloat16)
        pipe_state["send" + str(bucket)] = blank_payload
        pipe_state["recv" + str(bucket)] = blank_payload
        pipe_state["back" + str(bucket)] = blank_payload
        pipe_state["grad_in" + str(bucket)] = blank_payload
        pipe_state["saved" + str(bucket)] = encoder_blank(
            bucket_rows[bucket], model_width, hidden_width, adapter_width
        )
    pipe_state["outputs"] = jnp.zeros((2 * TGT, model_width), jnp.bfloat16)
    pipe_state["target_grads"] = jnp.zeros((2 * TGT, model_width), jnp.bfloat16)
    pipe_state["source_grads"] = jnp.zeros((sources.shape[0], model_width), jnp.bfloat16)
    pipe_state["totals"] = (
        jnp.zeros((2, PRE, model_width), jnp.float32),
        jnp.zeros((model_width, adapter_width), jnp.float32),
        jnp.zeros((adapter_width,), jnp.float32),
        jnp.zeros((adapter_width, model_width), jnp.float32),
        jnp.zeros((model_width,), jnp.float32),
    )

    def encoder_ahead(bucket):

        def encoder_run(pipe_state):
            memory, saved = encoder_forward(source_part(bucket), source_lengths[0, bucket], weights)
            new_state = dict(pipe_state)
            new_state["send" + str(bucket)] = memory
            new_state["saved" + str(bucket)] = saved
            return new_state

        return encoder_run

    def decoder_turn(bucket):

        def decoder_run(pipe_state):
            payload = pipe_state["recv" + str(bucket)]
            pair_rows = to_low(matmul(payload, cross_pairs))
            output, tokens_grad, pairs_grad, adjusted_grads = decoder_pass(
                target_part(targets, bucket),
                target_part(cotangent, bucket),
                target_lengths[0, bucket],
                source_lengths[0, bucket],
                pair_rows,
                weights,
                cross_params,
            )
            back_payload = to_low(matmul_nt(pairs_grad, cross_pairs))
            new_state = dict(pipe_state)
            new_state["back" + str(bucket)] = back_payload
            new_state["outputs"] = (
                pipe_state["outputs"].at[bucket * TGT : (bucket + 1) * TGT].set(output)
            )
            new_state["target_grads"] = (
                pipe_state["target_grads"].at[bucket * TGT : (bucket + 1) * TGT].set(tokens_grad)
            )
            new_state["totals"] = jax.tree.map(jnp.add, pipe_state["totals"], adjusted_grads)
            return new_state

        return decoder_run

    def encoder_behind(bucket):

        def behind_run(pipe_state):
            received = pipe_state["grad_in" + str(bucket)]
            tokens_grad, adjusted_grads = encoder_backward(
                source_part(bucket),
                source_lengths[0, bucket],
                pipe_state["saved" + str(bucket)],
                received,
                weights,
            )
            new_state = dict(pipe_state)
            new_state["source_grads"] = (
                pipe_state["source_grads"]
                .at[offsets[bucket] : offsets[bucket] + bucket_rows[bucket]]
                .set(tokens_grad)
            )
            new_state["totals"] = jax.tree.map(jnp.add, pipe_state["totals"], adjusted_grads)
            return new_state

        return behind_run

    def on_sections(encoder_work, decoder_work, pipe_state):
        return lax.cond(is_encoder, encoder_work, decoder_work, pipe_state)

    pipe_state = on_sections(chained(encoder_ahead(0), encoder_ahead(1)), unchanged, pipe_state)
    for bucket in range(2):
        pipe_state = forward_transfer(pipe_state, bucket)
    pipe_state = on_sections(unchanged, chained(decoder_turn(0), decoder_turn(1)), pipe_state)
    for bucket in range(2):
        pipe_state = backward_transfer(pipe_state, bucket)
    pipe_state = on_sections(chained(encoder_behind(0), encoder_behind(1)), unchanged, pipe_state)
    grad_sums = lax.psum(pipe_state["totals"], "dp")
    replicas = lax.axis_size("dp")
    stacked = tuple(((grad_part / replicas)[None] for grad_part in grad_sums))
    half_width = model_width // 2
    source_half = from_behind(for_sending(pipe_state["source_grads"][:, half_width:]), "section", 1)
    lower_halves = jnp.stack(
        [pipe_state["outputs"][:, :half_width], pipe_state["target_grads"][:, :half_width]]
    )
    target_halves = from_behind(for_sending(lower_halves), "section", -1).astype(lower_halves.dtype)
    decoder_output = jnp.where(is_encoder, target_halves[0], pipe_state["outputs"][:, half_width:])
    target_grad = jnp.where(
        is_encoder, target_halves[1], pipe_state["target_grads"][:, half_width:]
    )
    source_grad = jnp.where(is_encoder, pipe_state["source_grads"][:, :half_width], source_half)
    return (decoder_output, source_grad, target_grad) + stacked


def solution(mesh):
    placed = (
        P("dp", None),
        P("dp", None),
        P("dp", None),
        P("dp", None),
        P("dp", None),
        P("section", None, None),
        P("section", None, None),
        P("section", None, None),
        P("section", None, None),
        P("section", None, None),
        P("section", None, None, None),
        P("section", None, None),
        P("section", None),
        P("section", None, None),
        P("section", None),
        P(),
        P(),
        P(),
        P(),
    )
    return jax.shard_map(
        per_device,
        mesh=mesh,
        in_specs=placed,
        out_specs=(
            P("dp", "section"),
            P("dp", "section"),
            P("dp", "section"),
            P("section", None, None, None),
            P("section", None, None),
            P("section", None),
            P("section", None, None),
            P("section", None),
        ),
        check_vma=False,
    )
```

profile of v0, /device:TPU:0, one launch (start us, length us, event | category | flops | bytes accessed | tf_op | source)
XLA Modules:
  0.0 1178.6 jit_solution(255327659411322003)
XLA Ops:
  9.2 176.2 %conditional.3 = (f32[768,1024]{1,0:T(8,128)S(1)}, f32[768,1024]{1,0:T(8,128)}, bf16[768,3072]{1,0:T(8,128)(2,1)}, f32[16,768]{1,0:T(8,128)}, bf16[768,1024]{1,0...) conditional(s32[]{:T(128)} %convert_element_type.449, () %tuple.64, ...), branch_computations={%region_0.0_spmd, %region_1.16_spmd} | conditional | flops 26536407040 | bytes 496282240 | solution.py:433
  62.2 9.1 fusion.13
  79.0 8.6 fusion.45
  87.7 12.6 %fusion = (f32[16,512]{1,0:T(8,128)S(1)}, f32[16,512,798]{1,2,0:T(8,128)}) fusion(pred[798]{0:T(1024)(128)(4,1)S(1)} %add_compare_fusion, bf16[512,16,64]{0,2,1:T(8,128)(2,1)S(1)} %bitcast.491, bf16[768,16,64]{0,2,1:T(8,128)(2,1)S(1)} %bitcast.483, bf16[30,16,64]{0,2,1:T(8,128)(2,1)S(1)} %bitcast.496), kind=kOutput, calls=%fused_computation.3 | convolution fusion | flops 859635712 | bytes 28865310 | tf_op jit(solution)/shard_map/cond/branch_1_fun/qhd,khd->hqk/dot_general | solution.py:85
  100.3 11.6 fusion.1
  111.9 12.1 %fusion.42 = bf16[16,64,512]{2,1,0:T(8,128)(2,1)S(1)} fusion(f32[16,512,798]{1,2,0:T(8,128)} %get-tuple-element.605, f32[16,512]{1,0:T(8,128)S(1)} %fusion.1, f32[16,512]{1,0:T(8,128)S(1)} %get-tuple-element.604, pred[798]{0:T(1024)(128)(4,1)S(1)} %add_compare_fusion, bf16[768,16,64]{0,2,1:T(8,128)(2,1)S(1)} %bitcast.481, bf16[30,16,64]{0,2,1:T(8,128)(2,1)S(1)} %bitcast.533), kind=kOutput, calls=%fused_computation.85 | convolution fusion | flops 873242624 | bytes 28898078 | tf_op jit(solution)/shard_map/cond/branch_1_fun/hqk,khd->qhd/dot_general | solution.py:111
  133.9 9.4 fusion.759
  143.3 33.9 %fusion.16 = f32[768,1024]{1,0:T(8,128)S(1)} fusion(bf16[4096,1024]{1,0:T(8,128)(2,1)S(1)} %bitcast.567, f32[768,4096]{1,0:T(8,128)} %fusion.759), kind=kOutput, calls=%fused_computation.31 | convolution fusion | flops 6646923264 | bytes 24117248 | tf_op jit(solution)/shard_map/cond/branch_1_fun/dot_general | solution.py:34
  188.1 37.3 %collective-permute-done.1 = bf16[96,1024]{1,0:T(8,128)(2,1)S(1)} collective-permute-done((bf16[96,1024]{1,0:T(8,128)(2,1)S(1)}, bf16[96,1024]{1,0:T(8,128)(2,1)S(1)}, u32[]{:S(2)}, u32[]{:S(2)}) %collective-permute-start.1) | collective-permute-done | bytes 196640 | tf_op jit(solution)/shard_map/ppermute | solution.py:26
  225.5 14.2 %conditional.4 = (bf16[768,1024]{1,0:T(8,128)(2,1)}, bf16[96,1024]{1,0:T(8,128)(2,1)}, f32[2,30,1024]{2,0,1:T(2,128)S(1)}, f32[1024,512]{1,0:T(8,128)}, f32[512]...) conditional(s32[]{:T(128)} %convert_element_type.449, ...), branch_computations={%region_16.57_spmd, %region_57.58_spmd} | conditional | flops 45633441792 | bytes 1050951744 | solution.py:433
  242.3 429.5 %collective-permute-done.4 = bf16[96,1024]{1,0:T(8,128)(2,1)S(1)} collective-permute-done((bf16[96,1024]{1,0:T(8,128)(2,1)}, bf16[96,1024]{1,0:T(8,128)(2,1)S(1)}, u32[]{:S(2)}, u32[]{:S(2)}) %collective-permute-start.4) | collective-permute-done | bytes 196640 | tf_op jit(solution)/shard_map/ppermute | solution.py:26
  671.8 377.8 %conditional.5 = (bf16[864,1024]{1,0:T(8,128)(2,1)}, f32[2,30,1024]{2,0,1:T(2,128)}, f32[512]{0:T(512)}, f32[1024]{0:T(1024)}, f32[1024,512]{1,0:T(8,128)}, /*index=5*/f32[512,1024]{1,0:T(8,128)}) conditional(s32[]{:T(128)} %convert_element_type.449, (f32[2,30,1024]{2,0,1:T(2,128)}, f32[1024,512]{1,0:T(8,128)}, f32[512]{0:T(512)}, ...), branch_computations={%region_58.59_spmd, %region_59.83_spmd} | conditional | flops 32359503872 | bytes 762130752 | solution.py:433
  682.2 12.1 %fusion.556 = f32[96,1024]{1,0:T(8,128)S(1)} fusion(bf16[1024,4096]{1,0:T(8,128)(2,1)} %get-tuple-element.303, f32[96,4096]{1,0:T(8,128)} %get-tuple-element.314, bf16[4096,1024]{1,0:T(8,128)(2,1)} %get-tuple-element.302, f32[96,1024]{1,0:T(8,128)S(1)} %get-tuple-element.590, f32[96]{0:T(128)S(1)} %get-tuple-element.708), kind=kOutput, calls=%fused_computation.793 | convolution fusion | flops 1639120896 | bytes 19136896 | tf_op jit(solution)/shard_map/cond/branch_1_fun/dot_general | solution.py:44
  700.3 39.3 %fusion.921 = bf16[768,4096]{1,0:T(8,128)(2,1)S(1)} fusion(f32[768,4096]{1,0:T(8,128)} %get-tuple-element.301, bf16[4096,1024]{1,0:T(8,128)(2,1)} %get-tuple-element.302, f32[768,1024]{1,0:T(8,128)S(1)} %get-tuple-element.586, f32[768]{0:T(1024)S(1)} %get-tuple-element.710), kind=kOutput, calls=%fused_computation.668.clone.clone.1 | convolution fusion | flops 6670516224 | bytes 30411776 | tf_op jit(solution)/shard_map/cond/branch_1_fun/dot_general | solution.py:44
  847.4 21.2 %fusion.538 = bf16[16,64,256]{2,1,0:T(8,128)(2,1)} fusion(f32[16,798,256]{2,1,0:T(8,128)} %subtract_exponential_fusion.19, f32[16,256,798]{1,2,0:T(8,128)} %fusion.549, bf16[768,16,64]{0,2,1:T(8,128)(2,1)S(1)} %bitcast.426, bf16[30,16,64]{0,2,1:T(8,128)(2,1)} %bitcast.452), kind=kOutput, calls=%fused_computation.769 | convolution fusion | flops 438260512 | bytes 28307456 | tf_op jit(solution)/shard_map/cond/branch_1_fun/hqk,khd->qhd/dot_general | solution.py:139
  868.6 16.8 %fusion.550 = f32[16,512,798]{1,2,0:T(8,128)} fusion(bf16[512,16,64]{0,2,1:T(8,128)(2,1)} %bitcast.441, bf16[768,16,64]{0,2,1:T(8,128)(2,1)S(1)} %bitcast.421, bf16[30,16,64]{0,2,1:T(8,128)(2,1)S(1)} %bitcast.447), kind=kOutput, calls=%fused_computation.787 | convolution fusion | flops 840032256 | bytes 28831744 | tf_op jit(solution)/shard_map/cond/branch_1_fun/qhd,khd->hqk/dot_general | solution.py:134
  885.3 12.6 %fusion.707 = f32[16,798,512]{2,1,0:T(8,128)} fusion(bf16[512,16,64]{0,2,1:T(8,128)(2,1)S(1)} %bitcast.444, bf16[768,16,64]{0,2,1:T(8,128)(2,1)S(1)} %bitcast.427, bf16[30,16,64]{0,2,1:T(8,128)(2,1)S(1)} %bitcast.454), kind=kOutput, calls=%fused_computation.985 | convolution fusion | flops 840032256 | bytes 28831744 | tf_op jit(solution)/shard_map/cond/branch_1_fun/qhd,khd->hqk/dot_general | solution.py:85
  898.0 44.1 %convolution_convert_fusion.17 = bf16[16,64,512]{2,1,0:T(8,128)(2,1)} fusion(f32[16,512,798]{1,2,0:T(8,128)} %fusion.550, f32[16,798,512]{2,1,0:T(8,128)} %fusion.707, f32[16,512]{1,0:T(8,128)S(1)} %copy-done.191, pred[798]{0:T(1024)(128)(4,1)S(1)} %copy-done.237, bf16[768,16,64]{0,2,1:T(8,128)(2,1)S(1)} %bitcast.428, bf16[30,16,64]{0,2,1:T(8,128)(2,1)S(1)} %bitcast.455), kind=kOutput, calls=%fused_computation.768 | convolution fusion | flops 912474880 | bytes 55014176 | tf_op jit(solution)/shard_map/cond/branch_1_fun/hqk,khd->qhd/dot_general | solution.py:139
  942.1 44.7 %fusion.637 = f32[16,798,64]{1,2,0:T(8,128)} fusion(bf16[512,16,64]{0,2,1:T(8,128)(2,1)} %bitcast.443, f32[16,512,798]{1,2,0:T(8,128)} %fusion.550, f32[16,798,512]{2,1,0:T(8,128)} %fusion.707, f32[16,512]{1,0:T(8,128)S(1)} %copy-done.191, pred[798]{0:T(1024)(128)(4,1)S(1)} %copy-done.237), kind=kOutput, calls=%fused_computation.917 | convolution fusion | flops 908681984 | bytes 56648480 | tf_op jit(solution)/shard_map/cond/branch_1_fun/hqk,qhd->khd/dot_general | solution.py:143
  986.8 13.7 %fusion.480 = f32[16,64,798]{2,1,0:T(8,128)} fusion(bf16[512,16,64]{0,2,1:T(8,128)(2,1)S(1)} %bitcast.442, f32[16,798,512]{2,1,0:T(8,128)} %fusion.707, f32[16,512]{1,0:T(8,128)S(1)} %copy-done.191, pred[798]{0:T(1024)(128)(4,1)S(1)} %copy-done.237), kind=kOutput, calls=%fused_computation.662 | convolution fusion | flops 862912512 | bytes 30499614 | tf_op jit(solution)/shard_map/cond/branch_1_fun/hqk,qhd->khd/dot_general | solution.py:146
  1000.5 20.4 %add_bitcast_fusion.1 = f32[798,16,64]{0,2,1:T(8,128)} fusion(f32[16,798,64]{1,2,0:T(8,128)} %fusion.637, bf16[256,16,64]{0,2,1:T(8,128)(2,1)S(1)} %bitcast.517, f32[16,798,256]{2,1,0:T(8,128)} %subtract_exponential_fusion.19, f32[16,256,798]{1,2,0:T(8,128)} %fusion.549), kind=kOutput, calls=%fused_computation.700 | convolution fusion | flops 435546912 | bytes 33210368 | tf_op jit(solution)/shard_map/cond/branch_1_fun/hqk,qhd->khd/dot_general | solution.py:143
  1058.9 18.2 %collective-permute-done.2 = bf16[2,512,512]{2,1,0:T(8,128)(2,1)S(1)} collective-permute-done((bf16[2,512,512]{2,1,0:T(8,128)(2,1)S(1)}, bf16[2,512,512]{2,1,0:T(8,128)(2,1)S(1)}, u32[]{:S(2)}, u32[]{:S(2)}) %collective-permute-start.2) | collective-permute-done | bytes 1048608 | tf_op jit(solution)/shard_map/ppermute | solution.py:26
  1078.3 32.2 %all-reduce = (f32[512]{0:T(512)S(1)}, f32[1024]{0:T(1024)S(1)}) all-reduce(f32[512]{0:T(512)S(1)} %copy-done.199, f32[1024]{0:T(1024)S(1)} %copy-done.184), channel_id=1, replica_groups=mesh['section'=2,'dp'=16] {'dp'}, use_global_device_ids=true, to_apply=%region_85.86 | all-reduce | flops 1536 | bytes 12288 | tf_op jit(solution)/shard_map/psum | solution.py:442
  1113.9 51.1 %all-reduce.4.cloned.1.call-done = (f32[2,30,1024]{2,0,1:T(2,128)}, f32[1024,512]{1,0:T(8,128)}, f32[512,1024]{1,0:T(8,128)}) async-done(((f32[2,30,1024]{2,0,1:T(2,128)}, f32[1024,512]{1,0:T(8,128)}, f32[512,1024]{1,0:T(8,128)}), (f32[2,30,1024]{2,0,1:T(2,128)}, f32[1024,512]{1,0:T(8,128)}, f32[512,1024]{1,0:T(8,128)})) %all-reduce.4.cloned.1.call-update) | async-done | bytes 4440080 | tf_op jit(solution)/shard_map/psum | solution.py:442
  (398 shorter events, 265.4 us)
Async XLA Ops:
  7.2 1157.9 %all-reduce.4.cloned.1.call-start = ((), (), s32[]{:S(2)}) async-start(), calls=%async_computation | async-start | bytes 8880128 | tf_op jit(solution)/shard_map/psum | solution.py:442
  9.2 216.3 %copy-start.178 = (f32[1024]{0:T(1024)S(1)}, f32[1024]{0:T(1024)}, u32[]{:S(2)}) copy-start(f32[1024]{0:T(1024)} %param.55) | copy-start | bytes 12292
  9.2 216.3 %copy-start.229 = (s32[1,2]{1,0:T(1,128)S(1)}, s32[1,2]{1,0:T(1,128)}, u32[]{:S(2)}) copy-start(s32[1,2]{1,0:T(1,128)} %param.41) | copy-start | bytes 28
  14.6 112.6 %copy-start.168 = (f32[1,1024]{1,0:T(1,128)}, f32[1,1024]{1,0:T(1,128)S(1)}, u32[]{:S(2)}) copy-start(f32[1,1024]{1,0:T(1,128)S(1)} %get-tuple-element.599) | copy-start | bytes 12292 | tf_op jit(solution)/shard_map/cond
  143.3 34.0 %copy-start.27 = (bf16[512,1024]{1,0:T(8,128)(2,1)S(1)}, bf16[512,1024]{1,0:T(8,128)(2,1)}, u32[]{:S(2)}) copy-start(bf16[512,1024]{1,0:T(8,128)(2,1)} %get-tuple-element.268) | copy-start | bytes 3145732 | tf_op jit(solution)/shard_map/cond
  143.3 34.0 %copy-start.64 = (bf16[768,512]{1,0:T(8,128)(2,1)S(1)}, bf16[768,512]{1,0:T(8,128)(2,1)}, u32[]{:S(2)}) copy-start(bf16[768,512]{1,0:T(8,128)(2,1)} %get-tuple-element.739) | copy-start | bytes 2359300 | tf_op jit(solution)/shard_map/cond
  143.3 34.0 %copy-start.164 = (f32[1,1024]{1,0:T(1,128)S(1)}, f32[1,1024]{1,0:T(1,128)}, u32[]{:S(2)}) copy-start(f32[1,1024]{1,0:T(1,128)} %get-tuple-element.269) | copy-start | bytes 12292 | tf_op jit(solution)/shard_map/cond
  185.4 40.1 %copy-start.3 = (f32[768,1024]{1,0:T(8,128)}, f32[768,1024]{1,0:T(8,128)S(1)}, u32[]{:S(2)}) copy-start(f32[768,1024]{1,0:T(8,128)S(1)} %get-tuple-element.384) | copy-start | bytes 9437188
  185.4 40.1 %collective-permute-start = (bf16[768,1024]{1,0:T(8,128)(2,1)S(1)}, bf16[768,1024]{1,0:T(8,128)(2,1)S(1)}, u32[]{:S(2)}, u32[]{:S(2)}) collective-permute-start(bf16[768,1024]{1,0:T(8,128)(2,1)S(1)} %get-tuple-element.370), channel_id=1, source_target_pairs={{0,16},{1,17},{2,18},{3,19},{4,20},{5,21},{6,22},{7,23},{8,24},{9,... | collective-permute-start | bytes 4718600 | tf_op jit(solution)/shard_map/ppermute | solution.py:26
  186.8 38.7 %collective-permute-start.1 = (bf16[96,1024]{1,0:T(8,128)(2,1)S(1)}, bf16[96,1024]{1,0:T(8,128)(2,1)S(1)}, u32[]{:S(2)}, u32[]{:S(2)}) collective-permute-start(bf16[96,1024]{1,0:T(8,128)(2,1)S(1)} %get-tuple-element.371), channel_id=1, source_target_pairs={{0,16},{1,17},{2,18},{3,19},{4,20},{5,21},{6,22},{7,23},{8,24},{9,... | collective-permute-start | bytes 589832 | tf_op jit(solution)/shard_map/ppermute | solution.py:26
  225.4 446.3 %copy-start.35 = (f32[96,1024]{1,0:T(8,128)S(1)}, f32[96,1024]{1,0:T(8,128)}, u32[]{:S(2)}) copy-start(f32[96,1024]{1,0:T(8,128)} %get-tuple-element.388) | copy-start | bytes 1179652
  239.7 432.1 %copy-start.79 = (f32[2,30,1024]{2,0,1:T(2,128)}, f32[2,30,1024]{2,0,1:T(2,128)S(1)}, u32[]{:S(2)}) copy-start(f32[2,30,1024]{2,0,1:T(2,128)S(1)} %get-tuple-element.375) | copy-start | bytes 737284
  239.7 432.1 %copy-start.102 = (bf16[1,512,512]{2,1,0:T(8,128)(2,1)}, bf16[1,512,512]{2,1,0:T(8,128)(2,1)S(1)}, u32[]{:S(2)}) copy-start(bf16[1,512,512]{2,1,0:T(8,128)(2,1)S(1)} %get-tuple-element.373) | copy-start | bytes 1572868
  239.7 432.1 %copy-start.104 = (bf16[512,512]{1,0:T(8,128)(2,1)}, bf16[512,512]{1,0:T(8,128)(2,1)S(1)}, u32[]{:S(2)}) copy-start(bf16[512,512]{1,0:T(8,128)(2,1)S(1)} %get-tuple-element.399) | copy-start | bytes 1572868
  239.7 432.1 %collective-permute-start.3 = (bf16[768,1024]{1,0:T(8,128)(2,1)}, bf16[768,1024]{1,0:T(8,128)(2,1)S(1)}, u32[]{:S(2)}, u32[]{:S(2)}) collective-permute-start(bf16[768,1024]{1,0:T(8,128)(2,1)} %get-tuple-element.380), channel_id=1, source_target_pairs={{16,0},{17,1},{18,2},{19,3},{20,4},{21,5},{22,6},{23,7},{24,8},{25... | collective-permute-start | bytes 4718600 | tf_op jit(solution)/shard_map/ppermute | solution.py:26
  241.0 430.8 %collective-permute-start.4 = (bf16[96,1024]{1,0:T(8,128)(2,1)}, bf16[96,1024]{1,0:T(8,128)(2,1)S(1)}, u32[]{:S(2)}, u32[]{:S(2)}) collective-permute-start(bf16[96,1024]{1,0:T(8,128)(2,1)} %get-tuple-element.387), channel_id=1, source_target_pairs={{16,0},{17,1},{18,2},{19,3},{20,4},{21,5},{22,6},{23,7},{24,8},{25... | collective-permute-start | bytes 589832 | tf_op jit(solution)/shard_map/ppermute | solution.py:26
  681.6 67.6 %copy-start.61 = (f32[96,1024]{1,0:T(8,128)}, f32[96,1024]{1,0:T(8,128)S(1)}, u32[]{:S(2)}) copy-start(f32[96,1024]{1,0:T(8,128)S(1)} %get-tuple-element.590) | copy-start | bytes 1179652 | tf_op jit(solution)/shard_map/cond
  682.2 67.0 %copy-start.218 = (f32[96]{0:T(128)}, f32[96]{0:T(128)S(1)}, u32[]{:S(2)}) copy-start(f32[96]{0:T(128)S(1)} %get-tuple-element.708) | copy-start | bytes 1156 | tf_op jit(solution)/shard_map/cond
  697.2 42.4 %slice-start.8 = ((s8[8388608]{0:T(1024)(128)(4,1)}), s8[4194304]{0:T(1024)(128)(4,1)S(1)}, s32[]{:S(2)}) async-start(s8[8388608]{0:T(1024)(128)(4,1)} %bitcast.412), calls=%async_computation.9 | async-start | bytes 8388608 | tf_op jit(solution)/shard_map/cond
  700.2 39.3 %copy-start.10 = (f32[768,1024]{1,0:T(8,128)}, f32[768,1024]{1,0:T(8,128)S(1)}, u32[]{:S(2)}) copy-start(f32[768,1024]{1,0:T(8,128)S(1)} %get-tuple-element.586) | copy-start | bytes 9437188 | tf_op jit(solution)/shard_map/cond
  700.3 39.3 %slice-start.9 = ((s8[8388608]{0:T(1024)(128)(4,1)}), s8[4194304]{0:T(1024)(128)(4,1)S(1)}, s32[]{:S(2)}) async-start(s8[8388608]{0:T(1024)(128)(4,1)} %bitcast.412), calls=%async_computation.10 | async-start | bytes 8388608 | tf_op jit(solution)/shard_map/cond
  942.1 44.7 %copy-start.55 = (bf16[512,1024]{0,1:T(8,128)(2,1)S(1)}, bf16[512,1024]{0,1:T(8,128)(2,1)}, u32[]{:S(2)}) copy-start(bf16[512,1024]{0,1:T(8,128)(2,1)} %copy.149) | copy-start | bytes 3145732 | tf_op jit(solution)/shard_map/cond
  1050.8 26.3 %collective-permute-start.2 = (bf16[2,512,512]{2,1,0:T(8,128)(2,1)S(1)}, bf16[2,512,512]{2,1,0:T(8,128)(2,1)S(1)}, u32[]{:S(2)}, u32[]{:S(2)}) collective-permute-start(bf16[2,512,512]{2,1,0:T(8,128)(2,1)S(1)} %pad_maximum_fusion.33), channel_id=1, source_target_pairs={{16,0},{17,1},{18,2},{19,3},{20,4},{21,5},{22,6},{23,7},{24,8},{25... | collective-permute-start | bytes 3145736 | tf_op jit(solution)/shard_map/ppermute | solution.py:26
  1054.3 57.4 %collective-permute-start.5 = (bf16[864,512]{1,0:T(8,128)(2,1)}, bf16[864,512]{1,0:T(8,128)(2,1)S(1)}, u32[]{:S(2)}, u32[]{:S(2)}) collective-permute-start(bf16[864,512]{1,0:T(8,128)(2,1)} %slice.475), channel_id=1, source_target_pairs={{0,16},{1,17},{2,18},{3,19},{4,20},{5,21},{6,22},{7,23},{8,24},{9,... | collective-permute-start | bytes 2654216 | tf_op jit(solution)/shard_map/ppermute | solution.py:26
  (99 other events, 795.2 us)
Sparse Core Ops, SparseCore 0:
  1049.7 115.2 all-reduce.3
where the time goes:
time: 1180 us
  waiting for transfers between devices  536 us (45%)
  matrix products  426 us (36%)
  local copies, waits for them, and re-layouts  91.5 us (8%)
  other arithmetic  59.2 us (5%)
  blocking collectives  32.2 us (3%)
  between operations  14.4 us (1%)
    ppermute x6, waiting for transfers between devices, from_behind(): return lax.ppermute(block, axis, route)  485 us
    dot_general x11, matrix products, matmul_nt(): lax.dot_general(left_side, right_side, (((1,), (1,)), ((), ())), preferre...  84.5 us
    dot_general x12, matrix products, matmul(): return jnp.dot(left_side, right_side, preferred_element_type=jnp.float32)  75.6 us
    dot_general x3, matrix products, attend_backward(): jnp.einsum('hqk,khd->qhd', score_grad, key_heads, preferred_element_type=...  68.8 us
    dot_general x3, matrix products, attend_backward(): jnp.einsum('hqk,qhd->khd', score_grad, query_block, preferred_element_typ...  68.3 us
    psum x1, waiting for transfers between devices, per_device(): grad_sums = lax.psum(pipe_state['totals'], 'dp')  51.1 us
    dot_general x6, matrix products, block_scores(): jnp.einsum('qhd,khd->hqk', query_block, key_heads, preferred_element_type...  44.2 us
    psum x1, blocking collectives, per_device(): grad_sums = lax.psum(pipe_state['totals'], 'dp')  32.2 us
  transfers between devices with their start and end apart: 7, of which 4 were waited for; matrix products, arithmetic and copies ran while one was open for 1% of the time, Pallas kernels for 0%

commit v1 on v0

v1 whole, which is shorter than its diff:
```python
import functools

import jax
import jax.numpy as jnp
from jax import lax
from jax.experimental import pallas as pl
from jax.experimental.pallas import tpu as pltpu
from jax.sharding import PartitionSpec as P

HD = 64
PRE = 30
PRE_PAD = 32
SRC_LONG = 768
SRC_SHORT = 96
TGT = 256
LANES = 128

BF = jnp.bfloat16
F32 = jnp.float32
norm_eps = 1e-05
big_negative = -1e30
adapter_scale = 4.0
chunk = 512
vmem_bytes = 56 * 2**20

phi_poly = (
    0.797869713181688,
    0.036392283539041996,
    -8.782472977701046e-05,
    -3.669384069669515e-05,
    1.4250308145882202e-06,
)


def nn(left, right):
    return lax.dot_general(left, right, (((1,), (0,)), ((), ())), preferred_element_type=F32)


def nt(left, right):
    return lax.dot_general(left, right, (((1,), (1,)), ((), ())), preferred_element_type=F32)


def tn(left, right):
    return lax.dot_general(left, right, (((0,), (0,)), ((), ())), preferred_element_type=F32)


def gelu_pair(values):
    square = values * values
    poly = phi_poly[4]
    for coefficient in phi_poly[3::-1]:
        poly = poly * square + coefficient
    half = 0.5 * jnp.tanh(values * poly) + 0.5
    density = jnp.exp(square * -0.5) * 0.3989422804014327
    return values * half, half + values * density


def row_tiles(rows, most=288):
    count = -(-rows // most)
    size = rows // count
    return [(i * size, size) for i in range(count)]


def norm_rows(values):
    centered = values - jnp.mean(values, axis=-1, keepdims=True)
    scale = lax.rsqrt(jnp.mean(centered * centered, axis=-1, keepdims=True) + norm_eps)
    return centered * scale, scale


def norm_rows_back(hat, scale, grad_hat):
    mean_grad = jnp.mean(grad_hat, axis=-1, keepdims=True)
    mean_dot = jnp.mean(grad_hat * hat, axis=-1, keepdims=True)
    return scale * (grad_hat - mean_grad - hat * mean_dot)


def params(limit=vmem_bytes):
    return pltpu.CompilerParams(vmem_limit_bytes=limit)


def whole(shape):
    return pl.BlockSpec(shape, lambda *g: (0,) * len(shape))


def product_kernel(x_ref, w_ref, o_ref):
    o_ref[...] = nn(x_ref[...], w_ref[...]).astype(BF)


def product(x, w, tile=512):
    rows, depth = x.shape
    width = w.shape[1]
    return pl.pallas_call(
        product_kernel,
        grid=(width // tile,),
        in_specs=[whole((rows, depth)), pl.BlockSpec((depth, tile), lambda i: (0, i))],
        out_specs=pl.BlockSpec((rows, tile), lambda i: (0, i)),
        out_shape=jax.ShapeDtypeStruct((rows, width), BF),
        compiler_params=params(),
        name="product",
    )(x, w)


def back_product_kernel(*refs, parts, residual):
    grads = refs[:parts]
    w_ref = refs[parts]
    o_ref = refs[-1]
    total = None
    width = grads[0].shape[1]
    for i, grad in enumerate(grads):
        term = nt(grad[...], w_ref[:, i * width : (i + 1) * width])
        total = term if total is None else total + term
    if residual:
        total = total + refs[parts + 1][...]
    o_ref[...] = total.astype(BF)


def back_product(grads, w, residual=None, tile=256):
    rows, width = grads[0].shape
    depth = w.shape[0]
    parts = len(grads)
    specs = [whole((rows, width))] * parts + [
        pl.BlockSpec((tile, parts * width), lambda i: (i, 0))
    ]
    args = list(grads) + [w]
    if residual is not None:
        specs.append(pl.BlockSpec((rows, tile), lambda i: (0, i)))
        args.append(residual)
    return pl.pallas_call(
        functools.partial(back_product_kernel, parts=parts, residual=residual is not None),
        grid=(depth // tile,),
        in_specs=specs,
        out_specs=pl.BlockSpec((rows, tile), lambda i: (0, i)),
        out_shape=jax.ShapeDtypeStruct((rows, depth), BF),
        compiler_params=params(),
        name="back_product",
    )(*args)


def head_lanes(head):
    lane = lax.broadcasted_iota(jnp.int32, (1, LANES), 1)
    own = (lane < HD) if head == 0 else (lane >= HD)
    first = HD if head == 0 else 0
    return own, lane == first, lane == first + 1


def bf(value):
    return jnp.asarray(value, BF)


def stacked(rows_ref, prefix_ref, start, count):
    rows = rows_ref[start : start + count]
    if prefix_ref is None:
        return rows
    return jnp.concatenate([rows, prefix_ref[...]], 0)


def attend_kernel(*refs, segs, prefix, causal):
    len_ref, q_ref, k_ref, v_ref = refs[:4]
    at = 4
    pk_ref = pv_ref = None
    if prefix:
        pk_ref, pv_ref = refs[4:6]
        at = 6
    o_ref, inv_ref = refs[at : at + 2]
    p_refs = refs[at + 2 :]
    for seg, (q0, nq, k0, nk) in enumerate(segs):
        keys = stacked(k_ref, pk_ref, k0, nk)
        values = stacked(v_ref, pv_ref, k0, nk)
        count = keys.shape[0]
        row = lax.broadcasted_iota(jnp.int32, (count, 1), 0)
        seen = row < jnp.minimum(len_ref[0, seg], nk)
        if prefix:
            seen = seen | ((row >= nk) & (row < nk + PRE))
        queries = q_ref[q0 : q0 + nq] * bf(HD**-0.5)
        out = inv = None
        for head in range(2):
            own, first, _ = head_lanes(head)
            k_own = jnp.where(own, keys, jnp.where(first & ~seen, bf(big_negative), bf(0)))
            q_own = jnp.where(own, queries, jnp.where(first, bf(1), bf(0)))
            v_own = jnp.where(own, values, bf(1))
            scores = nt(k_own, q_own)
            if causal:
                key_at = lax.broadcasted_iota(jnp.int32, scores.shape, 0)
                query_at = lax.broadcasted_iota(jnp.int32, scores.shape, 1)
                allowed = (key_at <= query_at) | (key_at >= nk)
                scores = jnp.where(allowed, scores, big_negative)
            peak = jnp.max(scores, axis=0, keepdims=True)
            weights = jnp.exp(scores - peak).astype(BF)
            p_refs[seg][head] = weights
            mixed = tn(weights, v_own)
            inverse = 1.0 / pltpu.roll(mixed, HD, 1)
            mixed = mixed * inverse
            out = mixed if out is None else jnp.where(own, mixed, out)
            inv = inverse if inv is None else jnp.where(own, inverse, inv)
        o_ref[q0 : q0 + nq] = out.astype(BF)
        inv_ref[q0 : q0 + nq] = inv


def column_spec(rows, offset):
    return pl.BlockSpec((rows, LANES), lambda h: (0, h + offset))


def attend(lengths, q, k, v, prefixes, segs, causal):
    pairs = 8
    q_rows, k_rows = q[0].shape[0], k[0].shape[0]
    prefix = prefixes is not None
    extra = PRE_PAD if prefix else 0
    specs = [
        pl.BlockSpec(memory_space=pltpu.SMEM),
        column_spec(q_rows, q[1]),
        column_spec(k_rows, k[1]),
        column_spec(k_rows, v[1]),
    ]
    args = [lengths, q[0], k[0], v[0]]
    if prefix:
        specs += [column_spec(PRE_PAD, 0)] * 2
        args += list(prefixes)
    weight_shapes = [(2 * pairs, nk + extra, nq) for _, nq, _, nk in segs]
    return pl.pallas_call(
        functools.partial(attend_kernel, segs=segs, prefix=prefix, causal=causal),
        grid=(pairs,),
        in_specs=specs,
        out_specs=[column_spec(q_rows, 0), column_spec(q_rows, 0)]
        + [pl.BlockSpec((2,) + s[1:], lambda h: (h, 0, 0)) for s in weight_shapes],
        out_shape=[
            jax.ShapeDtypeStruct((q_rows, pairs * LANES), BF),
            jax.ShapeDtypeStruct((q_rows, pairs * LANES), F32),
        ]
        + [jax.ShapeDtypeStruct(s, BF) for s in weight_shapes],
        compiler_params=params(),
        name="attend",
    )(*args)


def attend_back_kernel(*refs, segs, prefix):
    q_ref, k_ref, v_ref, o_ref, inv_ref, g_ref = refs[:6]
    at = 6
    pk_ref = pv_ref = None
    if prefix:
        pk_ref, pv_ref = refs[6:8]
        at = 8
    p_refs = refs[at : at + len(segs)]
    outs = refs[at + len(segs) :]
    dq_ref, dk_ref, dv_ref = outs[:3]
    prefix_totals = [None, None]
    scale = HD**-0.5
    for seg, (q0, nq, k0, nk) in enumerate(segs):
        keys = stacked(k_ref, pk_ref, k0, nk)
        values = stacked(v_ref, pv_ref, k0, nk)
        queries = q_ref[q0 : q0 + nq]
        grads = g_ref[q0 : q0 + nq].astype(F32) * inv_ref[q0 : q0 + nq]
        grads_low = grads.astype(BF)
        dots = grads * o_ref[q0 : q0 + nq].astype(F32)
        dq = dk = dv = None
        for head in range(2):
            own, first, second = head_lanes(head)
            row_dot = -jnp.sum(jnp.where(own, dots, 0.0), axis=1, keepdims=True)
            high = row_dot.astype(BF)
            rest = (row_dot - high.astype(F32)).astype(BF)
            g_own = jnp.where(
                own, grads_low, jnp.where(first, high, jnp.where(second, rest, bf(0)))
            )
            v_own = jnp.where(own, values, jnp.where(first | second, bf(1), bf(0)))
            weights = p_refs[seg][head]
            score_grad = (weights.astype(F32) * nt(v_own, g_own)).astype(BF)
            dv_head = nn(weights, grads_low)
            dk_head = nn(score_grad, queries)
            dq_head = tn(score_grad, keys)
            dq = dq_head if dq is None else jnp.where(own, dq_head, dq)
            dk = dk_head if dk is None else jnp.where(own, dk_head, dk)
            dv = dv_head if dv is None else jnp.where(own, dv_head, dv)
        dk = dk * scale
        dq_ref[q0 : q0 + nq] = (dq * scale).astype(BF)
        dk_ref[k0 : k0 + nk] = dk[:nk].astype(BF)
        dv_ref[k0 : k0 + nk] = dv[:nk].astype(BF)
        if prefix:
            for i, grad in enumerate((dk, dv)):
                part = grad[nk:]
                prefix_totals[i] = part if seg == 0 else prefix_totals[i] + part
    if prefix:
        outs[3][...] = prefix_totals[0]
        outs[4][...] = prefix_totals[1]


def attend_back(q, k, v, prefixes, attended, inverse, grad, weights, segs):
    pairs = 8
    q_rows, k_rows = q[0].shape[0], k[0].shape[0]
    prefix = prefixes is not None
    specs = [
        column_spec(q_rows, q[1]),
        column_spec(k_rows, k[1]),
        column_spec(k_rows, v[1]),
        column_spec(q_rows, 0),
        column_spec(q_rows, 0),
        column_spec(q_rows, 0),
    ]
    args = [q[0], k[0], v[0], attended, inverse, grad]
    if prefix:
        specs += [column_spec(PRE_PAD, 0)] * 2
        args += list(prefixes)
    specs += [pl.BlockSpec((2,) + w.shape[1:], lambda h: (h, 0, 0)) for w in weights]
    args += list(weights)
    out_specs = [column_spec(q_rows, 0), column_spec(k_rows, 0), column_spec(k_rows, 0)]
    out_shape = [
        jax.ShapeDtypeStruct((q_rows, pairs * LANES), BF),
        jax.ShapeDtypeStruct((k_rows, pairs * LANES), BF),
        jax.ShapeDtypeStruct((k_rows, pairs * LANES), BF),
    ]
    if prefix:
        out_specs += [column_spec(PRE_PAD, 0)] * 2
        out_shape += [jax.ShapeDtypeStruct((PRE_PAD, pairs * LANES), F32)] * 2
    return pl.pallas_call(
        functools.partial(attend_back_kernel, segs=segs, prefix=prefix),
        grid=(pairs,),
        in_specs=specs,
        out_specs=out_specs,
        out_shape=out_shape,
        compiler_params=params(),
        name="attend_back",
    )(*args)


def ffn_step(low_ref, acc_ref, in_ref, out_ref, slope_ref, act_ref, bias_ref, scale):
    for start, size in row_tiles(low_ref.shape[0]):
        rows = slice(start, start + size)
        hidden = nn(low_ref[rows], in_ref[...])
        if bias_ref is not None:
            hidden = hidden + bias_ref[...]
        active, slope = gelu_pair(hidden)
        slope_ref[rows] = slope.astype(BF)
        active = active.astype(BF)
        if act_ref is not None:
            act_ref[rows] = active
        term = nn(active, out_ref[...])
        acc_ref[rows] += term if scale is None else scale * term


def enc_ffn_kernel(
    x_ref, att_ref, wo_ref, gain_ref, in_ref, out_ref, down_ref, downb_ref, up_ref, upb_ref,
    mem_ref, slope_ref, act_ref, low_ref, scales_ref, acc_ref,
):
    step = pl.program_id(0)
    last = pl.num_programs(0) - 1

    @pl.when(step == 0)
    def _():
        for start, size in row_tiles(x_ref.shape[0]):
            rows = slice(start, start + size)
            first = x_ref[rows].astype(F32) + nn(att_ref[rows], wo_ref[...])
            hat, scale = norm_rows(first)
            normed = hat * gain_ref[0:1]
            acc_ref[rows] = normed
            low_ref[rows] = normed.astype(BF)
            scales_ref[rows, 0:1] = scale

    @pl.when((step > 0) & (step < last))
    def _():
        ffn_step(low_ref, acc_ref, in_ref, out_ref, slope_ref, None, None, None)

    @pl.when(step == last)
    def _():
        ffn_step(low_ref, acc_ref, down_ref, up_ref, slope_ref, act_ref, downb_ref, adapter_scale)
        for start, size in row_tiles(x_ref.shape[0]):
            rows = slice(start, start + size)
            hat, scale = norm_rows(acc_ref[rows] + adapter_scale * upb_ref[...])
            mem_ref[rows] = (hat * gain_ref[1:2]).astype(BF)
            scales_ref[rows, 1:2] = scale


def enc_ffn(x, att, w):
    rows, width = x.shape
    hidden = w["ffn_in"].shape[1]
    steps = hidden // chunk

    def at(i):
        return jnp.clip(i - 1, 0, steps - 1)

    return pl.pallas_call(
        enc_ffn_kernel,
        grid=(steps + 2,),
        in_specs=[
            whole((rows, width)),
            whole((rows, width)),
            whole((width, width)),
            whole((2, width)),
            pl.BlockSpec((width, chunk), lambda i: (0, at(i))),
            pl.BlockSpec((chunk, width), lambda i: (at(i), 0)),
            whole((width, chunk)),
            whole((1, chunk)),
            whole((chunk, width)),
            whole((1, width)),
        ],
        out_specs=[
            whole((rows, width)),
            pl.BlockSpec((rows, chunk), lambda i: (0, jnp.clip(i - 1, 0, steps))),
            whole((rows, chunk)),
            whole((rows, width)),
            whole((rows, LANES)),
        ],
        out_shape=[
            jax.ShapeDtypeStruct((rows, width), BF),
            jax.ShapeDtypeStruct((rows, hidden + chunk), BF),
            jax.ShapeDtypeStruct((rows, chunk), BF),
            jax.ShapeDtypeStruct((rows, width), BF),
            jax.ShapeDtypeStruct((rows, LANES), F32),
        ],
        scratch_shapes=[pltpu.VMEM((rows, width), F32)],
        compiler_params=params(),
        name="enc_ffn",
    )(
        x, att, w["out"], w["gains"], w["ffn_in"], w["ffn_out"],
        w["down"], w["down_bias"], w["up"], w["up_bias"],
    )


def ffn_back_step(grad_ref, acc_ref, in_ref, out_ref, slope_ref):
    for start, size in row_tiles(grad_ref.shape[0]):
        rows = slice(start, start + size)
        pre = (nt(grad_ref[rows], out_ref[...]) * slope_ref[rows].astype(F32)).astype(BF)
        acc_ref[rows] += nt(pre, in_ref[...])


def adapter_back(grad_ref, acc_ref, low_ref, act_ref, slope_ref, down_ref, up_ref, outs, pre_ref):
    ddown_ref, ddownb_ref, dup_ref, dupb_ref = outs
    total = None
    for start, size in row_tiles(grad_ref.shape[0]):
        rows = slice(start, start + size)
        back = adapter_scale * nt(grad_ref[rows], up_ref[...])
        pre = (back * slope_ref[rows].astype(F32)).astype(BF)
        pre_ref[rows] = pre
        sums = jnp.sum(pre.astype(F32), axis=0, keepdims=True)
        total = sums if total is None else total + sums
        acc_ref[rows] += nt(pre, down_ref[...])
    ddownb_ref[...] = total
    ddown_ref[...] = tn(low_ref[...], pre_ref[...])
    dup_ref[...] = adapter_scale * tn(act_ref[...], grad_ref[...])
    dupb_ref[...] = adapter_scale * jnp.sum(grad_ref[...].astype(F32), axis=0, keepdims=True)


def enc_ffn_back_kernel(
    dmem_ref, mem_ref, low_ref, scales_ref, gain_ref, slope_ref, act_ref,
    in_ref, out_ref, down_ref, up_ref, wo_ref,
    dfirst_ref, datt_ref, ddown_ref, ddownb_ref, dup_ref, dupb_ref,
    acc_ref, grad_ref, pre_ref,
):
    step = pl.program_id(0)
    last = pl.num_programs(0) - 1

    @pl.when(step == 0)
    def _():
        for start, size in row_tiles(dmem_ref.shape[0]):
            rows = slice(start, start + size)
            gain = gain_ref[1:2]
            hat = mem_ref[rows].astype(F32) / gain
            grad = norm_rows_back(
                hat, scales_ref[rows, 1:2], dmem_ref[rows].astype(F32) * gain
            )
            acc_ref[rows] = grad
            grad_ref[rows] = grad.astype(BF)
        adapter_back(
            grad_ref, acc_ref, low_ref, act_ref, slope_ref, down_ref, up_ref,
            (ddown_ref, ddownb_ref, dup_ref, dupb_ref), pre_ref,
        )

    @pl.when(step > 0)
    def _():
        ffn_back_step(grad_ref, acc_ref, in_ref, out_ref, slope_ref)

    @pl.when(step == last)
    def _():
        for start, size in row_tiles(dmem_ref.shape[0]):
            rows = slice(start, start + size)
            gain = gain_ref[0:1]
            hat = low_ref[rows].astype(F32) / gain
            grad = norm_rows_back(hat, scales_ref[rows, 0:1], acc_ref[rows] * gain)
            dfirst_ref[rows] = grad
            datt_ref[rows] = nt(grad.astype(BF), wo_ref[...]).astype(BF)


def enc_ffn_back(dmem, mem, low, scales, slope, act, w):
    rows, width = dmem.shape
    hidden = w["ffn_in"].shape[1]
    steps = hidden // chunk

    def at(i):
        return jnp.clip(i - 1, 0, steps - 1)

    return pl.pallas_call(
        enc_ffn_back_kernel,
        grid=(steps + 1,),
        in_specs=[
            whole((rows, width)),
            whole((rows, width)),
            whole((rows, width)),
            whole((rows, LANES)),
            whole((2, width)),
            pl.BlockSpec((rows, chunk), lambda i: (0, jnp.where(i == 0, steps, i - 1))),
            whole((rows, chunk)),
            pl.BlockSpec((width, chunk), lambda i: (0, at(i))),
            pl.BlockSpec((chunk, width), lambda i: (at(i), 0)),
            whole((width, chunk)),
            whole((chunk, width)),
            whole((width, width)),
        ],
        out_specs=[
            whole((rows, width)),
            whole((rows, width)),
            whole((width, chunk)),
            whole((1, chunk)),
            whole((chunk, width)),
            whole((1, width)),
        ],
        out_shape=[
            jax.ShapeDtypeStruct((rows, width), F32),
            jax.ShapeDtypeStruct((rows, width), BF),
            jax.ShapeDtypeStruct((width, chunk), F32),
            jax.ShapeDtypeStruct((1, chunk), F32),
            jax.ShapeDtypeStruct((chunk, width), F32),
            jax.ShapeDtypeStruct((1, width), F32),
        ],
        scratch_shapes=[
            pltpu.VMEM((rows, width), F32),
            pltpu.VMEM((rows, width), BF),
            pltpu.VMEM((rows, chunk), BF),
        ],
        compiler_params=params(),
        name="enc_ffn_back",
    )(
        dmem, mem, low, scales, w["gains"], slope, act,
        w["ffn_in"], w["ffn_out"], w["down"], w["up"], w["out"],
    )


def dec_mid_kernel(x_ref, att_ref, wo_ref, gain_ref, wq_ref, n_ref, scale_ref, cq_ref):
    for start, size in row_tiles(x_ref.shape[0], 256):
        rows = slice(start, start + size)
        first = x_ref[rows].astype(F32) + nn(att_ref[rows], wo_ref[...])
        hat, scale = norm_rows(first)
        normed = hat * gain_ref[0:1]
        n_ref[rows] = normed
        scale_ref[rows, 0:1] = scale
        cq_ref[rows] = nn(normed.astype(BF), wq_ref[...]).astype(BF)


def dec_mid(x, att, w, cross):
    rows, width = x.shape
    return pl.pallas_call(
        dec_mid_kernel,
        out_shape=[
            jax.ShapeDtypeStruct((rows, width), F32),
            jax.ShapeDtypeStruct((rows, LANES), F32),
            jax.ShapeDtypeStruct((rows, width), BF),
        ],
        compiler_params=params(),
        name="dec_mid",
    )(x, att, w["out"], w["gains"], cross["query"])


def dec_ffn_kernel(
    len_ref, n_ref, catt_ref, cot_ref, wco_ref, cgain_ref, gain_ref,
    in_ref, out_ref, down_ref, downb_ref, up_ref, upb_ref,
    y_ref, dsecond_ref, dcatt_ref, ddown_ref, ddownb_ref, dup_ref, dupb_ref,
    acc_ref, low_ref, grad_ref, slope_ref, act_ref, pre_ref, scale_ref,
    *, steps,
):
    step = pl.program_id(0)
    tiles = row_tiles(n_ref.shape[0], TGT)

    @pl.when(step == 0)
    def _():
        for start, size in tiles:
            rows = slice(start, start + size)
            second = n_ref[rows] + nn(catt_ref[rows], wco_ref[...])
            hat, scale = norm_rows(second)
            middle = hat * cgain_ref[...]
            acc_ref[rows] = middle
            low_ref[rows] = middle.astype(BF)
            scale_ref[rows, 0:1] = scale

    @pl.when((step > 0) & (step <= steps))
    def _():
        ffn_step(low_ref, acc_ref, in_ref, out_ref, slope_ref.at[step - 1], None, None, None)

    @pl.when(step == steps + 1)
    def _():
        ffn_step(
            low_ref, acc_ref, down_ref, up_ref, slope_ref.at[steps], act_ref, downb_ref,
            adapter_scale,
        )
        for tile, (start, size) in enumerate(tiles):
            rows = slice(start, start + size)
            gain = gain_ref[1:2]
            hat, scale = norm_rows(acc_ref[rows] + adapter_scale * upb_ref[...])
            valid = lax.broadcasted_iota(jnp.int32, (size, 1), 0) < len_ref[0, tile]
            y_ref[rows] = jnp.where(valid, hat * gain, 0.0).astype(BF)
            cot = jnp.where(valid, cot_ref[rows].astype(F32), 0.0)
            grad = norm_rows_back(hat, scale, cot * gain)
            acc_ref[rows] = grad
            grad_ref[rows] = grad.astype(BF)
        adapter_back(
            grad_ref, acc_ref, low_ref, act_ref, slope_ref.at[steps], down_ref, up_ref,
            (ddown_ref, ddownb_ref, dup_ref, dupb_ref), pre_ref,
        )

    @pl.when(step > steps + 1)
    def _():
        ffn_back_step(grad_ref, acc_ref, in_ref, out_ref, slope_ref.at[2 * steps + 1 - step])

    @pl.when(step == 2 * steps + 1)
    def _():
        for start, size in tiles:
            rows = slice(start, start + size)
            gain = cgain_ref[...]
            hat = low_ref[rows].astype(F32) / gain
            grad = norm_rows_back(hat, scale_ref[rows, 0:1], acc_ref[rows] * gain)
            dsecond_ref[rows] = grad
            dcatt_ref[rows] = nt(grad.astype(BF), wco_ref[...]).astype(BF)


def dec_ffn(lengths, n, catt, cot, w, cross):
    rows, width = n.shape
    hidden = w["ffn_in"].shape[1]
    steps = hidden // chunk

    def at(i):
        return jnp.where(i <= steps, jnp.clip(i - 1, 0, steps - 1), jnp.clip(2 * steps + 1 - i, 0, steps - 1))

    return pl.pallas_call(
        functools.partial(dec_ffn_kernel, steps=steps),
        grid=(2 * steps + 2,),
        in_specs=[
            pl.BlockSpec(memory_space=pltpu.SMEM),
            whole((rows, width)),
            whole((rows, width)),
            whole((rows, width)),
            whole((width, width)),
            whole((1, width)),
            whole((2, width)),
            pl.BlockSpec((width, chunk), lambda i: (0, at(i))),
            pl.BlockSpec((chunk, width), lambda i: (at(i), 0)),
            whole((width, chunk)),
            whole((1, chunk)),
            whole((chunk, width)),
            whole((1, width)),
        ],
        out_specs=[
            whole((rows, width)),
            whole((rows, width)),
            whole((rows, width)),
            whole((width, chunk)),
            whole((1, chunk)),
            whole((chunk, width)),
            whole((1, width)),
        ],
        out_shape=[
            jax.ShapeDtypeStruct((rows, width), BF),
            jax.ShapeDtypeStruct((rows, width), F32),
            jax.ShapeDtypeStruct((rows, width), BF),
            jax.ShapeDtypeStruct((width, chunk), F32),
            jax.ShapeDtypeStruct((1, chunk), F32),
            jax.ShapeDtypeStruct((chunk, width), F32),
            jax.ShapeDtypeStruct((1, width), F32),
        ],
        scratch_shapes=[
            pltpu.VMEM((rows, width), F32),
            pltpu.VMEM((rows, width), BF),
            pltpu.VMEM((rows, width), BF),
            pltpu.VMEM((steps + 1, rows, chunk), BF),
            pltpu.VMEM((rows, chunk), BF),
            pltpu.VMEM((rows, chunk), BF),
            pltpu.VMEM((rows, LANES), F32),
        ],
        compiler_params=params(),
        name="dec_ffn",
    )(
        lengths, n, catt, cot, cross["out"], cross["gain"], w["gains"],
        w["ffn_in"], w["ffn_out"], w["down"], w["down_bias"], w["up"], w["up_bias"],
    )


def dec_mid_back_kernel(
    dsecond_ref, dcq_ref, wq_ref, n_ref, scale_ref, gain_ref, wo_ref, dfirst_ref, datt_ref
):
    for start, size in row_tiles(n_ref.shape[0], 256):
        rows = slice(start, start + size)
        gain = gain_ref[0:1]
        total = dsecond_ref[rows] + nt(dcq_ref[rows], wq_ref[...])
        grad = norm_rows_back(n_ref[rows] / gain, scale_ref[rows, 0:1], total * gain)
        dfirst_ref[rows] = grad
        datt_ref[rows] = nt(grad.astype(BF), wo_ref[...]).astype(BF)


def dec_mid_back(dsecond, dcq, n, scale, w, cross):
    rows, width = n.shape
    return pl.pallas_call(
        dec_mid_back_kernel,
        out_shape=[
            jax.ShapeDtypeStruct((rows, width), F32),
            jax.ShapeDtypeStruct((rows, width), BF),
        ],
        compiler_params=params(),
        name="dec_mid_back",
    )(dsecond, dcq, cross["query"], n, scale, w["gains"], w["out"])


enc_segs = ((0, SRC_LONG, 0, SRC_LONG), (SRC_LONG, SRC_SHORT, SRC_LONG, SRC_SHORT))
dec_segs = ((0, TGT, 0, TGT), (TGT, TGT, TGT, TGT))
cross_segs = ((0, TGT, 0, SRC_LONG), (TGT, TGT, SRC_LONG, SRC_SHORT))


def encoder_forward(x, lengths, w):
    qkv = product(x, w["qkv"])
    att, inv, *weights = attend(
        lengths, (qkv, 0), (qkv, 8), (qkv, 16), w["prefix"], enc_segs, False
    )
    mem, slope, act, low, scales = enc_ffn(x, att, w)
    return mem, (qkv, att, inv, weights, mem, slope, act, low, scales)


def encoder_back_ffn(saved, dmem, w):
    mem, slope, act, low, scales = saved[4:]
    dfirst, datt, *adapter = enc_ffn_back(dmem, mem, low, scales, slope, act, w)
    return dfirst, datt, adapter


def encoder_back_self(saved, dfirst, datt, w):
    qkv, att, inv, weights = saved[:4]
    dq, dk, dv, *dprefix = attend_back(
        (qkv, 0), (qkv, 8), (qkv, 16), w["prefix"], att, inv, datt, weights, enc_segs
    )
    return back_product([dq, dk, dv], w["qkv"], dfirst), dprefix


def decoder_self(t, lengths, w, cross):
    qkv = product(t, w["qkv"])
    att, inv, *weights = attend(
        lengths, (qkv, 0), (qkv, 8), (qkv, 16), w["prefix"], dec_segs, True
    )
    n, scale, cq = dec_mid(t, att, w, cross)
    return cq, (qkv, att, inv, weights, n, scale)


def decoder_cross(kept, mem, cq, cot, src_lengths, tgt_lengths, w, cross):
    n = kept[4]
    kv = product(mem, cross["pairs"])
    catt, cinv, *cweights = attend(
        src_lengths, (cq, 0), (kv, 0), (kv, 8), None, cross_segs, False
    )
    y, dsecond, dcatt, *adapter = dec_ffn(tgt_lengths, n, catt, cot, w, cross)
    dcq, dck, dcv = attend_back(
        (cq, 0), (kv, 0), (kv, 8), None, catt, cinv, dcatt, cweights, cross_segs
    )
    dmem = back_product([dck, dcv], cross["pairs"])
    return y, dmem, dcq, dsecond, adapter


def decoder_self_back(kept, dsecond, dcq, w, cross):
    qkv, att, inv, weights, n, scale = kept
    dfirst, datt = dec_mid_back(dsecond, dcq, n, scale, w, cross)
    dq, dk, dv, *dprefix = attend_back(
        (qkv, 0), (qkv, 8), (qkv, 16), w["prefix"], att, inv, datt, weights, dec_segs
    )
    return back_product([dq, dk, dv], w["qkv"], dfirst), dprefix


def blank_kernel(*refs):
    pass


def blanks(shapes):
    return pl.pallas_call(
        blank_kernel,
        out_shape=list(shapes),
        out_specs=[pl.BlockSpec(memory_space=pl.ANY)] * len(shapes),
        name="blank",
    )()


def on_section(is_encoder, encoder_work, decoder_work, *operands):
    enc_shapes = jax.eval_shape(encoder_work, *operands)
    dec_shapes = jax.eval_shape(decoder_work, *operands)

    def blank_like(shapes):
        leaves, tree = jax.tree.flatten(shapes)
        if not leaves:
            return shapes
        return jax.tree.unflatten(tree, blanks(leaves))

    return lax.cond(
        is_encoder,
        lambda *a: (encoder_work(*a), blank_like(dec_shapes)),
        lambda *a: (blank_like(enc_shapes), decoder_work(*a)),
        *operands,
    )


def to_decoder(block):
    return lax.ppermute(block, "section", [(0, 1)])


def to_encoder(block):
    return lax.ppermute(block, "section", [(1, 0)])


def per_device(
    sources, targets, cotangent, source_lengths, target_lengths,
    attn_qkv, attn_out, ffn_in, ffn_out, norm_gains, prefix_pairs,
    adapt_down, adapt_down_bias, adapt_up, adapt_up_bias,
    cross_query, cross_pairs, cross_out, cross_gain,
):
    is_encoder = lax.axis_index("section") == 0
    prefix = jnp.pad(prefix_pairs[0], ((0, 0), (0, PRE_PAD - PRE), (0, 0)))
    w = dict(
        qkv=attn_qkv[0], out=attn_out[0], ffn_in=ffn_in[0], ffn_out=ffn_out[0],
        gains=norm_gains[0], prefix=(prefix[0], prefix[1]),
        down=adapt_down[0], down_bias=adapt_down_bias,
        up=adapt_up[0], up_bias=adapt_up_bias,
    )
    cross = dict(query=cross_query, pairs=cross_pairs, out=cross_out, gain=cross_gain[None])
    half = sources.shape[1] // 2
    replicas = lax.axis_size("dp")

    (mem, saved), (cq, kept) = on_section(
        is_encoder,
        lambda: encoder_forward(sources, source_lengths, w),
        lambda: decoder_self(targets, target_lengths, w, cross),
    )
    mem_here = to_decoder(mem)
    _, (y, dmem, dcq, dsecond, dec_adapter) = on_section(
        is_encoder,
        lambda *a: (),
        lambda *a: decoder_cross(*a, cotangent, source_lengths, target_lengths, w, cross),
        kept, mem_here, cq,
    )
    dmem_here = to_encoder(dmem)
    y_low = to_encoder(y[:, :half])
    (dfirst, datt, enc_adapter), (dt, dec_prefix) = on_section(
        is_encoder,
        lambda *a: encoder_back_ffn(a[0], a[1], w),
        lambda *a: decoder_self_back(a[2], a[3], a[4], w, cross),
        saved, dmem_here, kept, dsecond, dcq,
    )
    dt_low = to_encoder(dt[:, :half])
    adapter = [
        jnp.where(is_encoder, a, b) / replicas for a, b in zip(enc_adapter, dec_adapter)
    ]
    down, down_bias, up, up_bias = lax.psum(adapter, "dp")
    (dx, enc_prefix), _ = on_section(
        is_encoder,
        lambda *a: encoder_back_self(*a, w),
        lambda *a: (),
        saved, dfirst, datt,
    )
    dx_high = to_decoder(dx[:, half:])
    prefix_grad = jnp.stack(
        [jnp.where(is_encoder, a, b)[:PRE] for a, b in zip(enc_prefix, dec_prefix)]
    )
    prefix_grad, down, up = lax.optimization_barrier((prefix_grad, down, up))
    prefix_grad = lax.psum(prefix_grad / replicas, "dp")
    return (
        jnp.where(is_encoder, y_low, y[:, half:]),
        jnp.where(is_encoder, dx[:, :half], dx_high),
        jnp.where(is_encoder, dt_low, dt[:, half:]),
        prefix_grad[None],
        down[None],
        down_bias,
        up[None],
        up_bias,
    )


def solution(mesh):
    layer2, layer3, rows = P("section", None), P("section", None, None), P("dp", None)
    return jax.shard_map(
        per_device,
        mesh=mesh,
        in_specs=(
            rows, rows, rows, rows, rows,
            layer3, layer3, layer3, layer3, layer3,
            P("section", None, None, None),
            layer3, layer2, layer3, layer2,
            P(), P(), P(), P(),
        ),
        out_specs=(
            P("dp", "section"), P("dp", "section"), P("dp", "section"),
            P("section", None, None, None), layer3, layer2, layer3, layer2,
        ),
        check_vma=False,
    )
```

time: 1180 us -> 522 us (0.44)
  matrix products: 426 us -> 0 us
  waiting for transfers between devices: 536 us -> 273 us
  Pallas kernels: 0 us -> 149 us
  local copies, waits for them, and re-layouts: 91.5 us -> 13.3 us
  other arithmetic: 59.2 us -> 11.4 us
    dot_general x48 -> x0, matrix products: 426 us -> none  [the longest x11 84.5 us: matmul_nt(): lax.dot_general(left_side, right_side, (((1,), (1,)), ((), ())), preferre...]
    ppermute x6 -> x5, waiting for transfers between devices: 485 us -> 169 us  [the longest x3 144 us: to_encoder(): return lax.ppermute(block, 'section', [(1, 0)])]
    pallas_call x0 -> x9, Pallas kernels: none -> 149 us  [the longest x1 36.8 us: enc_ffn(): pl.pallas_call(enc_ffn_kernel, grid=(steps + 2,), in_specs=[whole((rows,...]
    psum x1 -> x2, waiting for transfers between devices: 51.1 us -> 104 us  [the longest x1 89.9 us: per_device(): prefix_grad = lax.psum(prefix_grad / replicas, 'dp')]
    slice x36 -> x3, local copies, waits for them, and re-layouts: 51 us -> 3.02 us  [the longest x1 1.2 us: per_device(): y_low = to_encoder(y[:, :half])]
    reduce_sum x19 -> x0, other arithmetic: 36.7 us -> none  [the longest x3 19.7 us: attend_forward(): row_totals = jnp.sum(exp_scores, axis=-1, keepdims=True)]
    another operation x12 -> x2, local copies, waits for them, and re-layouts: 21.7 us -> 0.21 us  [per_device(): jnp.stack([jnp.where(is_encoder, a, b)[:PRE] for a, b in zip(enc_prefix,...]
  transfers between devices with their start and end apart: 7 -> 7, of which waited for: 4 -> 5; matrix products, arithmetic and copies ran while one was open for 1% -> 2% of each run, Pallas kernels for 0% -> 8%
where the time goes in v1:
time: 522 us; the launch traced here: 517 us
  waiting for transfers between devices  273 us (52%)
  Pallas kernels  149 us (29%)
  blocking collectives  32.5 us (6%)
  starting transfers between devices  21.4 us (4%)
  between operations  14.4 us (3%)
  local copies, waits for them, and re-layouts  13.3 us (3%)
  other arithmetic  11.4 us (2%)
    ppermute x3, waiting for transfers between devices, to_encoder(): return lax.ppermute(block, 'section', [(1, 0)])  144 us
    psum x1, waiting for transfers between devices, per_device(): prefix_grad = lax.psum(prefix_grad / replicas, 'dp')  89.9 us
    pallas_call x1, Pallas kernels, enc_ffn(): pl.pallas_call(enc_ffn_kernel, grid=(steps + 2,), in_specs=[whole((rows,...  36.8 us
    pallas_call x1, Pallas kernels, enc_ffn_back(): pl.pallas_call(enc_ffn_back_kernel, grid=(steps + 1,), in_specs=[whole((r...  36 us
    psum x1, blocking collectives, per_device(): down, down_bias, up, up_bias = lax.psum(adapter, 'dp')  32.5 us
    pallas_call x1, Pallas kernels, attend_back(): pl.pallas_call(functools.partial(attend_back_kernel, segs=segs, prefix=pr...  30.2 us
    pallas_call x1, Pallas kernels, attend(): pl.pallas_call(functools.partial(attend_kernel, segs=segs, prefix=prefix,...  26.2 us
    ppermute x2, waiting for transfers between devices, to_decoder(): return lax.ppermute(block, 'section', [(0, 1)])  25.1 us
  transfers between devices with their start and end apart: 7, of which 5 were waited for; matrix products, arithmetic and copies ran while one was open for 2% of the time, Pallas kernels for 8%

profile of v1, /device:TPU:0, one launch (start us, length us, event | category | flops | bytes accessed | tf_op | source)
XLA Modules:
  0.0 516.5 jit_solution(13291501956286749542)
XLA Ops:
  8.2 76.7 %conditional.4 = (bf16[864,1024]{1,0:T(8,128)(2,1)}, bf16[864,3072]{1,0:T(8,128)(2,1)}, bf16[864,1024]{1,0:T(8,128)(2,1)}, f32[864,1024]{1,0:T(8,128)}, bf16[16,...) conditional(s32[]{:T(128)} %convert_element_type.4, ...), branch_computations={%region_0.1_spmd, %region_1.2_spmd} | conditional | bytes 20373824 | solution.py:787
  8.5 10.4 %product.4.refs_1_.refs_2_.refs_3_ = bf16[864,3072]{1,0:T(8,128)(2,1)} custom-call(bf16[864,1024]{1,0:T(8,128)(2,1)} %get-tuple-element.394.x_ref, bf16[1024,3072]{1,0:T(8,128)(2,1)} %get-tuple-element.177.w_ref), custom_call_target="tpu_custom_call" | custom-call | tf_op jit(solution)/shard_map/cond/branch_1_fun/product/pallas_call | solution.py:90
  18.9 26.2 %attend.4 = (bf16[864,1024]{1,0:T(8,128)(2,1)}, f32[864,1024]{1,0:T(8,128)}, bf16[16,800,768]{2,1,0:T(8,128)(2,1)}, bf16[16,128,96]{2,1,0:T(8,128)(2,1)}) custom-call(s32[1,2]{1,0:T(1,128)} %get-tuple-element.176.refs_0_, bf16[864,3072]{1,0:T(8,128)(2,1)} %product.4.refs_1_.refs_2_.refs_3_, bf16[864,3072]{1,0:T(8,128)(2,1)} %product.4.refs_1_.refs_2_.refs_3_, ...), custom_call_target="tpu_custom_call" | custom-call | tf_op jit(solution)/shard_map/cond/branch_1_fun/attend/pallas_call | solution.py:217
  45.2 36.8 %enc_ffn.1 = (bf16[864,1024]{1,0:T(8,128)(2,1)}, bf16[864,4608]{1,0:T(8,128)(2,1)}, bf16[864,512]{1,0:T(8,128)(2,1)}, bf16[864,1024]{1,0:T(8,128)(2,1)}, f32[864,128]{1,0:T(8,128)}) custom-call(bf16[864,1024]{1,0:T(8,128)(2,1)} %get-tuple-element.394.x_ref, bf16[864,1024]{1,0:T(8,128)(2,1)} %get-tuple-element.430.att_ref, bf16[1024,1024]{1,0:T(8,128)(2,1)S(1)} %copy-done.1, ...), custom_call_target="tpu_custom_call" | custom-call | tf_op jit(solution)/shard_map/cond/branch_1_fun/enc_ffn/pallas_call | solution.py:376
  82.0 2.9 copy.62
  84.9 15.2 %collective-permute-start = (bf16[864,1024]{1,0:T(8,128)(2,1)}, bf16[864,1024]{1,0:T(8,128)(2,1)S(1)}, u32[]{:S(2)}, u32[]{:S(2)}) collective-permute-start(bf16[864,1024]{1,0:T(8,128)(2,1)} %get-tuple-element.349), channel_id=1, source_target_pairs={{0,16},{1,17},{2,18},{3,19},{4,20},{5,21},{6,22},{7,23},{8,24},{9,... | collective-permute-start | bytes 5308424 | tf_op jit(solution)/shard_map/ppermute | solution.py:796
  100.1 25.1 %collective-permute-done = bf16[864,1024]{1,0:T(8,128)(2,1)S(1)} collective-permute-done((bf16[864,1024]{1,0:T(8,128)(2,1)}, bf16[864,1024]{1,0:T(8,128)(2,1)S(1)}, u32[]{:S(2)}, u32[]{:S(2)}) %collective-permute-start) | collective-permute-done | bytes 1769504 | tf_op jit(solution)/shard_map/ppermute | solution.py:796
  126.5 130.5 %collective-permute-done.2 = bf16[864,1024]{1,0:T(8,128)(2,1)} collective-permute-done((bf16[864,1024]{1,0:T(8,128)(2,1)}, bf16[864,1024]{1,0:T(8,128)(2,1)}, u32[]{:S(2)}, u32[]{:S(2)}) %collective-permute-start.2) | collective-permute-done | bytes 1769504 | tf_op jit(solution)/shard_map/ppermute | solution.py:800
  257.0 36.2 %conditional.6 = (f32[864,1024]{1,0:T(8,128)}, bf16[864,1024]{1,0:T(8,128)(2,1)}, f32[1024,512]{1,0:T(8,128)}, f32[1,512]{1,0:T(1,128)S(1)}, f32[512,1024]{1,0:T...) conditional(s32[]{:T(128)} %convert_element_type.4, ...), branch_computations={%region_4.5_spmd, %region_5.6_spmd} | conditional | bytes 13631616 | solution.py:787
  257.2 36.0 %enc_ffn_back.1 = (f32[864,1024]{1,0:T(8,128)}, bf16[864,1024]{1,0:T(8,128)(2,1)}, f32[1024,512]{1,0:T(8,128)}, f32[1,512]{1,0:T(1,128)S(1)}, f32[512,1024]{1,0:T(8,128)}, /*index=5*/f32[1,1024]{1,0:T(1,128)S(1)}) custom-call(bf16[864,1024]{1,0:T(8,128)(2,1)} %get-tuple-element.263.dmem_ref, bf16[864,1024]{1,0:T(8,128)(2,1)} %get-tuple-element.264.mem_ref, ...), custom_call_target="tpu_custom_call" | custom-call | tf_op jit(solution)/shard_map/cond/branch_1_fun/enc_ffn_back/pallas_call | solution.py:486
  293.2 3.7 select_multiply_fusion
  296.9 1.8 select_multiply_fusion.1
  301.3 13.8 %collective-permute-done.1 = bf16[512,512]{1,0:T(8,128)(2,1)S(1)} collective-permute-done((bf16[512,512]{1,0:T(8,128)(2,1)S(1)}, bf16[512,512]{1,0:T(8,128)(2,1)S(1)}, u32[]{:S(2)}, u32[]{:S(2)}) %collective-permute-start.1) | collective-permute-done | bytes 524320 | tf_op jit(solution)/shard_map/ppermute | solution.py:800
  315.1 1.9 slice_select_fusion.2
  319.1 40.4 %conditional.7 = ((bf16[864,1024]{1,0:T(8,128)(2,1)S(1)}, f32[32,1024]{1,0:T(8,128)S(1)}, f32[32,1024]{1,0:T(8,128)})) conditional(s32[]{:T(128)} %convert_element_type.4, () %tuple.43, (bf16[864,3072]{1,0:T(8,128)(2,1)}, bf16[864,1024]{1,0:T(8,128)(2,1)S(1)}, f32[864,1024]{1,0:T(8,128)}, bf16[864,1024]{1,0:T(8,128)(2,1)}, ...), branch_computations={%region_6.7_spmd, %region_7.8_spmd} | conditional | bytes 14155836 | solution.py:787
  319.5 30.2 %attend_back.5 = (bf16[864,1024]{1,0:T(8,128)(2,1)}, bf16[864,1024]{1,0:T(8,128)(2,1)}, bf16[864,1024]{1,0:T(8,128)(2,1)}, f32[32,1024]{1,0:T(8,128)S(1)}, f32[32,1024]{1,0:T(8,128)}) custom-call(bf16[864,3072]{1,0:T(8,128)(2,1)} %get-tuple-element.284.refs_0_.refs_1_.refs_2_, bf16[864,3072]{1,0:T(8,128)(2,1)} %get-tuple-element.284.refs_0_.refs_1_.refs_2_, ...), custom_call_target="tpu_custom_call" | custom-call | tf_op jit(solution)/shard_map/cond/branch_1_fun/attend_back/pallas_call | solution.py:310
  349.7 9.8 %back_product.5 = bf16[864,1024]{1,0:T(8,128)(2,1)S(1)} custom-call(bf16[864,1024]{1,0:T(8,128)(2,1)} %get-tuple-element.292.refs_0_, bf16[864,1024]{1,0:T(8,128)(2,1)} %get-tuple-element.293.refs_1_, bf16[864,1024]{1,0:T(8,128)(2,1)} %get-tuple-element.294.refs_2_, bf16[1024,3072]{1,0:T(8,128)(2,1)} %get-tuple-element.295.refs_3_, f32[864,1024]{1,0:T(8,128)S(1)} %copy-done.11), custom_call_target="tpu_custom_call" | custom-call | tf_op jit(solution)/shard_map/cond/branch_1_fun/back_product/pallas_call | solution.py:126
  360.6 2.2 collective-permute-start.3
  363.1 32.5 %all-reduce.1 = (f32[1,512]{1,0:T(1,128)}, f32[1,1024]{1,0:T(1,128)}) all-reduce(f32[1,512]{1,0:T(1,128)S(1)} %fusion.4, f32[1,1024]{1,0:T(1,128)S(1)} %fusion.3), channel_id=1, replica_groups=mesh['section'=2,'dp'=16] {'dp'}, use_global_device_ids=true, to_apply=%region_11.12 | all-reduce | flops 1536 | bytes 12288 | tf_op jit(solution)/shard_map/psum | solution.py:845
  395.9 1.9 slice_select_fusion.1
  397.8 13.8 %all-reduce.8.cloned.1.call-done = (f32[1024,512]{1,0:T(8,128)}, f32[512,1024]{1,0:T(8,128)}) async-done(((f32[1024,512]{1,0:T(8,128)}, f32[512,1024]{1,0:T(8,128)}), (f32[1024,512]{1,0:T(8,128)}, f32[512,1024]{1,0:T(8,128)})) %all-reduce.8.cloned.1.call-update) | async-done | bytes 4194320 | tf_op jit(solution)/shard_map/psum | solution.py:845
  413.4 89.9 %all-reduce.6.cloned.1.call-done = f32[1,2,30,1024]{3,1,2,0:T(2,128)} async-done(((f32[1,2,30,1024]{3,1,2,0:T(2,128)}), f32[1,2,30,1024]{3,1,2,0:T(2,128)}) %all-reduce.6.cloned.1.call-update) | async-done | bytes 245776 | tf_op jit(solution)/shard_map/psum | solution.py:857
  503.3 1.7 copy.118
  505.0 3.2 copy.119
  (56 shorter events, 11.6 us)
Async XLA Ops:
  7.2 404.4 %all-reduce.8.cloned.1.call-start = ((), (), s32[]{:S(2)}) async-start(), calls=%async_computation.1 | async-start | bytes 8388608 | tf_op jit(solution)/shard_map/psum | solution.py:845
  18.9 26.2 %copy-start.1 = (bf16[1024,1024]{1,0:T(8,128)(2,1)S(1)}, bf16[1024,1024]{1,0:T(8,128)(2,1)}, u32[]{:S(2)}) copy-start(bf16[1024,1024]{1,0:T(8,128)(2,1)} %get-tuple-element.181.wo_ref) | copy-start | bytes 6291460 | tf_op jit(solution)/shard_map/cond
  18.9 26.2 %copy-start.3 = (bf16[1024,512]{1,0:T(8,128)(2,1)S(1)}, bf16[1024,512]{1,0:T(8,128)(2,1)}, u32[]{:S(2)}) copy-start(bf16[1024,512]{1,0:T(8,128)(2,1)} %get-tuple-element.185.down_ref) | copy-start | bytes 3145732 | tf_op jit(solution)/shard_map/cond
  18.9 26.2 %copy-start.5 = (bf16[512,1024]{1,0:T(8,128)(2,1)S(1)}, bf16[512,1024]{1,0:T(8,128)(2,1)}, u32[]{:S(2)}) copy-start(bf16[512,1024]{1,0:T(8,128)(2,1)} %get-tuple-element.187.up_ref) | copy-start | bytes 3145732 | tf_op jit(solution)/shard_map/cond
  18.9 26.3 %copy-start.17 = (f32[2,1024]{1,0:T(2,128)S(1)}, f32[2,1024]{1,0:T(2,128)}, u32[]{:S(2)}) copy-start(f32[2,1024]{1,0:T(2,128)} %get-tuple-element.182.gain_ref) | copy-start | bytes 24580 | tf_op jit(solution)/shard_map/cond
  18.9 26.2 %copy-start.20 = (f32[1,1024]{1,0:T(1,128)S(1)}, f32[1,1024]{1,0:T(1,128)}, u32[]{:S(2)}) copy-start(f32[1,1024]{1,0:T(1,128)} %get-tuple-element.188.upb_ref) | copy-start | bytes 12292 | tf_op jit(solution)/shard_map/cond
  18.9 26.2 %copy-start.22 = (f32[1,512]{1,0:T(1,128)S(1)}, f32[1,512]{1,0:T(1,128)}, u32[]{:S(2)}) copy-start(f32[1,512]{1,0:T(1,128)} %get-tuple-element.186.downb_ref) | copy-start | bytes 6148 | tf_op jit(solution)/shard_map/cond
  84.9 40.3 %collective-permute-start = (bf16[864,1024]{1,0:T(8,128)(2,1)}, bf16[864,1024]{1,0:T(8,128)(2,1)S(1)}, u32[]{:S(2)}, u32[]{:S(2)}) collective-permute-start(bf16[864,1024]{1,0:T(8,128)(2,1)} %get-tuple-element.349), channel_id=1, source_target_pairs={{0,16},{1,17},{2,18},{3,19},{4,20},{5,21},{6,22},{7,23},{8,24},{9,... | collective-permute-start | bytes 5308424 | tf_op jit(solution)/shard_map/ppermute | solution.py:796
  125.2 131.8 %collective-permute-start.2 = (bf16[864,1024]{1,0:T(8,128)(2,1)}, bf16[864,1024]{1,0:T(8,128)(2,1)}, u32[]{:S(2)}, u32[]{:S(2)}) collective-permute-start(bf16[864,1024]{1,0:T(8,128)(2,1)} %get-tuple-element.364), channel_id=1, source_target_pairs={{16,0},{17,1},{18,2},{19,3},{20,4},{21,5},{22,6},{23,7},{24,8},{25... | collective-permute-start | bytes 5308424 | tf_op jit(solution)/shard_map/ppermute | solution.py:800
  293.2 3.7 copy-start.13
  293.2 3.7 copy-start.14
  298.8 20.3 %copy-start.9 = (bf16[864,1024]{1,0:T(8,128)(2,1)S(1)}, bf16[864,1024]{1,0:T(8,128)(2,1)}, u32[]{:S(2)}) copy-start(bf16[864,1024]{1,0:T(8,128)(2,1)} %get-tuple-element.354) | copy-start | bytes 5308420
  298.8 204.5 %all-reduce.6.cloned.1.call-start = ((), (), s32[]{:S(2)}) async-start(), calls=%async_computation | async-start | bytes 491520 | tf_op jit(solution)/shard_map/psum | solution.py:857
  300.0 15.1 %collective-permute-start.1 = (bf16[512,512]{1,0:T(8,128)(2,1)S(1)}, bf16[512,512]{1,0:T(8,128)(2,1)S(1)}, u32[]{:S(2)}, u32[]{:S(2)}) collective-permute-start(bf16[512,512]{1,0:T(8,128)(2,1)S(1)} %slice.32), channel_id=1, source_target_pairs={{16,0},{17,1},{18,2},{19,3},{20,4},{21,5},{22,6},{23,7},{24,8},{25... | collective-permute-start | bytes 1572872 | tf_op jit(solution)/shard_map/ppermute | solution.py:800
  317.8 78.1 %collective-permute-start.4 = (bf16[512,512]{1,0:T(8,128)(2,1)}, bf16[512,512]{1,0:T(8,128)(2,1)}, u32[]{:S(2)}, u32[]{:S(2)}) collective-permute-start(bf16[512,512]{1,0:T(8,128)(2,1)} %slice.36), channel_id=1, source_target_pairs={{16,0},{17,1},{18,2},{19,3},{20,4},{21,5},{22,6},{23,7},{24,8},{25... | collective-permute-start | bytes 1572872 | tf_op jit(solution)/shard_map/ppermute | solution.py:800
  319.5 30.2 %copy-start.11 = (f32[864,1024]{1,0:T(8,128)S(1)}, f32[864,1024]{1,0:T(8,128)}, u32[]{:S(2)}) copy-start(f32[864,1024]{1,0:T(8,128)} %get-tuple-element.296.refs_4_) | copy-start | bytes 10616836 | tf_op jit(solution)/shard_map/cond
  359.5 3.3 copy-start.19
  359.5 3.3 copy-start.29
  359.5 3.5 copy-start.25
  360.6 51.9 %collective-permute-start.3 = (bf16[864,512]{1,0:T(8,128)(2,1)}, bf16[864,512]{1,0:T(8,128)(2,1)}, u32[]{:S(2)}, u32[]{:S(2)}) collective-permute-start(bf16[864,512]{1,0:T(8,128)(2,1)} %slice.35), channel_id=1, source_target_pairs={{0,16},{1,17},{2,18},{3,19},{4,20},{5,21},{6,22},{7,23},{8,24},{9,... | collective-permute-start | bytes 2654216 | tf_op jit(solution)/shard_map/ppermute | solution.py:796
  505.0 3.2 copy-start.15
Sparse Core Ops, SparseCore 0:
  298.9 112.6 all-reduce.7
  415.9 87.3 all-reduce.5

commit v2 on v1

--- a/solution.py
+++ b/solution.py
@@ -761,6 +761,150 @@
     return back_product([dq, dk, dv], w["qkv"], dfirst), dprefix
 
 
+def packed_rows(devices):
+    unit = 16 * devices
+    return -(-(2 * chunk + 2 * PRE_PAD + 16) // unit) * unit
+
+
+def group_sum_kernel(
+    up_ref, down_ref, pk_ref, pv_ref, upb_ref, downb_ref,
+    o_up_ref, o_down_ref, o_pk_ref, o_pv_ref, o_bias_ref,
+    mine, theirs, half_sum, landed, total, result,
+    pair_sems, spread_sems, gather_sems, back_sems,
+    *, devices,
+):
+    chips = devices // 2
+    rows = packed_rows(devices)
+    half, part = rows // 2, rows // devices
+    place = lax.axis_index("dp")
+    core, chip = lax.rem(place, 2), place // 2
+    partner = place + 1 - 2 * core
+
+    def peer(distance):
+        return lax.rem(chip + distance, chips) * 2 + core
+
+    barrier = pltpu.get_barrier_semaphore()
+    for other in [partner] + [peer(s) for s in range(1, chips)]:
+        pl.semaphore_signal(barrier, inc=1, device_id={"dp": other}, device_id_type=pl.DeviceIdType.MESH)
+
+    width = 2 * chunk
+    scale = 1.0 / devices
+    mine[0:chunk] = (up_ref[...] * scale).astype(BF)
+    mine[chunk:width, 0:chunk] = (down_ref[0:chunk] * scale).astype(BF)
+    mine[chunk:width, chunk:width] = (down_ref[chunk:width] * scale).astype(BF)
+    mine[width : width + PRE_PAD] = (pk_ref[...] * scale).astype(BF)
+    mine[width + PRE_PAD : width + 2 * PRE_PAD] = (pv_ref[...] * scale).astype(BF)
+    at = width + 2 * PRE_PAD
+    row = lax.broadcasted_iota(jnp.int32, (16, width), 0)
+    down_row = jnp.concatenate([downb_ref[...], jnp.zeros_like(downb_ref)], 1)
+    bias = jnp.where(row == 0, upb_ref[...], jnp.where(row == 1, down_row, 0.0)) * scale
+    mine[at : at + 16] = bias.astype(BF)
+    if rows > at + 16:
+        mine[at + 16 : rows] = jnp.zeros((rows - at - 16, width), BF)
+    pl.semaphore_wait(barrier, chips)
+
+    def remote(source, target, send_sem, recv_sem, other):
+        return pltpu.make_async_remote_copy(
+            src_ref=source, dst_ref=target, send_sem=send_sem, recv_sem=recv_sem,
+            device_id={"dp": other}, device_id_type=pl.DeviceIdType.MESH,
+        )
+
+    kept = pl.multiple_of(core * half, 16)
+    given = pl.multiple_of((1 - core) * half, 16)
+    swap = remote(
+        mine.at[pl.ds(given, half)], theirs, pair_sems.at[0], pair_sems.at[1], partner
+    )
+    swap.start()
+    swap.wait()
+    half_sum[...] = (
+        mine[pl.ds(kept, half)].astype(F32) + theirs[...].astype(F32)
+    ).astype(BF)
+    spread = []
+    for s in range(1, chips):
+        other_chip = lax.rem(chip + s, chips)
+        copy = remote(
+            half_sum.at[pl.ds(pl.multiple_of(other_chip * part, 16), part)],
+            landed.at[s - 1],
+            spread_sems.at[0, s - 1], spread_sems.at[1, s - 1], peer(s),
+        )
+        copy.start()
+        spread.append(copy)
+    summed = half_sum[pl.ds(pl.multiple_of(chip * part, 16), part)].astype(F32)
+    for s in range(1, chips):
+        spread[s - 1].wait()
+        summed = summed + landed[s - 1].astype(F32)
+    total[...] = summed.astype(BF)
+
+    here = pl.multiple_of(kept + chip * part, 16)
+    result[pl.ds(here, part)] = total[...]
+    gather = []
+    for s in range(1, chips):
+        copy = remote(
+            total, result.at[pl.ds(here, part)],
+            gather_sems.at[0, s - 1], gather_sems.at[1, s - 1], peer(s),
+        )
+        copy.start()
+        gather.append(copy)
+    back = [
+        remote(
+            total, result.at[pl.ds(here, part)], back_sems.at[0, 0], back_sems.at[1, 0], partner
+        )
+    ]
+    back[0].start()
+    for s in range(1, chips):
+        gather[s - 1].wait()
+        source = lax.rem(chip + chips - s, chips)
+        rows_there = pl.ds(pl.multiple_of(kept + source * part, 16), part)
+        copy = remote(
+            result.at[rows_there], result.at[rows_there],
+            back_sems.at[0, s], back_sems.at[1, s], partner,
+        )
+        copy.start()
+        back.append(copy)
+    for copy in back:
+        copy.wait()
+    o_up_ref[...] = result[0:chunk].astype(F32)
+    o_down_ref[0:chunk] = result[chunk:width, 0:chunk].astype(F32)
+    o_down_ref[chunk:width] = result[chunk:width, chunk:width].astype(F32)
+    o_pk_ref[...] = result[width : width + PRE_PAD].astype(F32)
+    o_pv_ref[...] = result[width + PRE_PAD : width + 2 * PRE_PAD].astype(F32)
+    o_bias_ref[...] = result[at : at + 16].astype(F32)
+
+
+def group_sum(up, down, pk, pv, up_bias, down_bias):
+    devices = lax.axis_size("dp")
+    rows = packed_rows(devices)
+    chips = devices // 2
+    width = up.shape[1]
+    part = rows // devices
+    return pl.pallas_call(
+        functools.partial(group_sum_kernel, devices=devices),
+        out_shape=[
+            jax.ShapeDtypeStruct(up.shape, F32),
+            jax.ShapeDtypeStruct(down.shape, F32),
+            jax.ShapeDtypeStruct(pk.shape, F32),
+            jax.ShapeDtypeStruct(pv.shape, F32),
+            jax.ShapeDtypeStruct((16, width), F32),
+        ],
+        scratch_shapes=[
+            pltpu.VMEM((rows, width), BF),
+            pltpu.VMEM((rows // 2, width), BF),
+            pltpu.VMEM((rows // 2, width), BF),
+            pltpu.VMEM((chips - 1, part, width), BF),
+            pltpu.VMEM((part, width), BF),
+            pltpu.VMEM((rows, width), BF),
+            pltpu.SemaphoreType.DMA((2,)),
+            pltpu.SemaphoreType.DMA((2, chips - 1)),
+            pltpu.SemaphoreType.DMA((2, chips - 1)),
+            pltpu.SemaphoreType.DMA((2, chips)),
+        ],
+        compiler_params=pltpu.CompilerParams(
+            vmem_limit_bytes=vmem_bytes, collective_id=0, has_side_effects=True
+        ),
+        name="group_sum",
+    )(up, down, pk, pv, up_bias, down_bias)
+
+
 def blank_kernel(*refs):
     pass
 
@@ -775,8 +919,8 @@
 
 
 def on_section(is_encoder, encoder_work, decoder_work, *operands):
-    enc_shapes = jax.eval_shape(encoder_work, *operands)
-    dec_shapes = jax.eval_shape(decoder_work, *operands)
+    enc_shapes, _ = jax.eval_shape(encoder_work, *operands)
+    dec_shapes, _ = jax.eval_shape(decoder_work, *operands)
 
     def blank_like(shapes):
         leaves, tree = jax.tree.flatten(shapes)
@@ -784,12 +928,15 @@
             return shapes
         return jax.tree.unflatten(tree, blanks(leaves))
 
-    return lax.cond(
-        is_encoder,
-        lambda *a: (encoder_work(*a), blank_like(dec_shapes)),
-        lambda *a: (blank_like(enc_shapes), decoder_work(*a)),
-        *operands,
-    )
+    def encoder_branch(*a):
+        own, shared = encoder_work(*a)
+        return own, blank_like(dec_shapes), shared
+
+    def decoder_branch(*a):
+        own, shared = decoder_work(*a)
+        return blank_like(enc_shapes), own, shared
+
+    return lax.cond(is_encoder, encoder_branch, decoder_branch, *operands)
 
 
 def to_decoder(block):
@@ -816,54 +963,51 @@
     )
     cross = dict(query=cross_query, pairs=cross_pairs, out=cross_out, gain=cross_gain[None])
     half = sources.shape[1] // 2
-    replicas = lax.axis_size("dp")
-
-    (mem, saved), (cq, kept) = on_section(
+
+    (mem, saved), (cq, kept), _ = on_section(
         is_encoder,
-        lambda: encoder_forward(sources, source_lengths, w),
-        lambda: decoder_self(targets, target_lengths, w, cross),
+        lambda: (encoder_forward(sources, source_lengths, w), ()),
+        lambda: (decoder_self(targets, target_lengths, w, cross), ()),
     )
     mem_here = to_decoder(mem)
-    _, (y, dmem, dcq, dsecond, dec_adapter) = on_section(
+    _, (y, dmem, dcq, dsecond, dec_adapter), _ = on_section(
         is_encoder,
-        lambda *a: (),
-        lambda *a: decoder_cross(*a, cotangent, source_lengths, target_lengths, w, cross),
+        lambda *a: ((), ()),
+        lambda *a: (decoder_cross(*a, cotangent, source_lengths, target_lengths, w, cross), ()),
         kept, mem_here, cq,
     )
     dmem_here = to_encoder(dmem)
-    y_low = to_encoder(y[:, :half])
-    (dfirst, datt, enc_adapter), (dt, dec_prefix) = on_section(
+
+    def encoder_c1(saved, dmem, kept, dsecond, dcq, dec_adapter):
+        dfirst, datt, adapter = encoder_back_ffn(saved, dmem, w)
+        return (dfirst, datt), adapter
+
+    def decoder_c1(saved, dmem, kept, dsecond, dcq, dec_adapter):
+        return decoder_self_back(kept, dsecond, dcq, w, cross), dec_adapter
+
+    (dfirst, datt), (dt, dec_prefix), adapter = on_section(
+        is_encoder, encoder_c1, decoder_c1, saved, dmem_here, kept, dsecond, dcq, dec_adapter
+    )
+    low_halves = to_encoder(jnp.concatenate([y[:, :half], dt[:, :half]], 0))
+    dx, _, prefix_grads = on_section(
         is_encoder,
-        lambda *a: encoder_back_ffn(a[0], a[1], w),
-        lambda *a: decoder_self_back(a[2], a[3], a[4], w, cross),
-        saved, dmem_here, kept, dsecond, dcq,
-    )
-    dt_low = to_encoder(dt[:, :half])
-    adapter = [
-        jnp.where(is_encoder, a, b) / replicas for a, b in zip(enc_adapter, dec_adapter)
-    ]
-    down, down_bias, up, up_bias = lax.psum(adapter, "dp")
-    (dx, enc_prefix), _ = on_section(
-        is_encoder,
-        lambda *a: encoder_back_self(*a, w),
-        lambda *a: (),
-        saved, dfirst, datt,
+        lambda saved, dfirst, datt, dec_prefix: encoder_back_self(saved, dfirst, datt, w),
+        lambda saved, dfirst, datt, dec_prefix: ((), dec_prefix),
+        saved, dfirst, datt, dec_prefix,
     )
     dx_high = to_decoder(dx[:, half:])
-    prefix_grad = jnp.stack(
-        [jnp.where(is_encoder, a, b)[:PRE] for a, b in zip(enc_prefix, dec_prefix)]
-    )
-    prefix_grad, down, up = lax.optimization_barrier((prefix_grad, down, up))
-    prefix_grad = lax.psum(prefix_grad / replicas, "dp")
+    ddown, ddownb, dup, dupb = adapter
+    up, down, pk, pv, bias = group_sum(dup, ddown, *prefix_grads, dupb, ddownb)
+    targets_rows = y.shape[0]
     return (
-        jnp.where(is_encoder, y_low, y[:, half:]),
+        jnp.where(is_encoder, low_halves[:targets_rows], y[:, half:]),
         jnp.where(is_encoder, dx[:, :half], dx_high),
-        jnp.where(is_encoder, dt_low, dt[:, half:]),
-        prefix_grad[None],
+        jnp.where(is_encoder, low_halves[targets_rows:], dt[:, half:]),
+        jnp.stack([pk[:PRE], pv[:PRE]])[None],
         down[None],
-        down_bias,
+        bias[1:2, : down.shape[1]],
         up[None],
-        up_bias,
+        bias[0:1],
     )
 
 

time: 522 us -> 425 us (0.81)
  the two profiles are of different devices: /device:TPU:0 before, /device:TPU:31 now
where the time goes in v2:
time: 425 us; the launch traced here: 421 us
  Pallas kernels  226 us (53%)
  waiting for transfers between devices  106 us (25%)
  starting transfers between devices  63.9 us (15%)
  local copies, waits for them, and re-layouts  15.7 us (4%)
  loops' own time  4.79 us (1%)
    pallas_call x1, Pallas kernels, group_sum(): pl.pallas_call(functools.partial(group_sum_kernel, devices=devices), out_...  76.9 us
    ppermute x2, waiting for transfers between devices, to_decoder(): return lax.ppermute(block, 'section', [(0, 1)])  72.3 us
    ppermute x2, starting transfers between devices, to_encoder(): return lax.ppermute(block, 'section', [(1, 0)])  47.3 us
    pallas_call x1, Pallas kernels, dec_ffn(): pl.pallas_call(functools.partial(dec_ffn_kernel, steps=steps), grid=(2 *...  43.7 us
    ppermute x2, waiting for transfers between devices, to_encoder(): return lax.ppermute(block, 'section', [(1, 0)])  34.1 us
    pallas_call x2, Pallas kernels, attend(): pl.pallas_call(functools.partial(attend_kernel, segs=segs, prefix=prefix,...  31.4 us
    pallas_call x2, Pallas kernels, attend_back(): pl.pallas_call(functools.partial(attend_back_kernel, segs=segs, prefix=pr...  29.6 us
    ppermute x2, starting transfers between devices, to_decoder(): return lax.ppermute(block, 'section', [(0, 1)])  16.7 us
  transfers between devices with their start and end apart: 4, of which 2 were waited for; matrix products, arithmetic and copies ran while one was open for 2% of the time, Pallas kernels for 18%

profile of v2, /device:TPU:31, one launch (start us, length us, event | category | flops | bytes accessed | tf_op | source)
XLA Modules:
  0.0 420.6 jit_solution(11058340913149047950)
XLA Ops:
  1.6 29.4 %conditional.4 = (bf16[864,1024]{1,0:T(8,128)(2,1)}, bf16[864,3072]{1,0:T(8,128)(2,1)}, bf16[864,1024]{1,0:T(8,128)(2,1)}, f32[864,1024]{1,0:T(8,128)}, bf16[16,...) conditional(s32[]{:T(128)} %convert_element_type.4, ...), branch_computations={%region_0.1_spmd, %region_1.2_spmd} | conditional | bytes 20373824 | solution.py:939
  1.6 7.1 %product.3.refs_1_.refs_2_.refs_3_ = bf16[512,3072]{1,0:T(8,128)(2,1)S(1)} custom-call(bf16[512,1024]{1,0:T(8,128)(2,1)} %get-tuple-element.438.x_ref, bf16[1024,3072]{1,0:T(8,128)(2,1)} %get-tuple-element.200.w_ref), custom_call_target="tpu_custom_call" | custom-call | tf_op jit(solution)/shard_map/cond/branch_0_fun/product/pallas_call | solution.py:90
  8.8 15.7 %attend.3 = (bf16[512,1024]{1,0:T(8,128)(2,1)}, f32[512,1024]{1,0:T(8,128)}, bf16[16,288,256]{2,1,0:T(8,128)(2,1)}, bf16[16,288,256]{2,1,0:T(8,128)(2,1)}) custom-call(s32[1,2]{1,0:T(1,128)S(1)} %copy-done.30, bf16[512,3072]{1,0:T(8,128)(2,1)S(1)} %product.3.refs_1_.refs_2_.refs_3_, bf16[512,3072]{1,0:T(8,128)(2,1)S(1)} %product.3.refs_1_.refs_2_.refs_3_, ...), custom_call_target="tpu_custom_call" | custom-call | tf_op jit(solution)/shard_map/cond/branch_0_fun/attend/pallas_call | solution.py:217
  24.5 6.1 %dec_mid.1 = (f32[512,1024]{1,0:T(8,128)}, f32[512,128]{1,0:T(8,128)S(1)}, bf16[512,1024]{1,0:T(8,128)(2,1)}) custom-call(bf16[512,1024]{1,0:T(8,128)(2,1)} %get-tuple-element.438.x_ref, bf16[512,1024]{1,0:T(8,128)(2,1)} %get-tuple-element.480.att_ref, bf16[1024,1024]{1,0:T(8,128)(2,1)S(1)} %copy-done, f32[2,1024]{1,0:T(2,128)S(1)} %copy-done.19, ...), custom_call_target="tpu_custom_call" | custom-call | tf_op jit(solution)/shard_map/cond/branch_0_fun/dec_mid/pallas_call | solution.py:545
  31.0 15.2 %collective-permute-start = (bf16[864,1024]{1,0:T(8,128)(2,1)}, bf16[864,1024]{1,0:T(8,128)(2,1)S(1)}, u32[]{:S(2)}, u32[]{:S(2)}) collective-permute-start(bf16[864,1024]{1,0:T(8,128)(2,1)} %get-tuple-element.392), channel_id=1, source_target_pairs={{0,16},{1,17},{2,18},{3,19},{4,20},{5,21},{6,22},{7,23},{8,24},{9,... | collective-permute-start | bytes 5308424 | tf_op jit(solution)/shard_map/ppermute | solution.py:943
  46.2 72.3 %collective-permute-done = bf16[864,1024]{1,0:T(8,128)(2,1)S(1)} collective-permute-done((bf16[864,1024]{1,0:T(8,128)(2,1)}, bf16[864,1024]{1,0:T(8,128)(2,1)S(1)}, u32[]{:S(2)}, u32[]{:S(2)}) %collective-permute-start) | collective-permute-done | bytes 1769504 | tf_op jit(solution)/shard_map/ppermute | solution.py:943
  118.5 89.1 %conditional.5 = ((bf16[512,1024]{1,0:T(8,128)(2,1)}, bf16[864,1024]{1,0:T(8,128)(2,1)}, bf16[512,1024]{1,0:T(8,128)(2,1)}, f32[512,1024]{1,0:T(8,128)}, f32[102...) conditional(s32[]{:T(128)} %convert_element_type.4, ...), branch_computations={%region_2.3_spmd, %region_3.4_spmd} | conditional | bytes 33628576 | solution.py:939
  118.5 7.1 %product.5.refs_2_.refs_3_.refs_1_ = bf16[864,2048]{1,0:T(8,128)(2,1)} custom-call(bf16[864,1024]{1,0:T(8,128)(2,1)S(1)} %get-tuple-element.247.x_ref, bf16[1024,2048]{1,0:T(8,128)(2,1)} %get-tuple-element.445.w_ref.refs_2_), custom_call_target="tpu_custom_call" | custom-call | tf_op jit(solution)/shard_map/cond/branch_0_fun/product/pallas_call | solution.py:90
  125.6 15.7 %attend.5 = (bf16[512,1024]{1,0:T(8,128)(2,1)}, f32[512,1024]{1,0:T(8,128)}, bf16[16,768,256]{2,1,0:T(8,128)(2,1)}, bf16[16,96,256]{2,1,0:T(8,128)(2,1)}) custom-call(s32[1,2]{1,0:T(1,128)S(1)} %copy-done.32, bf16[512,1024]{1,0:T(8,128)(2,1)} %get-tuple-element.246.refs_1_.refs_0_, bf16[864,2048]{1,0:T(8,128)(2,1)} %product.5.refs_2_.refs_3_.refs_1_, ...), custom_call_target="tpu_custom_call" | custom-call | tf_op jit(solution)/shard_map/cond/branch_0_fun/attend/pallas_call | solution.py:217
  141.4 43.7 %dec_ffn.1 = (bf16[512,1024]{1,0:T(8,128)(2,1)}, f32[512,1024]{1,0:T(8,128)}, bf16[512,1024]{1,0:T(8,128)(2,1)}, f32[1024,512]{1,0:T(8,128)}, f32[1,512]{1,0:T(1...) custom-call(s32[1,2]{1,0:T(1,128)S(1)} %copy-done.31, f32[512,1024]{1,0:T(8,128)S(1)} %copy-done.7, ...), custom_call_target="tpu_custom_call" | custom-call | tf_op jit(solution)/shard_map/cond/branch_0_fun/dec_ffn/pallas_call | solution.py:626
  185.2 15.1 %attend_back.4 = (bf16[512,1024]{1,0:T(8,128)(2,1)}, bf16[864,1024]{1,0:T(8,128)(2,1)}, bf16[864,1024]{1,0:T(8,128)(2,1)}) custom-call(bf16[512,1024]{1,0:T(8,128)(2,1)} %get-tuple-element.246.refs_1_.refs_0_, bf16[864,2048]{1,0:T(8,128)(2,1)} %product.5.refs_2_.refs_3_.refs_1_, bf16[864,2048]{1,0:T(8,128)(2,1)} %product.5.refs_2_.refs_3_.refs_1_, ...), custom_call_target="tpu_custom_call" | custom-call | tf_op jit(solution)/shard_map/cond/branch_0_fun/attend_back/pallas_call | solution.py:310
  200.3 7.3 %back_product.4 = bf16[864,1024]{1,0:T(8,128)(2,1)} custom-call(bf16[864,1024]{1,0:T(8,128)(2,1)} %get-tuple-element.265.refs_0_, bf16[864,1024]{1,0:T(8,128)(2,1)} %get-tuple-element.266.refs_1_, bf16[1024,2048]{1,0:T(8,128)(2,1)S(1)} %copy-done.2), custom_call_target="tpu_custom_call" | custom-call | tf_op jit(solution)/shard_map/cond/branch_0_fun/back_product/pallas_call | solution.py:126
  207.6 2.6 collective-permute-start.1
  210.2 1.9 slice.56
  212.1 34.1 %collective-permute-done.1 = bf16[864,1024]{1,0:T(8,128)(2,1)} collective-permute-done((bf16[864,1024]{1,0:T(8,128)(2,1)}, bf16[864,1024]{1,0:T(8,128)(2,1)}, u32[]{:S(2)}, u32[]{:S(2)}) %collective-permute-start.1) | collective-permute-done | bytes 1769504 | tf_op jit(solution)/shard_map/ppermute | solution.py:947
  246.2 32.5 %conditional.6 = (f32[864,1024]{1,0:T(8,128)}, bf16[864,1024]{1,0:T(8,128)(2,1)S(1)}, f32[32,1024]{1,0:T(8,128)}, f32[32,1024]{1,0:T(8,128)}, f32[1024,512]{1,0:...) conditional(s32[]{:T(128)} %convert_element_type.4, ...), branch_computations={%region_4.5_spmd, %region_5.6_spmd} | conditional | bytes 15728776 | solution.py:939
  246.2 8.2 %dec_mid_back.2 = (f32[512,1024]{1,0:T(8,128)}, bf16[512,1024]{1,0:T(8,128)(2,1)}) custom-call(f32[512,1024]{1,0:T(8,128)} %get-tuple-element.278.dsecond_ref, bf16[512,1024]{1,0:T(8,128)(2,1)} %get-tuple-element.279.dcq_ref, bf16[1024,1024]{1,0:T(8,128)(2,1)} %get-tuple-element.280.wq_ref, f32[512,1024]{1,0:T(8,128)} %get-tuple-element.281.n_ref, ...), custom_call_target="tpu_custom_call" | custom-call | tf_op jit(solution)/shard_map/cond/branch_0_fun/dec_mid_back/pallas_call | solution.py:693
  254.4 14.5 %attend_back.5 = (bf16[512,1024]{1,0:T(8,128)(2,1)}, bf16[512,1024]{1,0:T(8,128)(2,1)}, bf16[512,1024]{1,0:T(8,128)(2,1)}, f32[32,1024]{1,0:T(8,128)}, f32[32,1024]{1,0:T(8,128)}) custom-call(bf16[512,3072]{1,0:T(8,128)(2,1)S(1)} %get-tuple-element.275.refs_0_.refs_1_.refs_2_, bf16[512,3072]{1,0:T(8,128)(2,1)S(1)} %get-tuple-element.275.refs_0_.refs_1_.refs_2_, ...), custom_call_target="tpu_custom_call" | custom-call | tf_op jit(solution)/shard_map/cond/branch_0_fun/attend_back/pallas_call | solution.py:310
  268.9 8.1 %back_product.5 = bf16[512,1024]{1,0:T(8,128)(2,1)} custom-call(bf16[512,1024]{1,0:T(8,128)(2,1)} %get-tuple-element.296.refs_0_, bf16[512,1024]{1,0:T(8,128)(2,1)} %get-tuple-element.297.refs_1_, bf16[512,1024]{1,0:T(8,128)(2,1)} %get-tuple-element.298.refs_2_, bf16[1024,3072]{1,0:T(8,128)(2,1)} %get-tuple-element.299.refs_3_, ...), custom_call_target="tpu_custom_call" | custom-call | tf_op jit(solution)/shard_map/cond/branch_0_fun/back_product/pallas_call | solution.py:126
  280.1 3.8 conditional.7
  284.9 1.4 collective-permute-start.3
  287.5 44.7 %collective-permute-start.2 = (bf16[1024,512]{1,0:T(8,128)(2,1)S(1)}, bf16[1024,512]{1,0:T(8,128)(2,1)S(1)}, u32[]{:S(2)}, u32[]{:S(2)}) collective-permute-start(bf16[1024,512]{1,0:T(8,128)(2,1)S(1)} %pad_maximum_fusion), channel_id=1, source_target_pairs={{16,0},{17,1},{18,2},{19,3},{20,4},{21,5},{22,6},{23,7},{24,8},{25... | collective-permute-start | bytes 3145736 | tf_op jit(solution)/shard_map/ppermute | solution.py:947
  332.2 76.9 %group_sum.1 = (f32[512,1024]{1,0:T(8,128)}, f32[1024,512]{1,0:T(8,128)}, f32[32,1024]{1,0:T(8,128)}, f32[32,1024]{1,0:T(8,128)}, f32[16,1024]{1,0:T(8,128)}) custom-call(f32[512,1024]{1,0:T(8,128)} %get-tuple-element.426.up_ref, f32[1024,512]{1,0:T(8,128)S(1)} %copy-done.12, f32[32,1024]{1,0:T(8,128)S(1)} %copy-done.22, f32[32,1024]{1,0:T(8,128)S(1)} %copy-done.23, ...), custom_call_target="tpu_custom_call" | custom-call | tf_op jit(solution)/shard_map/group_sum/pallas_call | solution.py:880
  410.4 1.4 slice.65
  (72 shorter events, 15.7 us)
Async XLA Ops:
  1.6 7.2 %copy-start.30 = (s32[1,2]{1,0:T(1,128)S(1)}, s32[1,2]{1,0:T(1,128)}, u32[]{:S(2)}) copy-start(s32[1,2]{1,0:T(1,128)} %get-tuple-element.199.refs_0_) | copy-start | bytes 28 | tf_op jit(solution)/shard_map/cond
  8.8 15.7 %copy-start = (bf16[1024,1024]{1,0:T(8,128)(2,1)S(1)}, bf16[1024,1024]{1,0:T(8,128)(2,1)}, u32[]{:S(2)}) copy-start(bf16[1024,1024]{1,0:T(8,128)(2,1)} %get-tuple-element.204.wo_ref) | copy-start | bytes 6291460 | tf_op jit(solution)/shard_map/cond
  8.8 15.7 %copy-start.8 = (bf16[1024,1024]{1,0:T(8,128)(2,1)S(1)}, bf16[1024,1024]{1,0:T(8,128)(2,1)}, u32[]{:S(2)}) copy-start(bf16[1024,1024]{1,0:T(8,128)(2,1)} %get-tuple-element.206.wq_ref) | copy-start | bytes 6291460 | tf_op jit(solution)/shard_map/cond
  8.8 15.7 %copy-start.19 = (f32[2,1024]{1,0:T(2,128)S(1)}, f32[2,1024]{1,0:T(2,128)}, u32[]{:S(2)}) copy-start(f32[2,1024]{1,0:T(2,128)} %get-tuple-element.205.gain_ref) | copy-start | bytes 24580 | tf_op jit(solution)/shard_map/cond
  31.0 87.5 %collective-permute-start = (bf16[864,1024]{1,0:T(8,128)(2,1)}, bf16[864,1024]{1,0:T(8,128)(2,1)S(1)}, u32[]{:S(2)}, u32[]{:S(2)}) collective-permute-start(bf16[864,1024]{1,0:T(8,128)(2,1)} %get-tuple-element.392), channel_id=1, source_target_pairs={{0,16},{1,17},{2,18},{3,19},{4,20},{5,21},{6,22},{7,23},{8,24},{9,... | collective-permute-start | bytes 5308424 | tf_op jit(solution)/shard_map/ppermute | solution.py:943
  125.5 15.8 %copy-start.4 = (bf16[1024,512]{1,0:T(8,128)(2,1)S(1)}, bf16[1024,512]{1,0:T(8,128)(2,1)}, u32[]{:S(2)}) copy-start(bf16[1024,512]{1,0:T(8,128)(2,1)} %get-tuple-element.256.down_ref) | copy-start | bytes 3145732 | tf_op jit(solution)/shard_map/cond
  125.5 15.8 %copy-start.6 = (bf16[512,1024]{1,0:T(8,128)(2,1)S(1)}, bf16[512,1024]{1,0:T(8,128)(2,1)}, u32[]{:S(2)}) copy-start(bf16[512,1024]{1,0:T(8,128)(2,1)} %get-tuple-element.258.up_ref) | copy-start | bytes 3145732 | tf_op jit(solution)/shard_map/cond
  125.5 15.8 %copy-start.7 = (f32[512,1024]{1,0:T(8,128)S(1)}, f32[512,1024]{1,0:T(8,128)}, u32[]{:S(2)}) copy-start(f32[512,1024]{1,0:T(8,128)} %get-tuple-element.244.n_ref) | copy-start | bytes 6291460 | tf_op jit(solution)/shard_map/cond
  125.6 15.8 %copy-start.21 = (f32[2,1024]{1,0:T(2,128)S(1)}, f32[2,1024]{1,0:T(2,128)}, u32[]{:S(2)}) copy-start(f32[2,1024]{1,0:T(2,128)} %get-tuple-element.253.gain_ref) | copy-start | bytes 24580 | tf_op jit(solution)/shard_map/cond
  125.6 15.8 %copy-start.25 = (f32[1,1024]{1,0:T(1,128)S(1)}, f32[1,1024]{1,0:T(1,128)}, u32[]{:S(2)}) copy-start(f32[1,1024]{1,0:T(1,128)} %get-tuple-element.259.upb_ref) | copy-start | bytes 12292 | tf_op jit(solution)/shard_map/cond
  125.6 15.8 %copy-start.27 = (f32[1,512]{1,0:T(1,128)S(1)}, f32[1,512]{1,0:T(1,128)}, u32[]{:S(2)}) copy-start(f32[1,512]{1,0:T(1,128)} %get-tuple-element.257.downb_ref) | copy-start | bytes 6148 | tf_op jit(solution)/shard_map/cond
  125.6 15.8 %copy-start.28 = (f32[1024]{0:T(1024)S(1)}, f32[1024]{0:T(1024)}, u32[]{:S(2)}) copy-start(f32[1024]{0:T(1024)} %get-tuple-element.446) | copy-start | bytes 12292 | tf_op jit(solution)/shard_map/cond
  125.6 15.8 %copy-start.31 = (s32[1,2]{1,0:T(1,128)S(1)}, s32[1,2]{1,0:T(1,128)}, u32[]{:S(2)}) copy-start(s32[1,2]{1,0:T(1,128)} %get-tuple-element.243.len_ref) | copy-start | bytes 28 | tf_op jit(solution)/shard_map/cond
  185.1 15.1 %copy-start.2 = (bf16[1024,2048]{1,0:T(8,128)(2,1)S(1)}, bf16[1024,2048]{1,0:T(8,128)(2,1)}, u32[]{:S(2)}) copy-start(bf16[1024,2048]{1,0:T(8,128)(2,1)} %get-tuple-element.445.w_ref.refs_2_) | copy-start | bytes 12582916 | tf_op jit(solution)/shard_map/cond
  207.6 38.6 %collective-permute-start.1 = (bf16[864,1024]{1,0:T(8,128)(2,1)}, bf16[864,1024]{1,0:T(8,128)(2,1)}, u32[]{:S(2)}, u32[]{:S(2)}) collective-permute-start(bf16[864,1024]{1,0:T(8,128)(2,1)} %get-tuple-element.408), channel_id=1, source_target_pairs={{16,0},{17,1},{18,2},{19,3},{20,4},{21,5},{22,6},{23,7},{24,8},{25... | collective-permute-start | bytes 5308424 | tf_op jit(solution)/shard_map/ppermute | solution.py:947
  246.2 8.2 %copy-start.9 = (bf16[512,1024]{1,0:T(8,128)(2,1)S(1)}, bf16[512,1024]{1,0:T(8,128)(2,1)}, u32[]{:S(2)}) copy-start(bf16[512,1024]{1,0:T(8,128)(2,1)} %get-tuple-element.276.refs_3_) | copy-start | bytes 3145732 | tf_op jit(solution)/shard_map/cond
  246.2 8.2 %copy-start.11 = (bf16[16,288,256]{2,1,0:T(8,128)(2,1)S(1)}, bf16[16,288,256]{2,1,0:T(8,128)(2,1)}, u32[]{:S(2)}) copy-start(bf16[16,288,256]{2,1,0:T(8,128)(2,1)} %get-tuple-element.288.refs_8_) | copy-start | bytes 7077892 | tf_op jit(solution)/shard_map/cond
  283.9 48.3 %copy-start.12 = (f32[1024,512]{1,0:T(8,128)S(1)}, f32[1024,512]{1,0:T(8,128)}, u32[]{:S(2)}) copy-start(f32[1024,512]{1,0:T(8,128)} %get-tuple-element.427.down_ref) | copy-start | bytes 6291460
  283.9 48.3 %copy-start.22 = (f32[32,1024]{1,0:T(8,128)S(1)}, f32[32,1024]{1,0:T(8,128)}, u32[]{:S(2)}) copy-start(f32[32,1024]{1,0:T(8,128)} %get-tuple-element.428.pk_ref) | copy-start | bytes 393220
  283.9 48.3 %copy-start.23 = (f32[32,1024]{1,0:T(8,128)S(1)}, f32[32,1024]{1,0:T(8,128)}, u32[]{:S(2)}) copy-start(f32[32,1024]{1,0:T(8,128)} %get-tuple-element.429.pv_ref) | copy-start | bytes 393220
  283.9 48.3 %copy-start.29 = (f32[1,1024]{1,0:T(1,128)S(1)}, f32[1,1024]{1,0:T(1,128)}, u32[]{:S(2)}) copy-start(f32[1,1024]{1,0:T(1,128)} %get-tuple-element.430.upb_ref) | copy-start | bytes 12292
  283.9 48.3 %copy-start.33 = (f32[1,512]{1,0:T(1,128)S(1)}, f32[1,512]{1,0:T(1,128)}, u32[]{:S(2)}) copy-start(f32[1,512]{1,0:T(1,128)} %get-tuple-element.431.downb_ref) | copy-start | bytes 6148
  284.9 128.8 %collective-permute-start.3 = (bf16[864,512]{1,0:T(8,128)(2,1)}, bf16[864,512]{1,0:T(8,128)(2,1)S(1)}, u32[]{:S(2)}, u32[]{:S(2)}) collective-permute-start(bf16[864,512]{1,0:T(8,128)(2,1)} %slice.60), channel_id=1, source_target_pairs={{0,16},{1,17},{2,18},{3,19},{4,20},{5,21},{6,22},{7,23},{8,24},{9,... | collective-permute-start | bytes 2654216 | tf_op jit(solution)/shard_map/ppermute | solution.py:943
  287.5 127.3 %collective-permute-start.2 = (bf16[1024,512]{1,0:T(8,128)(2,1)S(1)}, bf16[1024,512]{1,0:T(8,128)(2,1)S(1)}, u32[]{:S(2)}, u32[]{:S(2)}) collective-permute-start(bf16[1024,512]{1,0:T(8,128)(2,1)S(1)} %pad_maximum_fusion), channel_id=1, source_target_pairs={{16,0},{17,1},{18,2},{19,3},{20,4},{21,5},{22,6},{23,7},{24,8},{25... | collective-permute-start | bytes 3145736 | tf_op jit(solution)/shard_map/ppermute | solution.py:947
  (7 other events, 23.4 us)

commit v3 on v1

--- a/solution.py
+++ b/solution.py
@@ -230,16 +230,9 @@
     )(*args)
 
 
-def attend_back_kernel(*refs, segs, prefix):
-    q_ref, k_ref, v_ref, o_ref, inv_ref, g_ref = refs[:6]
-    at = 6
-    pk_ref = pv_ref = None
-    if prefix:
-        pk_ref, pv_ref = refs[6:8]
-        at = 8
-    p_refs = refs[at : at + len(segs)]
-    outs = refs[at + len(segs) :]
-    dq_ref, dk_ref, dv_ref = outs[:3]
+def attend_back_pair(
+    q_ref, k_ref, v_ref, o_ref, inv_ref, g_ref, pk_ref, pv_ref, p_refs, dq_ref, dk_ref, dv_ref, segs
+):
     prefix_totals = [None, None]
     scale = HD**-0.5
     for seg, (q0, nq, k0, nk) in enumerate(segs):
@@ -271,13 +264,23 @@
         dq_ref[q0 : q0 + nq] = (dq * scale).astype(BF)
         dk_ref[k0 : k0 + nk] = dk[:nk].astype(BF)
         dv_ref[k0 : k0 + nk] = dv[:nk].astype(BF)
-        if prefix:
+        if pk_ref is not None:
             for i, grad in enumerate((dk, dv)):
                 part = grad[nk:]
                 prefix_totals[i] = part if seg == 0 else prefix_totals[i] + part
+    return prefix_totals
+
+
+def attend_back_kernel(*refs, segs, prefix):
+    at = 8 if prefix else 6
+    pk_ref, pv_ref = refs[6:8] if prefix else (None, None)
+    outs = refs[at + len(segs) :]
+    totals = attend_back_pair(
+        *refs[:6], pk_ref, pv_ref, refs[at : at + len(segs)], *outs[:3], segs
+    )
     if prefix:
-        outs[3][...] = prefix_totals[0]
-        outs[4][...] = prefix_totals[1]
+        outs[3][...] = totals[0]
+        outs[4][...] = totals[1]
 
 
 def attend_back(q, k, v, prefixes, attended, inverse, grad, weights, segs):
@@ -721,14 +724,6 @@
     return dfirst, datt, adapter
 
 
-def encoder_back_self(saved, dfirst, datt, w):
-    qkv, att, inv, weights = saved[:4]
-    dq, dk, dv, *dprefix = attend_back(
-        (qkv, 0), (qkv, 8), (qkv, 16), w["prefix"], att, inv, datt, weights, enc_segs
-    )
-    return back_product([dq, dk, dv], w["qkv"], dfirst), dprefix
-
-
 def decoder_self(t, lengths, w, cross):
     qkv = product(t, w["qkv"])
     att, inv, *weights = attend(
@@ -759,6 +754,290 @@
         (qkv, 0), (qkv, 8), (qkv, 16), w["prefix"], att, inv, datt, weights, dec_segs
     )
     return back_product([dq, dk, dv], w["qkv"], dfirst), dprefix
+
+
+def small_shape(devices):
+    return 8, 8 * (2 * chunk) // devices
+
+
+def finish_kernel(
+    q_ref, k_ref, v_ref, o_ref, inv_ref, g_ref, pk_ref, pv_ref, pl_ref, ps_ref,
+    dfirst_ref, wqkv_ref, up_ref, down_ref, upb_ref, downb_ref, dpk_ref, dpv_ref,
+    y_ref, dt_ref,
+    source_ref, low_ref, o_up_ref, o_down_ref, o_small_ref,
+    dq, dk, dv, small, mine, theirs, half_sum, landed, total, result,
+    small_landed, small_total, small_result, dx_low, dx_high, dx_landed, lows, lows_landed,
+    pair_sems, spread_sems, gather_sems, back_sems, small_sems, share_sems, cross_sems,
+    *, devices,
+):
+    step = pl.program_id(0)
+    pairs = 8
+    is_encoder = lax.axis_index("section") == 0
+    section = lax.axis_index("section")
+    chips = devices // 2
+    rows = 2 * chunk
+    half, part = rows // 2, rows // devices
+    place = lax.axis_index("dp")
+    core, chip = lax.rem(place, 2), place // 2
+    partner = place + 1 - 2 * core
+    small_rows, small_cols = small_shape(devices)
+    tile = 256
+    width = 2 * chunk
+    scale = 1.0 / devices
+
+    def peer(distance):
+        return lax.rem(chip + distance, chips) * 2 + core
+
+    def remote(source, target, send_sem, recv_sem, other):
+        return pltpu.make_async_remote_copy(
+            src_ref=source, dst_ref=target, send_sem=send_sem, recv_sem=recv_sem,
+            device_id=other, device_id_type=pl.DeviceIdType.MESH,
+        )
+
+    def in_group(other):
+        return {"dp": other}
+
+    across = {"section": 1 - section}
+    kept = pl.multiple_of(core * half, 16)
+    given = pl.multiple_of((1 - core) * half, 16)
+    here = pl.multiple_of(kept + chip * part, 16)
+
+    def swap():
+        return remote(
+            mine.at[pl.ds(given, half)], theirs, pair_sems.at[0], pair_sems.at[1],
+            in_group(partner),
+        )
+
+    def spread(s):
+        at = pl.multiple_of(lax.rem(chip + s, chips) * part, 16)
+        return remote(
+            half_sum.at[pl.ds(at, part)], landed.at[s - 1],
+            spread_sems.at[0, s - 1], spread_sems.at[1, s - 1], in_group(peer(s)),
+        )
+
+    def gather(s):
+        return remote(
+            total, result.at[pl.ds(here, part)],
+            gather_sems.at[0, s - 1], gather_sems.at[1, s - 1], in_group(peer(s)),
+        )
+
+    def back(s):
+        source = lax.rem(chip + chips - s, chips)
+        there = pl.ds(pl.multiple_of(kept + source * part, 16), part)
+        return remote(
+            total if s == 0 else result.at[there], result.at[there],
+            back_sems.at[0, s], back_sems.at[1, s], in_group(partner),
+        )
+
+    def piece(index):
+        row = pl.multiple_of(lax.rem(index, 8) * small_rows, 8)
+        col = pl.multiple_of((index // 8) * small_cols, LANES)
+        return pl.ds(row, small_rows), pl.ds(col, small_cols)
+
+    def small_out(s):
+        return remote(
+            small.at[piece(lax.rem(place + s, devices))], small_landed.at[s - 1],
+            small_sems.at[0, s - 1], small_sems.at[1, s - 1],
+            in_group(lax.rem(place + s, devices)),
+        )
+
+    def small_share(s):
+        return remote(
+            small_total, small_result.at[piece(place)],
+            share_sems.at[0, s - 1], share_sems.at[1, s - 1],
+            in_group(lax.rem(place + s, devices)),
+        )
+
+    def send_low():
+        return remote(lows, lows_landed, cross_sems.at[0, 0], cross_sems.at[1, 0], across)
+
+    def send_high(i):
+        return remote(
+            dx_high.at[i], dx_landed.at[i], cross_sems.at[0, 1 + i], cross_sems.at[1, 1 + i], across
+        )
+
+    @pl.when(step == 0)
+    def _():
+        barrier = pltpu.get_barrier_semaphore()
+        others = [in_group(lax.rem(place + s, devices)) for s in range(1, devices)] + [across]
+        for other in others:
+            pl.semaphore_signal(
+                barrier, inc=1, device_id=other, device_id_type=pl.DeviceIdType.MESH
+            )
+        mine[0:chunk] = (up_ref[...] * scale).astype(BF)
+        mine[chunk:width, 0:chunk] = (down_ref[0:chunk] * scale).astype(BF)
+        mine[chunk:width, chunk:width] = (down_ref[chunk:width] * scale).astype(BF)
+        pl.semaphore_wait(barrier, devices)
+        swap().start()
+
+        @pl.when(jnp.logical_not(is_encoder))
+        def _():
+            lows[0] = y_ref[...]
+            lows[1] = dt_ref[...]
+            send_low().start()
+            small[0:PRE_PAD] = dpk_ref[...] * scale
+            small[PRE_PAD : 2 * PRE_PAD] = dpv_ref[...] * scale
+
+    @pl.when(is_encoder & (step < pairs))
+    def _():
+        at = pl.multiple_of(step * LANES, LANES)
+        lanes = pl.ds(at, LANES)
+        prefix_totals = attend_back_pair(
+            q_ref, k_ref, v_ref, o_ref, inv_ref, g_ref, pk_ref, pv_ref, (pl_ref, ps_ref),
+            dq.at[:, lanes], dk.at[:, lanes], dv.at[:, lanes], enc_segs,
+        )
+        small[0:PRE_PAD, lanes] = prefix_totals[0] * scale
+        small[PRE_PAD : 2 * PRE_PAD, lanes] = prefix_totals[1] * scale
+
+    @pl.when(step == 1)
+    def _():
+        swap().wait()
+        half_sum[...] = (
+            mine[pl.ds(kept, half)].astype(F32) + theirs[...].astype(F32)
+        ).astype(BF)
+        for s in range(1, chips):
+            spread(s).start()
+
+    @pl.when(step == pairs - 1)
+    def _():
+        down_row = jnp.concatenate([downb_ref[...], jnp.zeros_like(downb_ref)], 1)
+        small[PRE : PRE + 1] = upb_ref[...] * scale
+        small[PRE + 1 : PRE + 2] = down_row * scale
+        for s in range(1, devices):
+            small_out(s).start()
+        summed = half_sum[pl.ds(pl.multiple_of(chip * part, 16), part)].astype(F32)
+        for s in range(1, chips):
+            spread(s).wait()
+            summed = summed + landed[s - 1].astype(F32)
+        total[...] = summed.astype(BF)
+        result[pl.ds(here, part)] = total[...]
+        for s in range(1, chips):
+            gather(s).start()
+        back(0).start()
+
+    for i in range(4):
+
+        @pl.when(is_encoder & (step == pairs + i))
+        def _(i=i):
+            acc = dfirst_ref[...]
+            for n, grad in enumerate((dq, dk, dv)):
+                acc = acc + nt(grad[...], wqkv_ref[:, n * width : (n + 1) * width])
+            if i < 2:
+                dx_high[i] = acc.astype(BF)
+                send_high(i).start()
+            else:
+                dx_low[:, (i - 2) * tile : (i - 1) * tile] = acc.astype(BF)
+
+    @pl.when(step == pairs + 1)
+    def _():
+        own_rows, own_cols = piece(place)
+        summed = small[own_rows, own_cols]
+        for s in range(1, devices):
+            small_out(s).wait()
+            summed = summed + small_landed[s - 1]
+        small_total[...] = summed
+        small_result[own_rows, own_cols] = summed
+        for s in range(1, devices):
+            small_share(s).start()
+
+    @pl.when(step == pairs + 3)
+    def _():
+        for s in range(1, chips):
+            gather(s).wait()
+            back(s).start()
+        for s in range(1, devices):
+            small_share(s).wait()
+        for s in range(chips):
+            back(s).wait()
+        o_small_ref[...] = small_result[...]
+        o_up_ref[...] = result[0:chunk].astype(F32)
+        o_down_ref[0:chunk] = result[chunk:width, 0:chunk].astype(F32)
+        o_down_ref[chunk:width] = result[chunk:width, chunk:width].astype(F32)
+
+        @pl.when(is_encoder)
+        def _():
+            send_low().wait_recv()
+            low_ref[...] = lows_landed[...]
+            source_ref[...] = dx_low[...]
+            for i in range(2):
+                send_high(i).wait_send()
+
+        @pl.when(jnp.logical_not(is_encoder))
+        def _():
+            send_low().wait_send()
+            for i in range(2):
+                send_high(i).wait_recv()
+                source_ref[:, i * tile : (i + 1) * tile] = dx_landed[i]
+
+
+def finish(saved, datt, dfirst, w, adapter, dec_prefix, y_low, dt_low):
+    qkv, att, inv, weights = saved[:4]
+    ddown, ddownb, dup, dupb = adapter
+    devices = lax.axis_size("dp")
+    chips = devices // 2
+    rows, width = dfirst.shape
+    targets = y_low.shape[0]
+    pairs, tile = 8, 256
+    half = width // 2
+    part = width // devices
+    small_rows, small_cols = small_shape(devices)
+
+    def pair(offset):
+        return pl.BlockSpec((rows, LANES), lambda i: (0, jnp.minimum(i, pairs - 1) + offset))
+
+    def at(i):
+        return jnp.where(i < pairs + 2, 2 + jnp.maximum(i - pairs, 0), i - pairs - 2)
+
+    def once(shape):
+        return pl.BlockSpec(shape, lambda i: (0,) * len(shape), pipeline_mode=pl.Buffered(1))
+
+    prefix_pair = pl.BlockSpec((PRE_PAD, LANES), lambda i: (0, jnp.minimum(i, pairs - 1)))
+    vmem = pltpu.VMEM
+    dma = pltpu.SemaphoreType.DMA
+    return pl.pallas_call(
+        functools.partial(finish_kernel, devices=devices),
+        grid=(pairs + 4,),
+        in_specs=[pair(0), pair(8), pair(16), pair(0), pair(0), pair(0), prefix_pair, prefix_pair]
+        + [
+            pl.BlockSpec((2,) + p.shape[1:], lambda i: (jnp.minimum(i, pairs - 1), 0, 0))
+            for p in weights
+        ]
+        + [
+            pl.BlockSpec((rows, tile), lambda i: (0, at(i))),
+            pl.BlockSpec((tile, 3 * width), lambda i: (at(i), 0)),
+        ]
+        + [once(a.shape) for a in (dup, ddown, dupb, ddownb, *dec_prefix, y_low, dt_low)],
+        out_specs=[
+            once((rows, half)), once((2, targets, half)), once(dup.shape), once(ddown.shape),
+            once((2 * PRE_PAD, width)),
+        ],
+        out_shape=[
+            jax.ShapeDtypeStruct((rows, half), BF),
+            jax.ShapeDtypeStruct((2, targets, half), BF),
+            jax.ShapeDtypeStruct(dup.shape, F32),
+            jax.ShapeDtypeStruct(ddown.shape, F32),
+            jax.ShapeDtypeStruct((2 * PRE_PAD, width), F32),
+        ],
+        scratch_shapes=[
+            vmem((rows, width), BF), vmem((rows, width), BF), vmem((rows, width), BF),
+            vmem((2 * PRE_PAD, width), F32),
+            vmem((width, width), BF), vmem((half, width), BF), vmem((half, width), BF),
+            vmem((chips - 1, part, width), BF), vmem((part, width), BF), vmem((width, width), BF),
+            vmem((devices - 1, small_rows, small_cols), F32), vmem((small_rows, small_cols), F32),
+            vmem((2 * PRE_PAD, width), F32),
+            vmem((rows, half), BF), vmem((2, rows, tile), BF), vmem((2, rows, tile), BF),
+            vmem((2, targets, half), BF), vmem((2, targets, half), BF),
+            dma((2,)), dma((2, chips - 1)), dma((2, chips - 1)), dma((2, chips)),
+            dma((2, devices - 1)), dma((2, devices - 1)), dma((2, 3)),
+        ],
+        compiler_params=pltpu.CompilerParams(
+            vmem_limit_bytes=vmem_bytes, collective_id=0, has_side_effects=True
+        ),
+        name="finish",
+    )(
+        qkv, qkv, qkv, att, inv, datt, *w["prefix"], *weights,
+        dfirst, w["qkv"], dup, ddown, dupb, ddownb, *dec_prefix, y_low, dt_low,
+    )
 
 
 def blank_kernel(*refs):
@@ -775,8 +1054,8 @@
 
 
 def on_section(is_encoder, encoder_work, decoder_work, *operands):
-    enc_shapes = jax.eval_shape(encoder_work, *operands)
-    dec_shapes = jax.eval_shape(decoder_work, *operands)
+    enc_shapes, _ = jax.eval_shape(encoder_work, *operands)
+    dec_shapes, _ = jax.eval_shape(decoder_work, *operands)
 
     def blank_like(shapes):
         leaves, tree = jax.tree.flatten(shapes)
@@ -784,12 +1063,15 @@
             return shapes
         return jax.tree.unflatten(tree, blanks(leaves))
 
-    return lax.cond(
-        is_encoder,
-        lambda *a: (encoder_work(*a), blank_like(dec_shapes)),
-        lambda *a: (blank_like(enc_shapes), decoder_work(*a)),
-        *operands,
-    )
+    def encoder_branch(*a):
+        own, shared = encoder_work(*a)
+        return own, blank_like(dec_shapes), shared
+
+    def decoder_branch(*a):
+        own, shared = decoder_work(*a)
+        return blank_like(enc_shapes), own, shared
+
+    return lax.cond(is_encoder, encoder_branch, decoder_branch, *operands)
 
 
 def to_decoder(block):
@@ -816,54 +1098,43 @@
     )
     cross = dict(query=cross_query, pairs=cross_pairs, out=cross_out, gain=cross_gain[None])
     half = sources.shape[1] // 2
-    replicas = lax.axis_size("dp")
-
-    (mem, saved), (cq, kept) = on_section(
+
+    (mem, saved), (cq, kept), _ = on_section(
         is_encoder,
-        lambda: encoder_forward(sources, source_lengths, w),
-        lambda: decoder_self(targets, target_lengths, w, cross),
+        lambda: (encoder_forward(sources, source_lengths, w), ()),
+        lambda: (decoder_self(targets, target_lengths, w, cross), ()),
     )
     mem_here = to_decoder(mem)
-    _, (y, dmem, dcq, dsecond, dec_adapter) = on_section(
+    _, (y, dmem, dcq, dsecond, dec_adapter), _ = on_section(
         is_encoder,
-        lambda *a: (),
-        lambda *a: decoder_cross(*a, cotangent, source_lengths, target_lengths, w, cross),
+        lambda *a: ((), ()),
+        lambda *a: (decoder_cross(*a, cotangent, source_lengths, target_lengths, w, cross), ()),
         kept, mem_here, cq,
     )
     dmem_here = to_encoder(dmem)
-    y_low = to_encoder(y[:, :half])
-    (dfirst, datt, enc_adapter), (dt, dec_prefix) = on_section(
-        is_encoder,
-        lambda *a: encoder_back_ffn(a[0], a[1], w),
-        lambda *a: decoder_self_back(a[2], a[3], a[4], w, cross),
-        saved, dmem_here, kept, dsecond, dcq,
-    )
-    dt_low = to_encoder(dt[:, :half])
-    adapter = [
-        jnp.where(is_encoder, a, b) / replicas for a, b in zip(enc_adapter, dec_adapter)
-    ]
-    down, down_bias, up, up_bias = lax.psum(adapter, "dp")
-    (dx, enc_prefix), _ = on_section(
-        is_encoder,
-        lambda *a: encoder_back_self(*a, w),
-        lambda *a: (),
-        saved, dfirst, datt,
-    )
-    dx_high = to_decoder(dx[:, half:])
-    prefix_grad = jnp.stack(
-        [jnp.where(is_encoder, a, b)[:PRE] for a, b in zip(enc_prefix, dec_prefix)]
-    )
-    prefix_grad, down, up = lax.optimization_barrier((prefix_grad, down, up))
-    prefix_grad = lax.psum(prefix_grad / replicas, "dp")
+
+    def encoder_c1(saved, dmem, kept, dsecond, dcq, dec_adapter):
+        dfirst, datt, adapter = encoder_back_ffn(saved, dmem, w)
+        return (dfirst, datt), adapter
+
+    def decoder_c1(saved, dmem, kept, dsecond, dcq, dec_adapter):
+        return decoder_self_back(kept, dsecond, dcq, w, cross), dec_adapter
+
+    (dfirst, datt), (dt, dec_prefix), adapter = on_section(
+        is_encoder, encoder_c1, decoder_c1, saved, dmem_here, kept, dsecond, dcq, dec_adapter
+    )
+    source_grad, low, up, down, small = finish(
+        saved, datt, dfirst, w, adapter, dec_prefix, y[:, :half], dt[:, :half]
+    )
     return (
-        jnp.where(is_encoder, y_low, y[:, half:]),
-        jnp.where(is_encoder, dx[:, :half], dx_high),
-        jnp.where(is_encoder, dt_low, dt[:, half:]),
-        prefix_grad[None],
+        jnp.where(is_encoder, low[0], y[:, half:]),
+        source_grad,
+        jnp.where(is_encoder, low[1], dt[:, half:]),
+        jnp.stack([small[:PRE], small[PRE_PAD : PRE_PAD + PRE]])[None],
         down[None],
-        down_bias,
+        small[PRE + 1 : PRE + 2, : down.shape[1]],
         up[None],
-        up_bias,
+        small[PRE : PRE + 1],
     )
 
 

time: 522 us -> 381 us (0.73)
  waiting for transfers between devices: 273 us -> 153 us
  Pallas kernels: 149 us -> 184 us
  blocking collectives: 32.5 us -> 0 us
  between operations: 14.4 us -> 0.94 us
  other arithmetic: 11.4 us -> 1.17 us
    psum x2 -> x0, waiting for transfers between devices: 104 us -> none  [the longest x1 89.9 us: per_device(): prefix_grad = lax.psum(prefix_grad / replicas, 'dp')]
    pallas_call x2 -> x1, Pallas kernels: 40 us -> 76 us  [finish(): pl.pallas_call(functools.partial(finish_kernel, devices=devices), grid=(p...]
    psum x1 -> x0, blocking collectives: 32.5 us -> none  [per_device(): down, down_bias, up, up_bias = lax.psum(adapter, 'dp')]
    ppermute x3 -> x1, waiting for transfers between devices: 144 us -> 128 us  [to_encoder(): return lax.ppermute(block, 'section', [(1, 0)])]
    div x4 -> x0, other arithmetic: 5.51 us -> none  [per_device(): jnp.where(is_encoder, a, b) / replicas]
    ppermute x2 -> x1, starting transfers between devices: 17.4 us -> 15.4 us  [to_decoder(): return lax.ppermute(block, 'section', [(0, 1)])]
    ppermute x2 -> x1, waiting for transfers between devices: 25.1 us -> 24.9 us  [to_decoder(): return lax.ppermute(block, 'section', [(0, 1)])]
  transfers between devices with their start and end apart: 7 -> 2, of which waited for: 5 -> 2; matrix products, arithmetic and copies ran while one was open for 2% -> 1% of each run, Pallas kernels for 8% -> 0%
where the time goes in v3:
time: 381 us; the launch traced here: 376 us
  Pallas kernels  184 us (48%)
  waiting for transfers between devices  153 us (40%)
  local copies, waits for them, and re-layouts  18.4 us (5%)
  starting transfers between devices  16.7 us (4%)
    ppermute x1, waiting for transfers between devices, to_encoder(): return lax.ppermute(block, 'section', [(1, 0)])  128 us
    pallas_call x1, Pallas kernels, finish(): pl.pallas_call(functools.partial(finish_kernel, devices=devices), grid=(p...  76 us
    pallas_call x1, Pallas kernels, enc_ffn(): pl.pallas_call(enc_ffn_kernel, grid=(steps + 2,), in_specs=[whole((rows,...  36.9 us
    pallas_call x1, Pallas kernels, enc_ffn_back(): pl.pallas_call(enc_ffn_back_kernel, grid=(steps + 1,), in_specs=[whole((r...  34.9 us
    pallas_call x1, Pallas kernels, attend(): pl.pallas_call(functools.partial(attend_kernel, segs=segs, prefix=prefix,...  26.2 us
    ppermute x1, waiting for transfers between devices, to_decoder(): return lax.ppermute(block, 'section', [(0, 1)])  24.9 us
    ppermute x1, starting transfers between devices, to_decoder(): return lax.ppermute(block, 'section', [(0, 1)])  15.4 us
    pallas_call x1, Pallas kernels, product(): pl.pallas_call(product_kernel, grid=(width // tile,), in_specs=[whole((ro...  10.4 us
  transfers between devices with their start and end apart: 2, of which 2 were waited for; matrix products, arithmetic and copies ran while one was open for 1% of the time, Pallas kernels for 0%

profile of v3, /device:TPU:0, one launch (start us, length us, event | category | flops | bytes accessed | tf_op | source)
XLA Modules:
  0.0 376.0 jit_solution(5003323875166343190)
XLA Ops:
  0.6 0.9 copy.36
  1.6 76.8 %conditional.3 = (bf16[864,1024]{1,0:T(8,128)(2,1)}, bf16[864,3072]{1,0:T(8,128)(2,1)}, bf16[864,1024]{1,0:T(8,128)(2,1)}, f32[864,1024]{1,0:T(8,128)}, bf16[16,...) conditional(s32[]{:T(128)} %convert_element_type.4, ...), branch_computations={%region_0.1_spmd, %region_1.2_spmd} | conditional | bytes 20373824 | solution.py:1074
  2.0 10.4 %product.4.refs_1_.refs_2_.refs_3_ = bf16[864,3072]{1,0:T(8,128)(2,1)} custom-call(bf16[864,1024]{1,0:T(8,128)(2,1)} %get-tuple-element.393.x_ref, bf16[1024,3072]{1,0:T(8,128)(2,1)} %get-tuple-element.191.w_ref), custom_call_target="tpu_custom_call" | custom-call | tf_op jit(solution)/shard_map/cond/branch_1_fun/product/pallas_call | solution.py:90
  12.5 26.2 %attend.4 = (bf16[864,1024]{1,0:T(8,128)(2,1)}, f32[864,1024]{1,0:T(8,128)}, bf16[16,800,768]{2,1,0:T(8,128)(2,1)}, bf16[16,128,96]{2,1,0:T(8,128)(2,1)}) custom-call(s32[1,2]{1,0:T(1,128)} %get-tuple-element.190.refs_0_, bf16[864,3072]{1,0:T(8,128)(2,1)} %product.4.refs_1_.refs_2_.refs_3_, bf16[864,3072]{1,0:T(8,128)(2,1)} %product.4.refs_1_.refs_2_.refs_3_, ...), custom_call_target="tpu_custom_call" | custom-call | tf_op jit(solution)/shard_map/cond/branch_1_fun/attend/pallas_call | solution.py:217
  38.7 36.9 %enc_ffn.1 = (bf16[864,1024]{1,0:T(8,128)(2,1)}, bf16[864,4608]{1,0:T(8,128)(2,1)}, bf16[864,512]{1,0:T(8,128)(2,1)}, bf16[864,1024]{1,0:T(8,128)(2,1)}, f32[864,128]{1,0:T(8,128)}) custom-call(bf16[864,1024]{1,0:T(8,128)(2,1)} %get-tuple-element.393.x_ref, bf16[864,1024]{1,0:T(8,128)(2,1)} %get-tuple-element.441.att_ref, bf16[1024,1024]{1,0:T(8,128)(2,1)S(1)} %copy-done.1, ...), custom_call_target="tpu_custom_call" | custom-call | tf_op jit(solution)/shard_map/cond/branch_1_fun/enc_ffn/pallas_call | solution.py:379
  75.6 2.9 copy.62
  78.5 15.4 %collective-permute-start = (bf16[864,1024]{1,0:T(8,128)(2,1)}, bf16[864,1024]{1,0:T(8,128)(2,1)S(1)}, u32[]{:S(2)}, u32[]{:S(2)}) collective-permute-start(bf16[864,1024]{1,0:T(8,128)(2,1)} %get-tuple-element.351), channel_id=1, source_target_pairs={{0,16},{1,17},{2,18},{3,19},{4,20},{5,21},{6,22},{7,23},{8,24},{9,... | collective-permute-start | bytes 5308424 | tf_op jit(solution)/shard_map/ppermute | solution.py:1078
  93.9 24.9 %collective-permute-done = bf16[864,1024]{1,0:T(8,128)(2,1)S(1)} collective-permute-done((bf16[864,1024]{1,0:T(8,128)(2,1)}, bf16[864,1024]{1,0:T(8,128)(2,1)S(1)}, u32[]{:S(2)}, u32[]{:S(2)}) %collective-permute-start) | collective-permute-done | bytes 1769504 | tf_op jit(solution)/shard_map/ppermute | solution.py:1078
  118.8 1.3 collective-permute-start.1
  120.1 1.9 slice.46.y_ref
  122.0 128.5 %collective-permute-done.1 = bf16[864,1024]{1,0:T(8,128)(2,1)S(1)} collective-permute-done((bf16[864,1024]{1,0:T(8,128)(2,1)}, bf16[864,1024]{1,0:T(8,128)(2,1)S(1)}, u32[]{:S(2)}, u32[]{:S(2)}) %collective-permute-start.1) | collective-permute-done | bytes 1769504 | tf_op jit(solution)/shard_map/ppermute | solution.py:1082
  250.4 38.9 %conditional.5 = (f32[864,1024]{1,0:T(8,128)S(1)}, bf16[864,1024]{1,0:T(8,128)(2,1)}, f32[32,1024]{1,0:T(8,128)}, f32[32,1024]{1,0:T(8,128)}, f32[1024,512]{1,0:...) conditional(s32[]{:T(128)} %convert_element_type.4, ...), branch_computations={%region_4.5_spmd, %region_5.6_spmd} | conditional | bytes 15728776 | solution.py:1074
  250.8 1.2 copy-done.14
  252.1 34.9 %enc_ffn_back.2 = (f32[864,1024]{1,0:T(8,128)S(1)}, bf16[864,1024]{1,0:T(8,128)(2,1)}, f32[1024,512]{1,0:T(8,128)}, f32[1,512]{1,0:T(1,128)}, f32[512,1024]{1,0:T(8,128)}, /*index=5*/f32[1,1024]{1,0:T(1,128)}) custom-call(bf16[864,1024]{1,0:T(8,128)(2,1)} %copy-done.14, bf16[864,1024]{1,0:T(8,128)(2,1)} %get-tuple-element.278.mem_ref, ...), custom_call_target="tpu_custom_call" | custom-call | tf_op jit(solution)/shard_map/cond/branch_1_fun/enc_ffn_back/pallas_call | solution.py:489
  287.0 2.2 fusion.3
  289.4 76.0 %finish.1 = (bf16[864,512]{1,0:T(8,128)(2,1)}, bf16[2,512,512]{2,1,0:T(8,128)(2,1)}, f32[512,1024]{1,0:T(8,128)}, f32[1024,512]{1,0:T(8,128)}, f32[64,1024]{1,0:T(8,128)}) custom-call(bf16[864,3072]{1,0:T(8,128)(2,1)} %get-tuple-element.348.q_ref.k_ref.v_ref, bf16[864,3072]{1,0:T(8,128)(2,1)} %get-tuple-element.348.q_ref.k_ref.v_ref, ...), custom_call_target="tpu_custom_call" | custom-call | tf_op jit(solution)/shard_map/finish/pallas_call | solution.py:997
  365.4 1.4 slice.52
  366.8 1.4 slice.53
  368.1 1.0 slice_bitcast_fusion.1
  370.1 1.2 bitcast_select_fusion
  371.2 0.9 copy.114
  372.1 1.3 copy.115
  373.4 1.0 copy-done.11
  374.5 1.3 copy.116
  (35 shorter events, 1.0 us)
Async XLA Ops:
  1.6 248.9 %copy-start.15 = (bf16[32,1024]{1,0:T(8,128)(2,1)}, bf16[32,1024]{1,0:T(8,128)(2,1)S(1)}, u32[]{:S(2)}) copy-start(bf16[32,1024]{1,0:T(8,128)(2,1)S(1)} %get-tuple-element.418.pv_ref) | copy-start | bytes 196612
  1.6 248.8 %copy-start.16 = (bf16[32,1024]{1,0:T(8,128)(2,1)}, bf16[32,1024]{1,0:T(8,128)(2,1)S(1)}, u32[]{:S(2)}) copy-start(bf16[32,1024]{1,0:T(8,128)(2,1)S(1)} %get-tuple-element.419.pk_ref) | copy-start | bytes 196612
  12.4 26.2 %copy-start.1 = (bf16[1024,1024]{1,0:T(8,128)(2,1)S(1)}, bf16[1024,1024]{1,0:T(8,128)(2,1)}, u32[]{:S(2)}) copy-start(bf16[1024,1024]{1,0:T(8,128)(2,1)} %get-tuple-element.195.wo_ref) | copy-start | bytes 6291460 | tf_op jit(solution)/shard_map/cond
  12.4 26.2 %copy-start.3 = (bf16[1024,512]{1,0:T(8,128)(2,1)S(1)}, bf16[1024,512]{1,0:T(8,128)(2,1)}, u32[]{:S(2)}) copy-start(bf16[1024,512]{1,0:T(8,128)(2,1)} %get-tuple-element.199.down_ref) | copy-start | bytes 3145732 | tf_op jit(solution)/shard_map/cond
  12.4 26.2 %copy-start.5 = (bf16[512,1024]{1,0:T(8,128)(2,1)S(1)}, bf16[512,1024]{1,0:T(8,128)(2,1)}, u32[]{:S(2)}) copy-start(bf16[512,1024]{1,0:T(8,128)(2,1)} %get-tuple-element.201.up_ref) | copy-start | bytes 3145732 | tf_op jit(solution)/shard_map/cond
  12.4 26.2 %copy-start.21 = (f32[2,1024]{1,0:T(2,128)S(1)}, f32[2,1024]{1,0:T(2,128)}, u32[]{:S(2)}) copy-start(f32[2,1024]{1,0:T(2,128)} %get-tuple-element.196.gain_ref) | copy-start | bytes 24580 | tf_op jit(solution)/shard_map/cond
  12.4 26.2 %copy-start.23 = (f32[1,1024]{1,0:T(1,128)S(1)}, f32[1,1024]{1,0:T(1,128)}, u32[]{:S(2)}) copy-start(f32[1,1024]{1,0:T(1,128)} %get-tuple-element.202.upb_ref) | copy-start | bytes 12292 | tf_op jit(solution)/shard_map/cond
  12.5 26.2 %copy-start.25 = (f32[1,512]{1,0:T(1,128)S(1)}, f32[1,512]{1,0:T(1,128)}, u32[]{:S(2)}) copy-start(f32[1,512]{1,0:T(1,128)} %get-tuple-element.200.downb_ref) | copy-start | bytes 6148 | tf_op jit(solution)/shard_map/cond
  78.5 40.3 %collective-permute-start = (bf16[864,1024]{1,0:T(8,128)(2,1)}, bf16[864,1024]{1,0:T(8,128)(2,1)S(1)}, u32[]{:S(2)}, u32[]{:S(2)}) collective-permute-start(bf16[864,1024]{1,0:T(8,128)(2,1)} %get-tuple-element.351), channel_id=1, source_target_pairs={{0,16},{1,17},{2,18},{3,19},{4,20},{5,21},{6,22},{7,23},{8,24},{9,... | collective-permute-start | bytes 5308424 | tf_op jit(solution)/shard_map/ppermute | solution.py:1078
  118.8 131.6 %collective-permute-start.1 = (bf16[864,1024]{1,0:T(8,128)(2,1)}, bf16[864,1024]{1,0:T(8,128)(2,1)S(1)}, u32[]{:S(2)}, u32[]{:S(2)}) collective-permute-start(bf16[864,1024]{1,0:T(8,128)(2,1)} %get-tuple-element.366), channel_id=1, source_target_pairs={{16,0},{17,1},{18,2},{19,3},{20,4},{21,5},{22,6},{23,7},{24,8},{25... | collective-permute-start | bytes 5308424 | tf_op jit(solution)/shard_map/ppermute | solution.py:1082
  250.8 1.2 copy-start.14
  289.4 80.7 %copy-start.13 = (bf16[512,512]{1,0:T(8,128)(2,1)S(1)}, bf16[512,512]{1,0:T(8,128)(2,1)}, u32[]{:S(2)}) copy-start(bf16[512,512]{1,0:T(8,128)(2,1)} %get-tuple-element.386) | copy-start | bytes 1572868
  289.4 80.7 %copy-start.18 = (bf16[512,1024]{1,0:T(8,128)(2,1)S(1)}, bf16[512,1024]{1,0:T(8,128)(2,1)}, u32[]{:S(2)}) copy-start(bf16[512,1024]{1,0:T(8,128)(2,1)} %get-tuple-element.382) | copy-start | bytes 3145732
  365.4 4.7 %copy-start.17 = (bf16[2,512,512]{2,1,0:T(8,128)(2,1)S(1)}, bf16[2,512,512]{2,1,0:T(8,128)(2,1)}, u32[]{:S(2)}) copy-start(bf16[2,512,512]{2,1,0:T(8,128)(2,1)} %get-tuple-element.384) | copy-start | bytes 3145732
  369.1 2.1 copy-start.19
  370.1 2.1 copy-start.12
  372.1 2.3 copy-start.11

commit v4 on v3

--- a/solution.py
+++ b/solution.py
@@ -21,6 +21,8 @@
 big_negative = -1e30
 adapter_scale = 4.0
 chunk = 512
+wide = 1024
+ENC_ROWS = (SRC_LONG + SRC_SHORT) // 3
 vmem_bytes = 56 * 2**20
 
 phi_poly = (
@@ -84,7 +86,7 @@
     o_ref[...] = nn(x_ref[...], w_ref[...]).astype(BF)
 
 
-def product(x, w, tile=512):
+def product(x, w, tile=1024):
     rows, depth = x.shape
     width = w.shape[1]
     return pl.pallas_call(
@@ -98,10 +100,10 @@
     )(x, w)
 
 
-def back_product_kernel(*refs, parts, residual):
+def back_product_kernel(*refs, parts, residual, cuts):
     grads = refs[:parts]
     w_ref = refs[parts]
-    o_ref = refs[-1]
+    outs = refs[-len(cuts) :]
     total = None
     width = grads[0].shape[1]
     for i, grad in enumerate(grads):
@@ -109,13 +111,15 @@
         total = term if total is None else total + term
     if residual:
         total = total + refs[parts + 1][...]
-    o_ref[...] = total.astype(BF)
-
-
-def back_product(grads, w, residual=None, tile=256):
+    for (start, size), o_ref in zip(cuts, outs):
+        o_ref[...] = total[start : start + size].astype(BF)
+
+
+def back_product(grads, w, residual=None, tile=512, cuts=None):
     rows, width = grads[0].shape
     depth = w.shape[0]
     parts = len(grads)
+    cuts = cuts or ((0, rows),)
     specs = [whole((rows, width))] * parts + [
         pl.BlockSpec((tile, parts * width), lambda i: (i, 0))
     ]
@@ -124,11 +128,13 @@
         specs.append(pl.BlockSpec((rows, tile), lambda i: (0, i)))
         args.append(residual)
     return pl.pallas_call(
-        functools.partial(back_product_kernel, parts=parts, residual=residual is not None),
+        functools.partial(
+            back_product_kernel, parts=parts, residual=residual is not None, cuts=cuts
+        ),
         grid=(depth // tile,),
         in_specs=specs,
-        out_specs=pl.BlockSpec((rows, tile), lambda i: (0, i)),
-        out_shape=jax.ShapeDtypeStruct((rows, depth), BF),
+        out_specs=[pl.BlockSpec((size, tile), lambda i: (0, i)) for _, size in cuts],
+        out_shape=[jax.ShapeDtypeStruct((size, depth), BF) for _, size in cuts],
         compiler_params=params(),
         name="back_product",
     )(*args)
@@ -145,28 +151,40 @@
     return jnp.asarray(value, BF)
 
 
-def stacked(rows_ref, prefix_ref, start, count):
-    rows = rows_ref[start : start + count]
-    if prefix_ref is None:
-        return rows
-    return jnp.concatenate([rows, prefix_ref[...]], 0)
-
-
-def attend_kernel(*refs, segs, prefix, causal):
-    len_ref, q_ref, k_ref, v_ref = refs[:4]
-    at = 4
+def rows_of(refs, start, count):
+    parts = []
+    for ref in refs:
+        size = ref.shape[0]
+        low, high = max(start, 0), min(start + count, size)
+        if low < high:
+            parts.append(ref[low:high])
+        start -= size
+    return parts
+
+
+def stacked(refs, prefix_ref, start, count):
+    parts = rows_of(refs, start, count)
+    if prefix_ref is not None:
+        parts.append(prefix_ref[...])
+    return parts[0] if len(parts) == 1 else jnp.concatenate(parts, 0)
+
+
+def attend_kernel(*refs, segs, prefix, causal, pieces, which):
+    len_ref, q_ref = refs[:2]
+    k_refs, v_refs = refs[2 : 2 + pieces], refs[2 + pieces : 2 + 2 * pieces]
+    at = 2 + 2 * pieces
     pk_ref = pv_ref = None
     if prefix:
-        pk_ref, pv_ref = refs[4:6]
-        at = 6
+        pk_ref, pv_ref = refs[at : at + 2]
+        at += 2
     o_ref, inv_ref = refs[at : at + 2]
     p_refs = refs[at + 2 :]
     for seg, (q0, nq, k0, nk) in enumerate(segs):
-        keys = stacked(k_ref, pk_ref, k0, nk)
-        values = stacked(v_ref, pv_ref, k0, nk)
+        keys = stacked(k_refs, pk_ref, k0, nk)
+        values = stacked(v_refs, pv_ref, k0, nk)
         count = keys.shape[0]
         row = lax.broadcasted_iota(jnp.int32, (count, 1), 0)
-        seen = row < jnp.minimum(len_ref[0, seg], nk)
+        seen = row < jnp.minimum(len_ref[0, which + seg], nk)
         if prefix:
             seen = seen | ((row >= nk) & (row < nk + PRE))
         queries = q_ref[q0 : q0 + nq] * bf(HD**-0.5)
@@ -194,28 +212,28 @@
         inv_ref[q0 : q0 + nq] = inv
 
 
-def column_spec(rows, offset):
-    return pl.BlockSpec((rows, LANES), lambda h: (0, h + offset))
-
-
-def attend(lengths, q, k, v, prefixes, segs, causal):
+def column_spec(rows, offset, row_block=0):
+    return pl.BlockSpec((rows, LANES), lambda h: (row_block, h + offset))
+
+
+def attend(lengths, q, keys, values, prefixes, segs, causal, which=0):
     pairs = 8
-    q_rows, k_rows = q[0].shape[0], k[0].shape[0]
+    q_rows = q[1]
     prefix = prefixes is not None
     extra = PRE_PAD if prefix else 0
-    specs = [
-        pl.BlockSpec(memory_space=pltpu.SMEM),
-        column_spec(q_rows, q[1]),
-        column_spec(k_rows, k[1]),
-        column_spec(k_rows, v[1]),
-    ]
-    args = [lengths, q[0], k[0], v[0]]
+    specs = [pl.BlockSpec(memory_space=pltpu.SMEM)]
+    args = [lengths]
+    for array, rows, block, offset in [q, *keys, *values]:
+        specs.append(column_spec(rows, offset, block))
+        args.append(array)
     if prefix:
         specs += [column_spec(PRE_PAD, 0)] * 2
         args += list(prefixes)
     weight_shapes = [(2 * pairs, nk + extra, nq) for _, nq, _, nk in segs]
     return pl.pallas_call(
-        functools.partial(attend_kernel, segs=segs, prefix=prefix, causal=causal),
+        functools.partial(
+            attend_kernel, segs=segs, prefix=prefix, causal=causal, pieces=len(keys), which=which
+        ),
         grid=(pairs,),
         in_specs=specs,
         out_specs=[column_spec(q_rows, 0), column_spec(q_rows, 0)]
@@ -231,15 +249,15 @@
 
 
 def attend_back_pair(
-    q_ref, k_ref, v_ref, o_ref, inv_ref, g_ref, pk_ref, pv_ref, p_refs, dq_ref, dk_ref, dv_ref, segs
+    q_ref, k_refs, v_refs, o_ref, inv_ref, g_refs, pk_ref, pv_ref, p_refs, dq_ref, dk_ref, dv_ref, segs
 ):
     prefix_totals = [None, None]
     scale = HD**-0.5
     for seg, (q0, nq, k0, nk) in enumerate(segs):
-        keys = stacked(k_ref, pk_ref, k0, nk)
-        values = stacked(v_ref, pv_ref, k0, nk)
+        keys = stacked(k_refs, pk_ref, k0, nk)
+        values = stacked(v_refs, pv_ref, k0, nk)
         queries = q_ref[q0 : q0 + nq]
-        grads = g_ref[q0 : q0 + nq].astype(F32) * inv_ref[q0 : q0 + nq]
+        grads = stacked(g_refs, None, q0, nq).astype(F32) * inv_ref[q0 : q0 + nq]
         grads_low = grads.astype(BF)
         dots = grads * o_ref[q0 : q0 + nq].astype(F32)
         dq = dk = dv = None
@@ -262,8 +280,9 @@
             dv = dv_head if dv is None else jnp.where(own, dv_head, dv)
         dk = dk * scale
         dq_ref[q0 : q0 + nq] = (dq * scale).astype(BF)
-        dk_ref[k0 : k0 + nk] = dk[:nk].astype(BF)
-        dv_ref[k0 : k0 + nk] = dv[:nk].astype(BF)
+        at = k0 - segs[0][2]
+        dk_ref[at : at + nk] = dk[:nk].astype(BF)
+        dv_ref[at : at + nk] = dv[:nk].astype(BF)
         if pk_ref is not None:
             for i, grad in enumerate((dk, dv)):
                 part = grad[nk:]
@@ -271,31 +290,34 @@
     return prefix_totals
 
 
-def attend_back_kernel(*refs, segs, prefix):
-    at = 8 if prefix else 6
-    pk_ref, pv_ref = refs[6:8] if prefix else (None, None)
+def attend_back_kernel(*refs, segs, prefix, pieces):
+    q_ref, o_ref, inv_ref, g_ref = refs[:4]
+    k_refs, v_refs = refs[4 : 4 + pieces], refs[4 + pieces : 4 + 2 * pieces]
+    at = 4 + 2 * pieces
+    pk_ref = pv_ref = None
+    if prefix:
+        pk_ref, pv_ref = refs[at : at + 2]
+        at += 2
     outs = refs[at + len(segs) :]
     totals = attend_back_pair(
-        *refs[:6], pk_ref, pv_ref, refs[at : at + len(segs)], *outs[:3], segs
+        q_ref, k_refs, v_refs, o_ref, inv_ref, [g_ref], pk_ref, pv_ref,
+        refs[at : at + len(segs)], *outs[:3], segs,
     )
     if prefix:
         outs[3][...] = totals[0]
         outs[4][...] = totals[1]
 
 
-def attend_back(q, k, v, prefixes, attended, inverse, grad, weights, segs):
+def attend_back(q, keys, values, prefixes, attended, inverse, grad, weights, segs):
     pairs = 8
-    q_rows, k_rows = q[0].shape[0], k[0].shape[0]
+    q_rows = q[1]
+    k_rows = sum(nk for _, _, _, nk in segs)
     prefix = prefixes is not None
-    specs = [
-        column_spec(q_rows, q[1]),
-        column_spec(k_rows, k[1]),
-        column_spec(k_rows, v[1]),
-        column_spec(q_rows, 0),
-        column_spec(q_rows, 0),
-        column_spec(q_rows, 0),
-    ]
-    args = [q[0], k[0], v[0], attended, inverse, grad]
+    specs, args = [], []
+    own = [(a, q_rows, 0, 0) for a in (attended, inverse, grad)]
+    for array, rows, block, offset in [q, *own, *keys, *values]:
+        specs.append(column_spec(rows, offset, block))
+        args.append(array)
     if prefix:
         specs += [column_spec(PRE_PAD, 0)] * 2
         args += list(prefixes)
@@ -311,7 +333,9 @@
         out_specs += [column_spec(PRE_PAD, 0)] * 2
         out_shape += [jax.ShapeDtypeStruct((PRE_PAD, pairs * LANES), F32)] * 2
     return pl.pallas_call(
-        functools.partial(attend_back_kernel, segs=segs, prefix=prefix),
+        functools.partial(
+            attend_back_kernel, segs=segs, prefix=prefix, pieces=len(keys)
+        ),
         grid=(pairs,),
         in_specs=specs,
         out_specs=out_specs,
@@ -338,21 +362,19 @@
 
 def enc_ffn_kernel(
     x_ref, att_ref, wo_ref, gain_ref, in_ref, out_ref, down_ref, downb_ref, up_ref, upb_ref,
-    mem_ref, slope_ref, act_ref, low_ref, scales_ref, acc_ref,
+    mem_ref, slope_ref, pre_slope_ref, act_ref, low_ref, scales_ref, acc_ref,
 ):
     step = pl.program_id(0)
     last = pl.num_programs(0) - 1
 
     @pl.when(step == 0)
     def _():
-        for start, size in row_tiles(x_ref.shape[0]):
-            rows = slice(start, start + size)
-            first = x_ref[rows].astype(F32) + nn(att_ref[rows], wo_ref[...])
-            hat, scale = norm_rows(first)
-            normed = hat * gain_ref[0:1]
-            acc_ref[rows] = normed
-            low_ref[rows] = normed.astype(BF)
-            scales_ref[rows, 0:1] = scale
+        first = x_ref[...].astype(F32) + nn(att_ref[...], wo_ref[...])
+        hat, scale = norm_rows(first)
+        normed = hat * gain_ref[0:1]
+        acc_ref[...] = normed
+        low_ref[...] = normed.astype(BF)
+        scales_ref[:, 0:1] = scale
 
     @pl.when((step > 0) & (step < last))
     def _():
@@ -360,18 +382,19 @@
 
     @pl.when(step == last)
     def _():
-        ffn_step(low_ref, acc_ref, down_ref, up_ref, slope_ref, act_ref, downb_ref, adapter_scale)
-        for start, size in row_tiles(x_ref.shape[0]):
-            rows = slice(start, start + size)
-            hat, scale = norm_rows(acc_ref[rows] + adapter_scale * upb_ref[...])
-            mem_ref[rows] = (hat * gain_ref[1:2]).astype(BF)
-            scales_ref[rows, 1:2] = scale
-
-
-def enc_ffn(x, att, w):
-    rows, width = x.shape
+        ffn_step(
+            low_ref, acc_ref, down_ref, up_ref, pre_slope_ref, act_ref, downb_ref, adapter_scale
+        )
+        hat, scale = norm_rows(acc_ref[...] + adapter_scale * upb_ref[...])
+        mem_ref[...] = (hat * gain_ref[1:2]).astype(BF)
+        scales_ref[:, 1:2] = scale
+
+
+def enc_ffn(x, att, w, part):
+    width = x.shape[1]
+    rows = ENC_ROWS
     hidden = w["ffn_in"].shape[1]
-    steps = hidden // chunk
+    steps = hidden // wide
 
     def at(i):
         return jnp.clip(i - 1, 0, steps - 1)
@@ -380,12 +403,12 @@
         enc_ffn_kernel,
         grid=(steps + 2,),
         in_specs=[
-            whole((rows, width)),
-            whole((rows, width)),
+            pl.BlockSpec((rows, width), lambda i: (part, 0)),
+            pl.BlockSpec((rows, width), lambda i: (part, 0)),
             whole((width, width)),
             whole((2, width)),
-            pl.BlockSpec((width, chunk), lambda i: (0, at(i))),
-            pl.BlockSpec((chunk, width), lambda i: (at(i), 0)),
+            pl.BlockSpec((width, wide), lambda i: (0, at(i))),
+            pl.BlockSpec((wide, width), lambda i: (at(i), 0)),
             whole((width, chunk)),
             whole((1, chunk)),
             whole((chunk, width)),
@@ -393,14 +416,16 @@
         ],
         out_specs=[
             whole((rows, width)),
-            pl.BlockSpec((rows, chunk), lambda i: (0, jnp.clip(i - 1, 0, steps))),
+            pl.BlockSpec((rows, wide), lambda i: (0, at(i))),
+            whole((rows, chunk)),
             whole((rows, chunk)),
             whole((rows, width)),
             whole((rows, LANES)),
         ],
         out_shape=[
             jax.ShapeDtypeStruct((rows, width), BF),
-            jax.ShapeDtypeStruct((rows, hidden + chunk), BF),
+            jax.ShapeDtypeStruct((rows, hidden), BF),
+            jax.ShapeDtypeStruct((rows, chunk), BF),
             jax.ShapeDtypeStruct((rows, chunk), BF),
             jax.ShapeDtypeStruct((rows, width), BF),
             jax.ShapeDtypeStruct((rows, LANES), F32),
@@ -439,66 +464,55 @@
 
 
 def enc_ffn_back_kernel(
-    dmem_ref, mem_ref, low_ref, scales_ref, gain_ref, slope_ref, act_ref,
+    dmem_ref, mem_ref, low_ref, scales_ref, gain_ref, slope_ref, pre_slope_ref,
     in_ref, out_ref, down_ref, up_ref, wo_ref,
-    dfirst_ref, datt_ref, ddown_ref, ddownb_ref, dup_ref, dupb_ref,
-    acc_ref, grad_ref, pre_ref,
+    dfirst_ref, datt_ref, grad_ref, pre_ref,
+    acc_ref,
 ):
     step = pl.program_id(0)
     last = pl.num_programs(0) - 1
 
     @pl.when(step == 0)
     def _():
-        for start, size in row_tiles(dmem_ref.shape[0]):
-            rows = slice(start, start + size)
-            gain = gain_ref[1:2]
-            hat = mem_ref[rows].astype(F32) / gain
-            grad = norm_rows_back(
-                hat, scales_ref[rows, 1:2], dmem_ref[rows].astype(F32) * gain
-            )
-            acc_ref[rows] = grad
-            grad_ref[rows] = grad.astype(BF)
-        adapter_back(
-            grad_ref, acc_ref, low_ref, act_ref, slope_ref, down_ref, up_ref,
-            (ddown_ref, ddownb_ref, dup_ref, dupb_ref), pre_ref,
-        )
-
-    @pl.when(step > 0)
-    def _():
-        ffn_back_step(grad_ref, acc_ref, in_ref, out_ref, slope_ref)
+        gain = gain_ref[1:2]
+        hat = mem_ref[...].astype(F32) / gain
+        grad = norm_rows_back(hat, scales_ref[:, 1:2], dmem_ref[...].astype(F32) * gain)
+        low = grad.astype(BF)
+        grad_ref[...] = low
+        back = adapter_scale * nt(low, up_ref[...])
+        pre = (back * pre_slope_ref[...].astype(F32)).astype(BF)
+        pre_ref[...] = pre
+        acc_ref[...] = grad + nt(pre, down_ref[...])
+
+    ffn_back_step(grad_ref, acc_ref, in_ref, out_ref, slope_ref)
 
     @pl.when(step == last)
     def _():
-        for start, size in row_tiles(dmem_ref.shape[0]):
-            rows = slice(start, start + size)
-            gain = gain_ref[0:1]
-            hat = low_ref[rows].astype(F32) / gain
-            grad = norm_rows_back(hat, scales_ref[rows, 0:1], acc_ref[rows] * gain)
-            dfirst_ref[rows] = grad
-            datt_ref[rows] = nt(grad.astype(BF), wo_ref[...]).astype(BF)
-
-
-def enc_ffn_back(dmem, mem, low, scales, slope, act, w):
+        gain = gain_ref[0:1]
+        hat = low_ref[...].astype(F32) / gain
+        grad = norm_rows_back(hat, scales_ref[:, 0:1], acc_ref[...] * gain)
+        dfirst_ref[...] = grad
+        datt_ref[...] = nt(grad.astype(BF), wo_ref[...]).astype(BF)
+
+
+def enc_ffn_back(dmem, saved, w):
+    mem, slope, pre_slope, act, low, scales = saved
     rows, width = dmem.shape
     hidden = w["ffn_in"].shape[1]
-    steps = hidden // chunk
-
-    def at(i):
-        return jnp.clip(i - 1, 0, steps - 1)
-
+    steps = hidden // wide
     return pl.pallas_call(
         enc_ffn_back_kernel,
-        grid=(steps + 1,),
+        grid=(steps,),
         in_specs=[
             whole((rows, width)),
             whole((rows, width)),
             whole((rows, width)),
             whole((rows, LANES)),
             whole((2, width)),
-            pl.BlockSpec((rows, chunk), lambda i: (0, jnp.where(i == 0, steps, i - 1))),
+            pl.BlockSpec((rows, wide), lambda i: (0, i)),
             whole((rows, chunk)),
-            pl.BlockSpec((width, chunk), lambda i: (0, at(i))),
-            pl.BlockSpec((chunk, width), lambda i: (at(i), 0)),
+            pl.BlockSpec((width, wide), lambda i: (0, i)),
+            pl.BlockSpec((wide, width), lambda i: (i, 0)),
             whole((width, chunk)),
             whole((chunk, width)),
             whole((width, width)),
@@ -506,30 +520,47 @@
         out_specs=[
             whole((rows, width)),
             whole((rows, width)),
-            whole((width, chunk)),
-            whole((1, chunk)),
-            whole((chunk, width)),
-            whole((1, width)),
+            whole((rows, width)),
+            whole((rows, chunk)),
         ],
         out_shape=[
             jax.ShapeDtypeStruct((rows, width), F32),
             jax.ShapeDtypeStruct((rows, width), BF),
+            jax.ShapeDtypeStruct((rows, width), BF),
+            jax.ShapeDtypeStruct((rows, chunk), BF),
+        ],
+        scratch_shapes=[pltpu.VMEM((rows, width), F32)],
+        compiler_params=params(),
+        name="enc_ffn_back",
+    )(
+        dmem, mem, low, scales, w["gains"], slope, pre_slope,
+        w["ffn_in"], w["ffn_out"], w["down"], w["up"], w["out"],
+    )
+
+
+def adapter_grads_kernel(*refs, parts):
+    groups = [refs[n * parts : (n + 1) * parts] for n in range(4)]
+    low, act, grad, pre = [jnp.concatenate([r[...] for r in g], 0) for g in groups]
+    ddown_ref, ddownb_ref, dup_ref, dupb_ref = refs[4 * parts :]
+    ddown_ref[...] = tn(low, pre)
+    ddownb_ref[...] = jnp.sum(pre.astype(F32), axis=0, keepdims=True)
+    dup_ref[...] = adapter_scale * tn(act, grad)
+    dupb_ref[...] = adapter_scale * jnp.sum(grad.astype(F32), axis=0, keepdims=True)
+
+
+def adapter_grads(lows, acts, grads, pres):
+    width = lows[0].shape[1]
+    return pl.pallas_call(
+        functools.partial(adapter_grads_kernel, parts=len(lows)),
+        out_shape=[
             jax.ShapeDtypeStruct((width, chunk), F32),
             jax.ShapeDtypeStruct((1, chunk), F32),
             jax.ShapeDtypeStruct((chunk, width), F32),
             jax.ShapeDtypeStruct((1, width), F32),
         ],
-        scratch_shapes=[
-            pltpu.VMEM((rows, width), F32),
-            pltpu.VMEM((rows, width), BF),
-            pltpu.VMEM((rows, chunk), BF),
-        ],
         compiler_params=params(),
-        name="enc_ffn_back",
-    )(
-        dmem, mem, low, scales, w["gains"], slope, act,
-        w["ffn_in"], w["ffn_out"], w["down"], w["up"], w["out"],
-    )
+        name="adapter_grads",
+    )(*lows, *acts, *grads, *pres)
 
 
 def dec_mid_kernel(x_ref, att_ref, wo_ref, gain_ref, wq_ref, n_ref, scale_ref, cq_ref):
@@ -561,8 +592,8 @@
     len_ref, n_ref, catt_ref, cot_ref, wco_ref, cgain_ref, gain_ref,
     in_ref, out_ref, down_ref, downb_ref, up_ref, upb_ref,
     y_ref, dsecond_ref, dcatt_ref, ddown_ref, ddownb_ref, dup_ref, dupb_ref,
-    acc_ref, low_ref, grad_ref, slope_ref, act_ref, pre_ref, scale_ref,
-    *, steps,
+    acc_ref, low_ref, grad_ref, slope_ref, pre_slope_ref, act_ref, pre_ref, scale_ref,
+    *, steps, which,
 ):
     step = pl.program_id(0)
     tiles = row_tiles(n_ref.shape[0], TGT)
@@ -585,21 +616,21 @@
     @pl.when(step == steps + 1)
     def _():
         ffn_step(
-            low_ref, acc_ref, down_ref, up_ref, slope_ref.at[steps], act_ref, downb_ref,
+            low_ref, acc_ref, down_ref, up_ref, pre_slope_ref, act_ref, downb_ref,
             adapter_scale,
         )
-        for tile, (start, size) in enumerate(tiles):
+        for start, size in tiles:
             rows = slice(start, start + size)
             gain = gain_ref[1:2]
             hat, scale = norm_rows(acc_ref[rows] + adapter_scale * upb_ref[...])
-            valid = lax.broadcasted_iota(jnp.int32, (size, 1), 0) < len_ref[0, tile]
+            valid = lax.broadcasted_iota(jnp.int32, (size, 1), 0) < len_ref[0, which]
             y_ref[rows] = jnp.where(valid, hat * gain, 0.0).astype(BF)
             cot = jnp.where(valid, cot_ref[rows].astype(F32), 0.0)
             grad = norm_rows_back(hat, scale, cot * gain)
             acc_ref[rows] = grad
             grad_ref[rows] = grad.astype(BF)
         adapter_back(
-            grad_ref, acc_ref, low_ref, act_ref, slope_ref.at[steps], down_ref, up_ref,
+            grad_ref, acc_ref, low_ref, act_ref, pre_slope_ref, down_ref, up_ref,
             (ddown_ref, ddownb_ref, dup_ref, dupb_ref), pre_ref,
         )
 
@@ -618,27 +649,27 @@
             dcatt_ref[rows] = nt(grad.astype(BF), wco_ref[...]).astype(BF)
 
 
-def dec_ffn(lengths, n, catt, cot, w, cross):
-    rows, width = n.shape
+def dec_ffn(lengths, n, catt, cot, w, cross, which):
+    rows, width = catt.shape
     hidden = w["ffn_in"].shape[1]
-    steps = hidden // chunk
+    steps = hidden // wide
 
     def at(i):
         return jnp.where(i <= steps, jnp.clip(i - 1, 0, steps - 1), jnp.clip(2 * steps + 1 - i, 0, steps - 1))
 
     return pl.pallas_call(
-        functools.partial(dec_ffn_kernel, steps=steps),
+        functools.partial(dec_ffn_kernel, steps=steps, which=which),
         grid=(2 * steps + 2,),
         in_specs=[
             pl.BlockSpec(memory_space=pltpu.SMEM),
+            pl.BlockSpec((rows, width), lambda i: (which, 0)),
             whole((rows, width)),
-            whole((rows, width)),
-            whole((rows, width)),
+            pl.BlockSpec((rows, width), lambda i: (which, 0)),
             whole((width, width)),
             whole((1, width)),
             whole((2, width)),
-            pl.BlockSpec((width, chunk), lambda i: (0, at(i))),
-            pl.BlockSpec((chunk, width), lambda i: (at(i), 0)),
+            pl.BlockSpec((width, wide), lambda i: (0, at(i))),
+            pl.BlockSpec((wide, width), lambda i: (at(i), 0)),
             whole((width, chunk)),
             whole((1, chunk)),
             whole((chunk, width)),
@@ -666,7 +697,8 @@
             pltpu.VMEM((rows, width), F32),
             pltpu.VMEM((rows, width), BF),
             pltpu.VMEM((rows, width), BF),
-            pltpu.VMEM((steps + 1, rows, chunk), BF),
+            pltpu.VMEM((steps, rows, wide), BF),
+            pltpu.VMEM((rows, chunk), BF),
             pltpu.VMEM((rows, chunk), BF),
             pltpu.VMEM((rows, chunk), BF),
             pltpu.VMEM((rows, LANES), F32),
@@ -706,54 +738,49 @@
 
 enc_segs = ((0, SRC_LONG, 0, SRC_LONG), (SRC_LONG, SRC_SHORT, SRC_LONG, SRC_SHORT))
 dec_segs = ((0, TGT, 0, TGT), (TGT, TGT, TGT, TGT))
-cross_segs = ((0, TGT, 0, SRC_LONG), (TGT, TGT, SRC_LONG, SRC_SHORT))
-
-
-def encoder_forward(x, lengths, w):
-    qkv = product(x, w["qkv"])
-    att, inv, *weights = attend(
-        lengths, (qkv, 0), (qkv, 8), (qkv, 16), w["prefix"], enc_segs, False
-    )
-    mem, slope, act, low, scales = enc_ffn(x, att, w)
-    return mem, (qkv, att, inv, weights, mem, slope, act, low, scales)
-
-
-def encoder_back_ffn(saved, dmem, w):
-    mem, slope, act, low, scales = saved[4:]
-    dfirst, datt, *adapter = enc_ffn_back(dmem, mem, low, scales, slope, act, w)
-    return dfirst, datt, adapter
+cross_segs = (((0, TGT, 0, SRC_LONG),), ((0, TGT, SRC_LONG % ENC_ROWS, SRC_SHORT),))
+
+
+def self_columns(qkv):
+    rows = qkv.shape[0]
+    return (qkv, rows, 0, 0), [(qkv, rows, 0, 8)], [(qkv, rows, 0, 16)]
+
+
+def cross_columns(cq, kvs, which):
+    return (
+        (cq, TGT, which, 0),
+        [(kv, ENC_ROWS, 0, 0) for kv in kvs],
+        [(kv, ENC_ROWS, 0, 8) for kv in kvs],
+    )
 
 
 def decoder_self(t, lengths, w, cross):
     qkv = product(t, w["qkv"])
-    att, inv, *weights = attend(
-        lengths, (qkv, 0), (qkv, 8), (qkv, 16), w["prefix"], dec_segs, True
-    )
+    att, inv, *weights = attend(lengths, *self_columns(qkv), w["prefix"], dec_segs, True)
     n, scale, cq = dec_mid(t, att, w, cross)
     return cq, (qkv, att, inv, weights, n, scale)
 
 
-def decoder_cross(kept, mem, cq, cot, src_lengths, tgt_lengths, w, cross):
-    n = kept[4]
-    kv = product(mem, cross["pairs"])
-    catt, cinv, *cweights = attend(
-        src_lengths, (cq, 0), (kv, 0), (kv, 8), None, cross_segs, False
-    )
-    y, dsecond, dcatt, *adapter = dec_ffn(tgt_lengths, n, catt, cot, w, cross)
-    dcq, dck, dcv = attend_back(
-        (cq, 0), (kv, 0), (kv, 8), None, catt, cinv, dcatt, cweights, cross_segs
-    )
-    dmem = back_product([dck, dcv], cross["pairs"])
-    return y, dmem, dcq, dsecond, adapter
+def cross_forward(lengths, cq, kvs, which):
+    return attend(
+        lengths, *cross_columns(cq, kvs, which), None, cross_segs[which], False, which
+    )
+
+
+def cross_backward(cq, kvs, forward, dcatt, which):
+    catt, inv, *weights = forward
+    return attend_back(
+        *cross_columns(cq, kvs, which), None, catt, inv, dcatt, weights, cross_segs[which]
+    )
 
 
 def decoder_self_back(kept, dsecond, dcq, w, cross):
     qkv, att, inv, weights, n, scale = kept
     dfirst, datt = dec_mid_back(dsecond, dcq, n, scale, w, cross)
     dq, dk, dv, *dprefix = attend_back(
-        (qkv, 0), (qkv, 8), (qkv, 16), w["prefix"], att, inv, datt, weights, dec_segs
-    )
-    return back_product([dq, dk, dv], w["qkv"], dfirst), dprefix
+        *self_columns(qkv), w["prefix"], att, inv, datt, weights, dec_segs
+    )
+    return back_product([dq, dk, dv], w["qkv"], dfirst)[0], dprefix
 
 
 def small_shape(devices):
@@ -761,12 +788,12 @@
 
 
 def finish_kernel(
-    q_ref, k_ref, v_ref, o_ref, inv_ref, g_ref, pk_ref, pv_ref, pl_ref, ps_ref,
-    dfirst_ref, wqkv_ref, up_ref, down_ref, upb_ref, downb_ref, dpk_ref, dpv_ref,
-    y_ref, dt_ref,
+    q_ref, k_ref, v_ref, o_ref, inv_ref, g0_ref, g1_ref, g2_ref, pk_ref, pv_ref, pl_ref, ps_ref,
+    dfirst0_ref, dfirst1_ref, dfirst2_ref, wqkv_ref, up_ref, down_ref, upb_ref, downb_ref, dpk_ref, dpv_ref,
+    lows,
     source_ref, low_ref, o_up_ref, o_down_ref, o_small_ref,
     dq, dk, dv, small, mine, theirs, half_sum, landed, total, result,
-    small_landed, small_total, small_result, dx_low, dx_high, dx_landed, lows, lows_landed,
+    small_landed, small_total, small_result, dx_low, dx_high, dx_landed, lows_landed,
     pair_sems, spread_sems, gather_sems, back_sems, small_sems, share_sems, cross_sems,
     *, devices,
 ):
@@ -872,8 +899,6 @@
 
         @pl.when(jnp.logical_not(is_encoder))
         def _():
-            lows[0] = y_ref[...]
-            lows[1] = dt_ref[...]
             send_low().start()
             small[0:PRE_PAD] = dpk_ref[...] * scale
             small[PRE_PAD : 2 * PRE_PAD] = dpv_ref[...] * scale
@@ -883,7 +908,8 @@
         at = pl.multiple_of(step * LANES, LANES)
         lanes = pl.ds(at, LANES)
         prefix_totals = attend_back_pair(
-            q_ref, k_ref, v_ref, o_ref, inv_ref, g_ref, pk_ref, pv_ref, (pl_ref, ps_ref),
+            q_ref, [k_ref], [v_ref], o_ref, inv_ref, [g0_ref, g1_ref, g2_ref], pk_ref, pv_ref,
+            (pl_ref, ps_ref),
             dq.at[:, lanes], dk.at[:, lanes], dv.at[:, lanes], enc_segs,
         )
         small[0:PRE_PAD, lanes] = prefix_totals[0] * scale
@@ -919,7 +945,7 @@
 
         @pl.when(is_encoder & (step == pairs + i))
         def _(i=i):
-            acc = dfirst_ref[...]
+            acc = jnp.concatenate([dfirst0_ref[...], dfirst1_ref[...], dfirst2_ref[...]], 0)
             for n, grad in enumerate((dq, dk, dv)):
                 acc = acc + nt(grad[...], wqkv_ref[:, n * width : (n + 1) * width])
             if i < 2:
@@ -970,13 +996,13 @@
                 source_ref[:, i * tile : (i + 1) * tile] = dx_landed[i]
 
 
-def finish(saved, datt, dfirst, w, adapter, dec_prefix, y_low, dt_low):
-    qkv, att, inv, weights = saved[:4]
+def finish(saved, datts, dfirsts, w, adapter, dec_prefix, lows):
+    qkv, att, inv, weights = saved
     ddown, ddownb, dup, dupb = adapter
     devices = lax.axis_size("dp")
     chips = devices // 2
-    rows, width = dfirst.shape
-    targets = y_low.shape[0]
+    rows, width = att.shape
+    targets = lows.shape[1]
     pairs, tile = 8, 256
     half = width // 2
     part = width // devices
@@ -997,16 +1023,22 @@
     return pl.pallas_call(
         functools.partial(finish_kernel, devices=devices),
         grid=(pairs + 4,),
-        in_specs=[pair(0), pair(8), pair(16), pair(0), pair(0), pair(0), prefix_pair, prefix_pair]
+        in_specs=[pair(0), pair(8), pair(16), pair(0), pair(0)]
+        + [pl.BlockSpec((ENC_ROWS, LANES), lambda i: (0, jnp.minimum(i, pairs - 1)))] * 3
+        + [prefix_pair] * 2
         + [
             pl.BlockSpec((2,) + p.shape[1:], lambda i: (jnp.minimum(i, pairs - 1), 0, 0))
             for p in weights
         ]
         + [
-            pl.BlockSpec((rows, tile), lambda i: (0, at(i))),
+            pl.BlockSpec((ENC_ROWS, tile), lambda i: (0, at(i))),
+        ]
+        * 3
+        + [
             pl.BlockSpec((tile, 3 * width), lambda i: (at(i), 0)),
         ]
-        + [once(a.shape) for a in (dup, ddown, dupb, ddownb, *dec_prefix, y_low, dt_low)],
+        + [once(a.shape) for a in (dup, ddown, dupb, ddownb, *dec_prefix)]
+        + [pl.BlockSpec(memory_space=pl.ANY)],
         out_specs=[
             once((rows, half)), once((2, targets, half)), once(dup.shape), once(ddown.shape),
             once((2 * PRE_PAD, width)),
@@ -1026,7 +1058,7 @@
             vmem((devices - 1, small_rows, small_cols), F32), vmem((small_rows, small_cols), F32),
             vmem((2 * PRE_PAD, width), F32),
             vmem((rows, half), BF), vmem((2, rows, tile), BF), vmem((2, rows, tile), BF),
-            vmem((2, targets, half), BF), vmem((2, targets, half), BF),
+            vmem((2, targets, half), BF),
             dma((2,)), dma((2, chips - 1)), dma((2, chips - 1)), dma((2, chips)),
             dma((2, devices - 1)), dma((2, devices - 1)), dma((2, 3)),
         ],
@@ -1035,8 +1067,8 @@
         ),
         name="finish",
     )(
-        qkv, qkv, qkv, att, inv, datt, *w["prefix"], *weights,
-        dfirst, w["qkv"], dup, ddown, dupb, ddownb, *dec_prefix, y_low, dt_low,
+        qkv, qkv, qkv, att, inv, *datts, *w["prefix"], *weights,
+        *dfirsts, w["qkv"], dup, ddown, dupb, ddownb, *dec_prefix, lows,
     )
 
 
@@ -1099,37 +1131,101 @@
     cross = dict(query=cross_query, pairs=cross_pairs, out=cross_out, gain=cross_gain[None])
     half = sources.shape[1] // 2
 
-    (mem, saved), (cq, kept), _ = on_section(
-        is_encoder,
-        lambda: (encoder_forward(sources, source_lengths, w), ()),
-        lambda: (decoder_self(targets, target_lengths, w, cross), ()),
-    )
-    mem_here = to_decoder(mem)
-    _, (y, dmem, dcq, dsecond, dec_adapter), _ = on_section(
-        is_encoder,
-        lambda *a: ((), ()),
-        lambda *a: (decoder_cross(*a, cotangent, source_lengths, target_lengths, w, cross), ()),
-        kept, mem_here, cq,
-    )
-    dmem_here = to_encoder(dmem)
-
-    def encoder_c1(saved, dmem, kept, dsecond, dcq, dec_adapter):
-        dfirst, datt, adapter = encoder_back_ffn(saved, dmem, w)
-        return (dfirst, datt), adapter
-
-    def decoder_c1(saved, dmem, kept, dsecond, dcq, dec_adapter):
-        return decoder_self_back(kept, dsecond, dcq, w, cross), dec_adapter
-
-    (dfirst, datt), (dt, dec_prefix), adapter = on_section(
-        is_encoder, encoder_c1, decoder_c1, saved, dmem_here, kept, dsecond, dcq, dec_adapter
-    )
+    def at_encoder(work, *operands):
+        return on_section(is_encoder, lambda *a: (work(*a), ()), lambda *a: ((), ()), *operands)[0]
+
+    def at_decoder(work, *operands):
+        return on_section(is_encoder, lambda *a: ((), ()), lambda *a: (work(*a), ()), *operands)[1]
+
+    def at_both(enc_work, dec_work, *operands):
+        return on_section(
+            is_encoder, lambda *a: (enc_work(*a), ()), lambda *a: (dec_work(*a), ()), *operands
+        )[:2]
+
+    def encoder_start():
+        qkv = product(sources, w["qkv"])
+        att, inv, *weights = attend(
+            source_lengths, *self_columns(qkv), w["prefix"], enc_segs, False
+        )
+        return (qkv, att, inv, weights), enc_ffn(sources, att, w, 2)
+
+    (saved, part2), (cq, kept) = at_both(
+        encoder_start, lambda: decoder_self(targets, target_lengths, w, cross)
+    )
+    mem2 = to_decoder(part2[0])
+    part1 = at_encoder(lambda saved: enc_ffn(sources, saved[1], w, 1), saved)
+    mem1 = to_decoder(part1[0])
+
+    def decoder_short(saved, mem2, cq):
+        kv2 = product(mem2, cross["pairs"])
+        return kv2, cross_forward(source_lengths, cq, [kv2], 1)
+
+    part0, (kv2, short) = at_both(
+        lambda saved, mem2, cq: enc_ffn(sources, saved[1], w, 0), decoder_short, saved, mem2, cq
+    )
+    mem0 = to_decoder(part0[0])
+    kv1 = at_decoder(lambda mem1: product(mem1, cross["pairs"]), mem1)
+
+    def decoder_long(mem0, kv1, kv2, cq, kept):
+        kvs = [product(mem0, cross["pairs"]), kv1, kv2]
+        long = cross_forward(source_lengths, cq, kvs, 0)
+        y, dsecond, dcatt, *adapter = dec_ffn(
+            target_lengths, kept[4], long[0], cotangent, w, cross, 0
+        )
+        dcq, dck, dcv = cross_backward(cq, kvs, long, dcatt, 0)
+        cuts = ((0, ENC_ROWS), (ENC_ROWS, ENC_ROWS), (2 * ENC_ROWS, SRC_LONG - 2 * ENC_ROWS))
+        return back_product([dck, dcv], cross["pairs"], cuts=cuts), y, dsecond, dcq, adapter
+
+    dmems, *long = at_decoder(decoder_long, mem0, kv1, kv2, cq, kept)
+    dmem0, dmem1, dmem2 = [to_encoder(block) for block in dmems]
+
+    def decoder_short_back(dmem0, part0, kv2, cq, kept, short):
+        y, dsecond, dcatt, *adapter = dec_ffn(
+            target_lengths, kept[4], short[0], cotangent, w, cross, 1
+        )
+        dcq, dck, dcv = cross_backward(cq, [kv2], short, dcatt, 1)
+        return back_product([dck, dcv], cross["pairs"])[0], y, dsecond, dcq, adapter
+
+    back0, (dmem_short, *short) = at_both(
+        lambda dmem0, part0, *a: enc_ffn_back(dmem0, part0, w),
+        decoder_short_back, dmem0, part0, kv2, cq, kept, short,
+    )
+    dmem_short = to_encoder(dmem_short)
+
+    def decoder_end(dmem1, part1, kept, long, short):
+        y, dsecond, dcq = [jnp.concatenate([a, b], 0) for a, b in zip(long[:3], short[:3])]
+        dt, dprefix = decoder_self_back(kept, dsecond, dcq, w, cross)
+        adapter = jax.tree.map(jnp.add, long[3], short[3])
+        highs = jnp.stack([y[:, half:], dt[:, half:]])
+        return highs, jnp.stack([y[:, :half], dt[:, :half]]), dprefix, adapter
+
+    back1, (highs, lows, dec_prefix, dec_adapter) = at_both(
+        lambda dmem1, part1, *a: enc_ffn_back(dmem1, part1, w),
+        decoder_end, dmem1, part1, kept, long, short,
+    )
+
+    def encoder_end(dmem2, dmem_short, part0, part1, part2, back0, back1, dec_adapter):
+        back2 = enc_ffn_back(jnp.concatenate([dmem2, dmem_short], 0), part2, w)
+        parts, backs = (part0, part1, part2), (back0, back1, back2)
+        adapter = adapter_grads(
+            [p[4] for p in parts], [p[3] for p in parts],
+            [b[2] for b in backs], [b[3] for b in backs],
+        )
+        return back2, list(adapter)
+
+    back2, _, adapter = on_section(
+        is_encoder, encoder_end, lambda *a: ((), list(a[-1])),
+        dmem2, dmem_short, part0, part1, part2, back0, back1, dec_adapter,
+    )
+    backs = (back0, back1, back2)
     source_grad, low, up, down, small = finish(
-        saved, datt, dfirst, w, adapter, dec_prefix, y[:, :half], dt[:, :half]
-    )
+        saved, [b[1] for b in backs], [b[0] for b in backs], w, adapter, dec_prefix, lows
+    )
+    target_halves = jnp.where(is_encoder, low, highs)
     return (
-        jnp.where(is_encoder, low[0], y[:, half:]),
+        target_halves[0],
         source_grad,
-        jnp.where(is_encoder, low[1], dt[:, half:]),
+        target_halves[1],
         jnp.stack([small[:PRE], small[PRE_PAD : PRE_PAD + PRE]])[None],
         down[None],
         small[PRE + 1 : PRE + 2, : down.shape[1]],

time: 381 us -> 372 us (0.976)
  Pallas kernels: 184 us -> 233 us
  waiting for transfers between devices: 153 us -> 105 us
  local copies, waits for them, and re-layouts: 18.4 us -> 11.2 us
  starting transfers between devices: 16.7 us -> 11.5 us
    ppermute x1 -> x4, waiting for transfers between devices: 128 us -> 91.7 us  [to_encoder(): return lax.ppermute(block, 'section', [(1, 0)])]
    pallas_call x2 -> x7, Pallas kernels: 71.8 us -> 101 us  [the longest x3 48.9 us: enc_ffn(): pl.pallas_call(enc_ffn_kernel, grid=(steps + 2,), in_specs=[pl.BlockSpec(...]
    pallas_call x1, Pallas kernels: 76 us -> 95.9 us  [finish(): pl.pallas_call(functools.partial(finish_kernel, devices=devices), grid=(p...]
    ppermute x1 -> x3, waiting for transfers between devices: 24.9 us -> 12.9 us  [to_decoder(): return lax.ppermute(block, 'section', [(0, 1)])]
    ppermute x1 -> x3, starting transfers between devices: 15.4 us -> 6.39 us  [to_decoder(): return lax.ppermute(block, 'section', [(0, 1)])]
    slice x2 -> x0, local copies, waits for them, and re-layouts: 4.14 us -> none  [the longest x1 2.25 us: per_device(): dt[:, half:]]
    cond x15 -> x30, local copies, waits for them, and re-layouts: 4.11 us -> 0.07 us
    ppermute x1 -> x4, starting transfers between devices: 1.28 us -> 5.16 us  [to_encoder(): return lax.ppermute(block, 'section', [(1, 0)])]
  transfers between devices with their start and end apart: 2 -> 7, of which waited for: 2 -> 3; matrix products, arithmetic and copies ran while one was open for 1% -> 0% of each run, Pallas kernels for 0% -> 18%
where the time goes in v4:
time: 372 us; the launch traced here: 367 us
  Pallas kernels  233 us (63%)
  waiting for transfers between devices  105 us (28%)
  starting transfers between devices  11.5 us (3%)
  local copies, waits for them, and re-layouts  11.2 us (3%)
    pallas_call x1, Pallas kernels, finish(): pl.pallas_call(functools.partial(finish_kernel, devices=devices), grid=(p...  95.9 us
    ppermute x4, waiting for transfers between devices, to_encoder(): return lax.ppermute(block, 'section', [(1, 0)])  91.7 us
    pallas_call x3, Pallas kernels, enc_ffn(): pl.pallas_call(enc_ffn_kernel, grid=(steps + 2,), in_specs=[pl.BlockSpec(...  48.9 us
    pallas_call x3, Pallas kernels, enc_ffn_back(): pl.pallas_call(enc_ffn_back_kernel, grid=(steps,), in_specs=[whole((rows,...  47.4 us
    pallas_call x1, Pallas kernels, attend(): pl.pallas_call(functools.partial(attend_kernel, segs=segs, prefix=prefix,...  26.2 us
    ppermute x3, waiting for transfers between devices, to_decoder(): return lax.ppermute(block, 'section', [(0, 1)])  12.9 us
    pallas_call x1, Pallas kernels, product(): pl.pallas_call(product_kernel, grid=(width // tile,), in_specs=[whole((ro...  9.68 us
  transfers between devices with their start and end apart: 7, of which 3 were waited for; matrix products, arithmetic and copies ran while one was open for 0% of the time, Pallas kernels for 18%

profile of v4, /device:TPU:0, one launch (start us, length us, event | category | flops | bytes accessed | tf_op | source)
XLA Modules:
  0.0 366.5 jit_solution(743737908596517418)
XLA Ops:
  1.6 51.7 %conditional.8 = (bf16[864,3072]{1,0:T(8,128)(2,1)}, bf16[864,1024]{1,0:T(8,128)(2,1)}, f32[864,1024]{1,0:T(8,128)}, bf16[16,800,768]{2,1,0:T(8,128)(2,1)}, bf16...) conditional(s32[]{:T(128)} %convert_element_type.4, ...), branch_computations={%region_0.1_spmd, %region_1.2_spmd} | conditional | bytes 16834880 | solution.py:1106
  1.8 9.7 %product.6.refs_1_.refs_2_.refs_3_ = bf16[864,3072]{1,0:T(8,128)(2,1)} custom-call(bf16[864,1024]{1,0:T(8,128)(2,1)} %get-tuple-element.349.x_ref, bf16[1024,3072]{1,0:T(8,128)(2,1)} %get-tuple-element.350.w_ref), custom_call_target="tpu_custom_call" | custom-call | tf_op jit(solution)/shard_map/cond/branch_1_fun/product/pallas_call | solution.py:92
  11.5 26.2 %attend.5 = (bf16[864,1024]{1,0:T(8,128)(2,1)}, f32[864,1024]{1,0:T(8,128)}, bf16[16,800,768]{2,1,0:T(8,128)(2,1)}, bf16[16,128,96]{2,1,0:T(8,128)(2,1)}) custom-call(s32[1,2]{1,0:T(1,128)} %get-tuple-element.351.refs_0_, bf16[864,3072]{1,0:T(8,128)(2,1)} %product.6.refs_1_.refs_2_.refs_3_, bf16[864,3072]{1,0:T(8,128)(2,1)} %product.6.refs_1_.refs_2_.refs_3_, ...), custom_call_target="tpu_custom_call" | custom-call | tf_op jit(solution)/shard_map/cond/branch_1_fun/attend/pallas_call | solution.py:233
  37.7 15.5 %enc_ffn.3 = (bf16[288,1024]{1,0:T(8,128)(2,1)}, bf16[288,4096]{1,0:T(8,128)(2,1)}, bf16[288,512]{1,0:T(8,128)(2,1)}, bf16[288,512]{1,0:T(8,128)(2,1)}, bf16[288,1024]{1,0:T(8,128)(2,1)}, /*index=5*/f32[288,128]{1,0:T(8,128)}) custom-call(bf16[864,1024]{1,0:T(8,128)(2,1)} %get-tuple-element.349.x_ref, bf16[864,1024]{1,0:T(8,128)(2,1)} %get-tuple-element.823.att_ref, ...), custom_call_target="tpu_custom_call" | custom-call | tf_op jit(solution)/shard_map/cond/branch_1_fun/enc_ffn/pallas_call | solution.py:402
  53.2 2.1 collective-permute-start
  55.4 16.6 %conditional.10 = ((bf16[288,1024]{1,0:T(8,128)(2,1)}, bf16[288,4096]{1,0:T(8,128)(2,1)}, bf16[288,512]{1,0:T(8,128)(2,1)}, bf16[288,512]{1,0:T(8,128)(2,1)}, bf...) conditional(s32[]{:T(128)} %convert_element_type.4, () %tuple.72, (bf16[864,1024]{1,0:T(8,128)(2,1)}, ...), branch_computations={%region_4.5_spmd, %region_5.6_spmd} | conditional | bytes 8 | solution.py:1106
  55.4 16.6 %enc_ffn.5 = (bf16[288,1024]{1,0:T(8,128)(2,1)}, bf16[288,4096]{1,0:T(8,128)(2,1)}, bf16[288,512]{1,0:T(8,128)(2,1)}, bf16[288,512]{1,0:T(8,128)(2,1)}, bf16[288,1024]{1,0:T(8,128)(2,1)}, /*index=5*/f32[288,128]{1,0:T(8,128)}) custom-call(bf16[864,1024]{1,0:T(8,128)(2,1)} %get-tuple-element.413.x_ref, bf16[864,1024]{1,0:T(8,128)(2,1)} %get-tuple-element.414.att_ref, ...), custom_call_target="tpu_custom_call" | custom-call | tf_op jit(solution)/shard_map/cond/branch_1_fun/enc_ffn/pallas_call | solution.py:402
  72.0 2.1 collective-permute-start.2
  74.1 17.1 %conditional.9 = (bf16[288,1024]{1,0:T(8,128)(2,1)}, bf16[288,4096]{1,0:T(8,128)(2,1)}, bf16[288,512]{1,0:T(8,128)(2,1)}, bf16[288,512]{1,0:T(8,128)(2,1)}, bf16...) conditional(s32[]{:T(128)} %convert_element_type.4, ...), branch_computations={%region_2.3_spmd, %region_3.4_spmd} | conditional | bytes 8913032 | solution.py:1106
  74.5 16.7 %enc_ffn.4 = (bf16[288,1024]{1,0:T(8,128)(2,1)}, bf16[288,4096]{1,0:T(8,128)(2,1)}, bf16[288,512]{1,0:T(8,128)(2,1)}, bf16[288,512]{1,0:T(8,128)(2,1)}, bf16[288,1024]{1,0:T(8,128)(2,1)}, /*index=5*/f32[288,128]{1,0:T(8,128)}) custom-call(bf16[864,1024]{1,0:T(8,128)(2,1)} %get-tuple-element.393.x_ref, bf16[864,1024]{1,0:T(8,128)(2,1)} %get-tuple-element.394.att_ref, ...), custom_call_target="tpu_custom_call" | custom-call | tf_op jit(solution)/shard_map/cond/branch_1_fun/enc_ffn/pallas_call | solution.py:402
  91.2 2.2 collective-permute-start.1
  93.4 12.9 %collective-permute-done.1 = bf16[288,1024]{1,0:T(8,128)(2,1)} collective-permute-done((bf16[288,1024]{1,0:T(8,128)(2,1)}, bf16[288,1024]{1,0:T(8,128)(2,1)}, u32[]{:S(2)}, u32[]{:S(2)}) %collective-permute-start.1) | collective-permute-done | bytes 589856 | tf_op jit(solution)/shard_map/ppermute | solution.py:1110
  110.2 80.2 %collective-permute-done.3 = bf16[288,1024]{1,0:T(8,128)(2,1)} collective-permute-done((bf16[288,1024]{1,0:T(8,128)(2,1)}, bf16[288,1024]{1,0:T(8,128)(2,1)}, u32[]{:S(2)}, u32[]{:S(2)}) %collective-permute-start.3) | collective-permute-done | bytes 589856 | tf_op jit(solution)/shard_map/ppermute | solution.py:1114
  190.5 16.0 %conditional.13 = (f32[288,1024]{1,0:T(8,128)}, bf16[288,1024]{1,0:T(8,128)(2,1)}, bf16[288,1024]{1,0:T(8,128)(2,1)}, bf16[288,512]{1,0:T(8,128)(2,1)}, bf16[96,...) conditional(s32[]{:T(128)} %convert_element_type.4, ...), branch_computations={%region_10.11_spmd, %region_11.12_spmd} | conditional | bytes 18874520 | solution.py:1106
  190.6 15.8 %enc_ffn_back.3 = (f32[288,1024]{1,0:T(8,128)}, bf16[288,1024]{1,0:T(8,128)(2,1)}, bf16[288,1024]{1,0:T(8,128)(2,1)}, bf16[288,512]{1,0:T(8,128)(2,1)}) custom-call(bf16[288,1024]{1,0:T(8,128)(2,1)} %get-tuple-element.491.dmem_ref, bf16[288,1024]{1,0:T(8,128)(2,1)} %get-tuple-element.492.mem_ref, bf16[288,1024]{1,0:T(8,128)(2,1)} %get-tuple-element.493.low_ref, ...), custom_call_target="tpu_custom_call" | custom-call | tf_op jit(solution)/shard_map/cond/branch_1_fun/enc_ffn_back/pallas_call | solution.py:503
  207.7 15.6 %conditional.14 = (f32[288,1024]{1,0:T(8,128)S(1)}, bf16[288,1024]{1,0:T(8,128)(2,1)S(1)}, bf16[288,1024]{1,0:T(8,128)(2,1)}, bf16[288,512]{1,0:T(8,128)(2,1)}, ...) conditional(s32[]{:T(128)} %convert_element_type.4, ...), branch_computations={%region_12.13_spmd, %region_13.14_spmd} | conditional | flops 4720128 | bytes 92293496 | solution.py:1106
  208.1 15.2 %enc_ffn_back.4 = (f32[288,1024]{1,0:T(8,128)S(1)}, bf16[288,1024]{1,0:T(8,128)(2,1)S(1)}, bf16[288,1024]{1,0:T(8,128)(2,1)}, bf16[288,512]{1,0:T(8,128)(2,1)}) custom-call(bf16[288,1024]{1,0:T(8,128)(2,1)} %get-tuple-element.553.dmem_ref, bf16[288,1024]{1,0:T(8,128)(2,1)} %get-tuple-element.554.mem_ref, bf16[288,1024]{1,0:T(8,128)(2,1)} %get-tuple-element.555.low_ref, ...), custom_call_target="tpu_custom_call" | custom-call | tf_op jit(solution)/shard_map/cond/branch_1_fun/enc_ffn_back/pallas_call | solution.py:503
  223.4 11.5 %collective-permute-done.6 = bf16[96,1024]{1,0:T(8,128)(2,1)} collective-permute-done((bf16[96,1024]{1,0:T(8,128)(2,1)}, bf16[96,1024]{1,0:T(8,128)(2,1)}, u32[]{:S(2)}, u32[]{:S(2)}) %collective-permute-start.6) | collective-permute-done | bytes 196640 | tf_op jit(solution)/shard_map/ppermute | solution.py:1114
  234.9 24.0 %conditional.15 = (f32[288,1024]{1,0:T(8,128)}, bf16[288,1024]{1,0:T(8,128)(2,1)}, f32[1024,512]{1,0:T(8,128)}, f32[1,512]{1,0:T(1,128)S(1)}, f32[512,1024]{1,0:T(8,128)}, /*index=5*/f32[1,1024]{1,0:T(1,128)S(1)}) conditional(s32[]{:T(128)} %convert_element_type.4, (f32[1024,512]{1,0:T(8,128)}, f32[1,512]{1,0:T(1,128)S(1)}, ...), branch_computations={%region_14.15_spmd, %region_15.16_spmd} | conditional | flops 1179648 | bytes 17695020 | solution.py:1106
  235.1 2.0 pad_maximum_fusion.4.dmem_ref
  237.2 16.4 %enc_ffn_back.5 = (f32[288,1024]{1,0:T(8,128)}, bf16[288,1024]{1,0:T(8,128)(2,1)}, bf16[288,1024]{1,0:T(8,128)(2,1)}, bf16[288,512]{1,0:T(8,128)(2,1)}) custom-call(bf16[288,1024]{1,0:T(8,128)(2,1)} %pad_maximum_fusion.4.dmem_ref, bf16[288,1024]{1,0:T(8,128)(2,1)} %get-tuple-element.585.mem_ref, bf16[288,1024]{1,0:T(8,128)(2,1)} %get-tuple-element.586.low_ref.refs_2_, ...), custom_call_target="tpu_custom_call" | custom-call | tf_op jit(solution)/shard_map/cond/branch_1_fun/enc_ffn_back/pallas_call | solution.py:503
  253.6 5.3 %adapter_grads.1 = (f32[1024,512]{1,0:T(8,128)}, f32[1,512]{1,0:T(1,128)S(1)}, f32[512,1024]{1,0:T(8,128)}, f32[1,1024]{1,0:T(1,128)S(1)}) custom-call(bf16[288,1024]{1,0:T(8,128)(2,1)S(1)} %copy-done.18, bf16[288,1024]{1,0:T(8,128)(2,1)S(1)} %copy-done.19, bf16[288,1024]{1,0:T(8,128)(2,1)S(1)} %copy-done.17, bf16[288,512]{1,0:T(8,128)(2,1)S(1)} %copy-done.41, ...), custom_call_target="tpu_custom_call" | custom-call | tf_op jit(solution)/shard_map/cond/branch_1_fun/adapter_grads/pallas_call | solution.py:553
  258.9 95.9 %finish.1 = (bf16[864,512]{1,0:T(8,128)(2,1)}, bf16[2,512,512]{2,1,0:T(8,128)(2,1)}, f32[512,1024]{1,0:T(8,128)}, f32[1024,512]{1,0:T(8,128)}, f32[64,1024]{1,0:T(8,128)}) custom-call(bf16[864,3072]{1,0:T(8,128)(2,1)} %get-tuple-element.701.q_ref.k_ref.v_ref, bf16[864,3072]{1,0:T(8,128)(2,1)} %get-tuple-element.701.q_ref.k_ref.v_ref, ...), custom_call_target="tpu_custom_call" | custom-call | tf_op jit(solution)/shard_map/finish/pallas_call | solution.py:1023
  356.1 1.4 slice.43
  (79 shorter events, 16.4 us)
Async XLA Ops:
  11.5 26.2 %copy-start.1 = (bf16[1024,1024]{1,0:T(8,128)(2,1)S(1)}, bf16[1024,1024]{1,0:T(8,128)(2,1)}, u32[]{:S(2)}) copy-start(bf16[1024,1024]{1,0:T(8,128)(2,1)} %get-tuple-element.358.wo_ref) | copy-start | bytes 6291460 | tf_op jit(solution)/shard_map/cond
  11.5 26.2 %copy-start.7 = (bf16[1024,512]{1,0:T(8,128)(2,1)S(1)}, bf16[1024,512]{1,0:T(8,128)(2,1)}, u32[]{:S(2)}) copy-start(bf16[1024,512]{1,0:T(8,128)(2,1)} %get-tuple-element.362.down_ref) | copy-start | bytes 3145732 | tf_op jit(solution)/shard_map/cond
  11.5 26.2 %copy-start.9 = (bf16[512,1024]{1,0:T(8,128)(2,1)S(1)}, bf16[512,1024]{1,0:T(8,128)(2,1)}, u32[]{:S(2)}) copy-start(bf16[512,1024]{1,0:T(8,128)(2,1)} %get-tuple-element.364.up_ref) | copy-start | bytes 3145732 | tf_op jit(solution)/shard_map/cond
  11.5 26.2 %copy-start.34 = (f32[2,1024]{1,0:T(2,128)S(1)}, f32[2,1024]{1,0:T(2,128)}, u32[]{:S(2)}) copy-start(f32[2,1024]{1,0:T(2,128)} %get-tuple-element.359.gain_ref) | copy-start | bytes 24580 | tf_op jit(solution)/shard_map/cond
  11.5 26.2 %copy-start.44 = (f32[1,1024]{1,0:T(1,128)S(1)}, f32[1,1024]{1,0:T(1,128)}, u32[]{:S(2)}) copy-start(f32[1,1024]{1,0:T(1,128)} %get-tuple-element.365.upb_ref) | copy-start | bytes 12292 | tf_op jit(solution)/shard_map/cond
  11.5 26.2 %copy-start.46 = (f32[1,512]{1,0:T(1,128)S(1)}, f32[1,512]{1,0:T(1,128)}, u32[]{:S(2)}) copy-start(f32[1,512]{1,0:T(1,128)} %get-tuple-element.363.downb_ref) | copy-start | bytes 6148 | tf_op jit(solution)/shard_map/cond
  53.2 20.9 %collective-permute-start = (bf16[288,1024]{1,0:T(8,128)(2,1)}, bf16[288,1024]{1,0:T(8,128)(2,1)}, u32[]{:S(2)}, u32[]{:S(2)}) collective-permute-start(bf16[288,1024]{1,0:T(8,128)(2,1)} %get-tuple-element.705), channel_id=1, source_target_pairs={{0,16},{1,17},{2,18},{3,19},{4,20},{5,21},{6,22},{7,23},{8,24},{9,... | collective-permute-start | bytes 1769480 | tf_op jit(solution)/shard_map/ppermute | solution.py:1110
  55.4 18.8 %copy-start.50 = (s32[1,2]{1,0:T(1,128)S(1)}, s32[1,2]{1,0:T(1,128)}, u32[]{:S(2)}) copy-start(s32[1,2]{1,0:T(1,128)} %param.38) | copy-start | bytes 28
  72.0 21.4 %collective-permute-start.2 = (bf16[288,1024]{1,0:T(8,128)(2,1)}, bf16[288,1024]{1,0:T(8,128)(2,1)}, u32[]{:S(2)}, u32[]{:S(2)}) collective-permute-start(bf16[288,1024]{1,0:T(8,128)(2,1)} %get-tuple-element.712), channel_id=1, source_target_pairs={{0,16},{1,17},{2,18},{3,19},{4,20},{5,21},{6,22},{7,23},{8,24},{9,... | collective-permute-start | bytes 1769480 | tf_op jit(solution)/shard_map/ppermute | solution.py:1110
  91.2 15.1 %collective-permute-start.1 = (bf16[288,1024]{1,0:T(8,128)(2,1)}, bf16[288,1024]{1,0:T(8,128)(2,1)}, u32[]{:S(2)}, u32[]{:S(2)}) collective-permute-start(bf16[288,1024]{1,0:T(8,128)(2,1)} %get-tuple-element.711), channel_id=1, source_target_pairs={{0,16},{1,17},{2,18},{3,19},{4,20},{5,21},{6,22},{7,23},{8,24},{9,... | collective-permute-start | bytes 1769480 | tf_op jit(solution)/shard_map/ppermute | solution.py:1110
  106.3 84.1 %collective-permute-start.3 = (bf16[288,1024]{1,0:T(8,128)(2,1)}, bf16[288,1024]{1,0:T(8,128)(2,1)}, u32[]{:S(2)}, u32[]{:S(2)}) collective-permute-start(bf16[288,1024]{1,0:T(8,128)(2,1)} %get-tuple-element.713), channel_id=1, source_target_pairs={{16,0},{17,1},{18,2},{19,3},{20,4},{21,5},{22,6},{23,7},{24,8},{25... | collective-permute-start | bytes 1769480 | tf_op jit(solution)/shard_map/ppermute | solution.py:1114
  107.6 100.1 %collective-permute-start.4 = (bf16[288,1024]{1,0:T(8,128)(2,1)}, bf16[288,1024]{1,0:T(8,128)(2,1)}, u32[]{:S(2)}, u32[]{:S(2)}) collective-permute-start(bf16[288,1024]{1,0:T(8,128)(2,1)} %get-tuple-element.739), channel_id=1, source_target_pairs={{16,0},{17,1},{18,2},{19,3},{20,4},{21,5},{22,6},{23,7},{24,8},{25... | collective-permute-start | bytes 1769480 | tf_op jit(solution)/shard_map/ppermute | solution.py:1114
  108.9 114.4 %collective-permute-start.5 = (bf16[192,1024]{1,0:T(8,128)(2,1)}, bf16[192,1024]{1,0:T(8,128)(2,1)}, u32[]{:S(2)}, u32[]{:S(2)}) collective-permute-start(bf16[192,1024]{1,0:T(8,128)(2,1)} %get-tuple-element.749), channel_id=1, source_target_pairs={{16,0},{17,1},{18,2},{19,3},{20,4},{21,5},{22,6},{23,7},{24,8},{25... | collective-permute-start | bytes 1179656 | tf_op jit(solution)/shard_map/ppermute | solution.py:1114
  206.4 28.5 %collective-permute-start.6 = (bf16[96,1024]{1,0:T(8,128)(2,1)}, bf16[96,1024]{1,0:T(8,128)(2,1)}, u32[]{:S(2)}, u32[]{:S(2)}) collective-permute-start(bf16[96,1024]{1,0:T(8,128)(2,1)} %get-tuple-element.750), channel_id=1, source_target_pairs={{16,0},{17,1},{18,2},{19,3},{20,4},{21,5},{22,6},{23,7},{24,8},{25... | collective-permute-start | bytes 589832 | tf_op jit(solution)/shard_map/ppermute | solution.py:1114
  234.9 24.0 %copy-start.12 = (bf16[864,1024]{1,0:T(8,128)(2,1)S(1)}, bf16[864,1024]{1,0:T(8,128)(2,1)}, u32[]{:S(2)}) copy-start(bf16[864,1024]{1,0:T(8,128)(2,1)} %get-tuple-element.702.o_ref) | copy-start | bytes 5308420
  237.1 16.4 %copy-start.18 = (bf16[288,1024]{1,0:T(8,128)(2,1)S(1)}, bf16[288,1024]{1,0:T(8,128)(2,1)}, u32[]{:S(2)}) copy-start(bf16[288,1024]{1,0:T(8,128)(2,1)} %get-tuple-element.598.refs_0_) | copy-start | bytes 1769476 | tf_op jit(solution)/shard_map/cond
  237.1 16.4 %copy-start.19 = (bf16[288,1024]{1,0:T(8,128)(2,1)S(1)}, bf16[288,1024]{1,0:T(8,128)(2,1)}, u32[]{:S(2)}) copy-start(bf16[288,1024]{1,0:T(8,128)(2,1)} %get-tuple-element.599.refs_1_) | copy-start | bytes 1769476 | tf_op jit(solution)/shard_map/cond
  237.1 16.5 %copy-start.35 = (bf16[288,1024]{1,0:T(8,128)(2,1)S(1)}, bf16[288,1024]{1,0:T(8,128)(2,1)}, u32[]{:S(2)}) copy-start(bf16[288,1024]{1,0:T(8,128)(2,1)} %get-tuple-element.603.refs_6_) | copy-start | bytes 1769476 | tf_op jit(solution)/shard_map/cond
  237.1 16.5 %copy-start.36 = (bf16[288,1024]{1,0:T(8,128)(2,1)S(1)}, bf16[288,1024]{1,0:T(8,128)(2,1)}, u32[]{:S(2)}) copy-start(bf16[288,1024]{1,0:T(8,128)(2,1)} %get-tuple-element.604.refs_7_) | copy-start | bytes 1769476 | tf_op jit(solution)/shard_map/cond
  237.1 16.5 %copy-start.39 = (bf16[288,512]{1,0:T(8,128)(2,1)S(1)}, bf16[288,512]{1,0:T(8,128)(2,1)}, u32[]{:S(2)}) copy-start(bf16[288,512]{1,0:T(8,128)(2,1)} %get-tuple-element.602.refs_5_) | copy-start | bytes 884740 | tf_op jit(solution)/shard_map/cond
  237.2 16.5 %copy-start.40 = (bf16[288,512]{1,0:T(8,128)(2,1)S(1)}, bf16[288,512]{1,0:T(8,128)(2,1)}, u32[]{:S(2)}) copy-start(bf16[288,512]{1,0:T(8,128)(2,1)} %get-tuple-element.607.refs_10_) | copy-start | bytes 884740 | tf_op jit(solution)/shard_map/cond
  237.2 16.5 %copy-start.41 = (bf16[288,512]{1,0:T(8,128)(2,1)S(1)}, bf16[288,512]{1,0:T(8,128)(2,1)}, u32[]{:S(2)}) copy-start(bf16[288,512]{1,0:T(8,128)(2,1)} %get-tuple-element.600.refs_3_) | copy-start | bytes 884740 | tf_op jit(solution)/shard_map/cond
  237.2 16.5 %copy-start.42 = (bf16[288,512]{1,0:T(8,128)(2,1)S(1)}, bf16[288,512]{1,0:T(8,128)(2,1)}, u32[]{:S(2)}) copy-start(bf16[288,512]{1,0:T(8,128)(2,1)} %get-tuple-element.601.refs_4_) | copy-start | bytes 884740 | tf_op jit(solution)/shard_map/cond
  258.9 99.6 %copy-start.16 = (bf16[2,512,512]{2,1,0:T(8,128)(2,1)S(1)}, bf16[2,512,512]{2,1,0:T(8,128)(2,1)}, u32[]{:S(2)}) copy-start(bf16[2,512,512]{2,1,0:T(8,128)(2,1)} %get-tuple-element.776) | copy-start | bytes 3145732
  (9 other events, 85.4 us)
